TPU v7x, 32 devices: a whole 2x2x4 slice. The times are simulated.
32 devices in a mesh: wide: 8 (over y, x, core), narrow: 4 (over z).
Axes of the slice: x: 2, y: 2, z: 4, core: 2. Of those that a mesh axis runs over, the one named last changes fastest.
Arguments:
- series: float32 [512, 512], P(('wide', 'narrow')), may hold values from -18 to 18
- flags: int32 [512, 512], P(('wide', 'narrow')), may hold values from 0 to 1, as said below
- lengths: int32 [512], P(('wide', 'narrow')), may hold values from 1 to 16, as said below
- lift_weight: bfloat16 [64, 1280], replicated, may hold values from -0.75 to 0.75
- mix_weight: bfloat16 [1280, 1280], replicated, may hold values from -0.15625 to 0.15625
- skip_weight: bfloat16 [64, 1280], replicated, may hold values from -0.75 to 0.75
- gain_first: float32 [1280], replicated, may hold values from 0.5 to 1.5
- joint_weight: bfloat16 [1280, 3840], replicated, may hold values from -0.15625 to 0.15625
- merge_weight: bfloat16 [1280, 1280], replicated, may hold values from -0.5 to 0.5
- gain_second: float32 [1280], replicated, may hold values from 0.5 to 1.5
- grow_weight: bfloat16 [1280, 1280], replicated, may hold values from -0.15625 to 0.15625
- shrink_weight: bfloat16 [1280, 1280], replicated, may hold values from -0.15625 to 0.15625
- head_weight: bfloat16 [1280, 128], replicated, may hold values from -0.15625 to 0.15625
- cotangent: float32 [512, 16, 128], P(('wide', 'narrow')), may hold values from -6 to 6
Outputs:
- predictions: float32 [512, 16, 128], P(('wide', 'narrow'))
- series_grad: float32 [512, 512], P(('wide', 'narrow'))
- lift_grad: float32 [64, 1280], P(None, ('wide', 'narrow'))
- mix_grad: float32 [1280, 1280], P(('wide', 'narrow'))
- skip_grad: float32 [64, 1280], P(None, ('wide', 'narrow'))
- first_grad: float32 [1280], P(('wide', 'narrow'))
- joint_grad: float32 [1280, 3840], P(('wide', 'narrow'))
- merge_grad: float32 [1280, 1280], P(('wide', 'narrow'))
- second_grad: float32 [1280], P(('wide', 'narrow'))
- grow_grad: float32 [1280, 1280], P(('wide', 'narrow'))
- shrink_grad: float32 [1280, 1280], P(None, ('wide', 'narrow'))
- head_grad: float32 [1280, 128], P(('wide', 'narrow'))
Inputs may be any that keep to these rules, and one draw needn't show every extreme that they name: `lengths`: each series ends in its real patches; patch p of a series is real when p >= 16 - length. Some series of every draw has all 16. `flags`: 1 marks a missing time point. In some series of every draw every point of the first real patch is missing.
All inputs are finite; a program needn't handle non-finite values.
Results may differ from a plain program's by a relative error of at most 0.014.
Values sent between devices are 32-bit elements; how exact they have to be, the bound alone decides.
No kernel may reach another device: no remote copies, remote signals or barrier semaphores. Data moves between devices by JAX's collectives and lax.ppermute only.
A program may use at most 256 MiB of HBM per device.

v0:
```python
import jax
import jax.numpy as jnp
from jax import lax
from jax.sharding import PartitionSpec as P

HEADS = 16


epsilon = 1e-06
masked_value = -1000000000.0


def product(left_side, right_side):
    return jnp.dot(left_side, right_side, preferred_element_type=jnp.float32)


def product_back(left_side, right_side):
    return lax.dot_general(
        left_side, right_side, (((1,), (1,)), ((), ())), preferred_element_type=jnp.float32
    )


def contract_rows(left_side, right_side):
    return lax.dot_general(
        left_side, right_side, (((0,), (0,)), ((), ())), preferred_element_type=jnp.float32
    )


def silu_slope(values):
    logistic = jax.nn.sigmoid(values)
    return logistic * (1.0 + values * (1.0 - logistic))


def rotary_tables(patches, head_dim):
    positions = jnp.arange(patches, dtype=jnp.int32).astype(jnp.float32)
    exponent = jnp.arange(head_dim // 2, dtype=jnp.int32).astype(jnp.float32) * (2.0 / head_dim)
    frequency = 10000.0 ** (-exponent)
    angles = positions[:, None] * frequency[None, :]
    angles = jnp.concatenate([angles, angles], axis=-1)[:, None, :]
    return (jnp.cos(angles), jnp.sin(angles))


def rotate(values, cosine, sine_table):
    half_width = values.shape[-1] // 2
    turned = jnp.concatenate([-values[..., half_width:], values[..., :half_width]], axis=-1)
    return values * cosine + turned * sine_table


def rotate_back(gradient, cosine, sine_table):
    half_width = gradient.shape[-1] // 2
    sine_part = gradient * sine_table
    turned = jnp.concatenate([sine_part[..., half_width:], -sine_part[..., :half_width]], axis=-1)
    return gradient * cosine + turned


def attention_mask(starts, patches):
    position = jnp.arange(patches, dtype=jnp.int32)
    query_pos = position[:, None]
    key_pos = position[None, :]
    allowed = (key_pos[None] <= query_pos[None]) & (
        (key_pos[None] >= starts[:, None, None]) | (key_pos[None] == query_pos[None])
    )
    return allowed[:, None, :, :]


def norm_back(inputs, scale_inv, gain_vector, upstream):
    gain_terms = upstream * inputs * scale_inv
    through = upstream * gain_vector
    inner_mean = jnp.mean(through * inputs, axis=-1, keepdims=True)
    return (gain_terms, scale_inv * through - inputs * scale_inv**3 * inner_mean)


def gradient_rows(pairs):
    columns = []
    for left_side, right_side in pairs:
        if right_side is None:
            columns.append(jnp.sum(left_side, axis=0)[:, None])
        else:
            columns.append(contract_rows(left_side, right_side))
    return jnp.concatenate(columns, axis=1)


def reduce_grads(pairs):
    summed = lax.psum_scatter(
        gradient_rows(pairs), ("wide", "narrow"), scatter_dimension=0, tiled=True
    )
    results = []
    begin = 0
    for left_side, right_side in pairs:
        span = 1 if right_side is None else right_side.shape[1]
        piece = summed[:, begin : begin + span]
        results.append(piece[:, 0] if right_side is None else piece)
        begin = begin + span
    return tuple(results)


def per_device(
    series,
    flags,
    lengths,
    lift_weight,
    mix_weight,
    skip_weight,
    gain_first,
    joint_weight,
    merge_weight,
    gain_second,
    grow_weight,
    shrink_weight,
    head_weight,
    cotangent,
):
    series_count = series.shape[0]
    patches = cotangent.shape[1]
    horizon = cotangent.shape[2]
    model_width = mix_weight.shape[0]
    patch_len = lift_weight.shape[0] // 2
    head_count = HEADS
    head_dim = model_width // head_count
    row_count = series_count * patches
    values = series.reshape(series_count, patches, patch_len)
    flag_values = flags.reshape(series_count, patches, patch_len).astype(jnp.float32)
    kept_mask = 1.0 - flag_values
    starts = patches - lengths
    position = jnp.arange(patches, dtype=jnp.int32)
    first_hot = (position[None, :] == starts[:, None]).astype(jnp.float32)
    observed_flags = (position[None, :] >= starts[:, None]).astype(jnp.float32)
    first_patch = jnp.sum(first_hot[:, :, None] * values, axis=1)
    first_kept = jnp.sum(first_hot[:, :, None] * kept_mask, axis=1)
    kept_count = jnp.maximum(jnp.sum(first_kept, axis=-1), 1.0)
    center = jnp.sum(first_kept * first_patch, axis=-1) / kept_count
    offset = first_patch - center[:, None]
    spread = jnp.sum(first_kept * offset * offset, axis=-1) / kept_count
    deviation = jnp.sqrt(jnp.maximum(spread, 1.0))
    shifted = values - center[:, None, None]
    scaled = shifted / deviation[:, None, None] * kept_mask
    tokens = (
        jnp.concatenate([scaled, flag_values], axis=-1)
        .reshape(row_count, 2 * patch_len)
        .astype(jnp.bfloat16)
    )
    hidden_pre = product(tokens, lift_weight)
    hidden_act = jax.nn.silu(hidden_pre).astype(jnp.bfloat16)
    embedded = product(hidden_act, mix_weight) + product(tokens, skip_weight)
    scale_one = lax.rsqrt(jnp.mean(embedded * embedded, axis=-1, keepdims=True) + epsilon)
    normed_one = (embedded * scale_one * gain_first).astype(jnp.bfloat16)
    joint_out = product(normed_one, joint_weight)
    cosine, sine_table = rotary_tables(patches, head_dim)
    shape_heads = (series_count, patches, head_count, head_dim)
    query_rot = rotate(joint_out[:, :model_width].reshape(shape_heads), cosine, sine_table).astype(
        jnp.bfloat16
    )
    key_rot = rotate(
        joint_out[:, model_width : 2 * model_width].reshape(shape_heads), cosine, sine_table
    ).astype(jnp.bfloat16)
    value_heads = joint_out[:, 2 * model_width :].reshape(shape_heads).astype(jnp.bfloat16)
    allowed = attention_mask(starts, patches)
    score_scale = head_dim ** (-0.5)

    def score_block():
        raw_scores = (
            jnp.einsum("bqhe,bkhe->bhqk", query_rot, key_rot, preferred_element_type=jnp.float32)
            * score_scale
        )
        return jnp.where(allowed, raw_scores, masked_value)

    masked = score_block()
    row_max = jnp.max(masked, axis=-1, keepdims=True)
    raised = jnp.exp(masked - row_max)
    row_total = jnp.sum(raised, axis=-1, keepdims=True)
    probs_full = raised / row_total
    logsum = row_max + jnp.log(row_total)
    mixed_heads = (
        jnp.einsum(
            "bhqk,bkhe->bqhe",
            probs_full.astype(jnp.bfloat16),
            value_heads,
            preferred_element_type=jnp.float32,
        )
        .astype(jnp.bfloat16)
        .reshape(row_count, model_width)
    )
    resid_one = embedded + product(mixed_heads, merge_weight)
    scale_two = lax.rsqrt(jnp.mean(resid_one * resid_one, axis=-1, keepdims=True) + epsilon)
    normed_two = (resid_one * scale_two * gain_second).astype(jnp.bfloat16)
    upper_pre = product(normed_two, grow_weight)
    active = jax.nn.silu(upper_pre).astype(jnp.bfloat16)
    resid_two = resid_one + product(active, shrink_weight)
    resid_low = resid_two.astype(jnp.bfloat16)
    head_out = product(resid_low, head_weight).reshape(series_count, patches, horizon)
    predictions = observed_flags[:, :, None] * (
        head_out * deviation[:, None, None] + center[:, None, None]
    )
    outer = cotangent * observed_flags[:, :, None]
    sigma_back = jnp.sum(outer * head_out, axis=(1, 2))
    center_back = jnp.sum(outer, axis=(1, 2))
    head_back = (outer * deviation[:, None, None]).astype(jnp.bfloat16).reshape(row_count, horizon)
    resid_back = product_back(head_back, head_weight)
    branch_back = resid_back.astype(jnp.bfloat16)
    upper_back = (product_back(branch_back, shrink_weight) * silu_slope(upper_pre)).astype(
        jnp.bfloat16
    )
    normed_back = product_back(upper_back, grow_weight)
    second_terms, middle_norm = norm_back(resid_one, scale_two, gain_second, normed_back)
    middle_back = resid_back + middle_norm
    merge_back = middle_back.astype(jnp.bfloat16)
    head_grad, shrink_shard, grow_grad, second_grad, merge_grad = reduce_grads(
        (
            (resid_low, head_back),
            (branch_back, active),
            (normed_two, upper_back),
            (second_terms, None),
            (mixed_heads, merge_back),
        )
    )
    mixed_back = product_back(merge_back, merge_weight).astype(jnp.bfloat16).reshape(shape_heads)
    probs_again = jnp.exp(score_block() - logsum)
    value_back = jnp.einsum(
        "bhqk,bqhe->bkhe",
        probs_again.astype(jnp.bfloat16),
        mixed_back,
        preferred_element_type=jnp.float32,
    )
    probs_back = jnp.einsum(
        "bqhe,bkhe->bhqk", mixed_back, value_heads, preferred_element_type=jnp.float32
    )
    row_inner = jnp.sum(probs_again * probs_back, axis=-1, keepdims=True)
    scores_back = (probs_again * (probs_back - row_inner) * score_scale).astype(jnp.bfloat16)
    query_back = rotate_back(
        jnp.einsum("bhqk,bkhe->bqhe", scores_back, key_rot, preferred_element_type=jnp.float32),
        cosine,
        sine_table,
    )
    key_back = rotate_back(
        jnp.einsum("bhqk,bqhe->bkhe", scores_back, query_rot, preferred_element_type=jnp.float32),
        cosine,
        sine_table,
    )
    joint_back = jnp.concatenate(
        [
            query_back.reshape(row_count, model_width),
            key_back.reshape(row_count, model_width),
            value_back.reshape(row_count, model_width),
        ],
        axis=-1,
    ).astype(jnp.bfloat16)
    first_back = product_back(joint_back, joint_weight)
    first_terms, embed_norm = norm_back(embedded, scale_one, gain_first, first_back)
    embed_low = (middle_back + embed_norm).astype(jnp.bfloat16)
    pre_back = (product_back(embed_low, mix_weight) * silu_slope(hidden_pre)).astype(jnp.bfloat16)
    joint_grad, first_grad, mix_grad, skip_shard, lift_shard = reduce_grads(
        (
            (normed_one, joint_back),
            (first_terms, None),
            (hidden_act, embed_low),
            (embed_low, tokens),
            (pre_back, tokens),
        )
    )
    token_back = product_back(pre_back, lift_weight) + product_back(embed_low, skip_weight)
    scaled_back = token_back.reshape(series_count, patches, 2 * patch_len)[:, :, :patch_len]
    kept_back = scaled_back * kept_mask
    point_back = kept_back / deviation[:, None, None]
    center_total = center_back - jnp.sum(point_back, axis=(1, 2))
    sigma_total = sigma_back - jnp.sum(kept_back * shifted, axis=(1, 2)) / (deviation * deviation)
    spread_back = jnp.where(spread > 1.0, sigma_total * 0.5 / deviation, 0.0)
    center_all = (
        center_total - spread_back * jnp.sum(first_kept * 2.0 * offset, axis=-1) / kept_count
    )
    first_point = (
        first_kept
        * (center_all[:, None] + 2.0 * offset * spread_back[:, None])
        / kept_count[:, None]
    )
    series_grad = (point_back + first_hot[:, :, None] * first_point[:, None, :]).reshape(
        series_count, patches * patch_len
    )
    return (
        predictions,
        series_grad,
        lift_shard.T,
        mix_grad,
        skip_shard.T,
        first_grad,
        joint_grad,
        merge_grad,
        second_grad,
        grow_grad,
        shrink_shard.T,
        head_grad,
    )


def solution(mesh):
    in_specs = (
        P(("wide", "narrow"), None),
        P(("wide", "narrow"), None),
        P(("wide", "narrow")),
        P(),
        P(),
        P(),
        P(),
        P(),
        P(),
        P(),
        P(),
        P(),
        P(),
        P(("wide", "narrow"), None, None),
    )
    out_specs = (
        P(("wide", "narrow"), None, None),
        P(("wide", "narrow"), None),
        P(None, ("wide", "narrow")),
        P(("wide", "narrow"), None),
        P(None, ("wide", "narrow")),
        P(("wide", "narrow")),
        P(("wide", "narrow"), None),
        P(("wide", "narrow"), None),
        P(("wide", "narrow")),
        P(("wide", "narrow"), None),
        P(None, ("wide", "narrow")),
        P(("wide", "narrow"), None),
    )
    return jax.shard_map(
        per_device, mesh=mesh, in_specs=in_specs, out_specs=out_specs, check_vma=False
    )
```

profile of v0, /device:TPU:0, one launch (start us, length us, event | category | flops | bytes accessed | tf_op | source)
XLA Modules:
  0.0 896.8 jit_solution(3977455761595879624)
XLA Ops:
  9.5 1.4 convert_convert_fusion
  14.4 1.5 reshape.405
  15.9 1.5 reshape.420
  22.0 1.1 multiply_convert_fusion.6
  24.0 1.2 fusion.68
  25.3 3.6 fusion.60
  29.9 1.1 copy-done.72
  31.1 2.8 fusion.56
  34.8 1.7 fusion.62
  36.7 3.3 convert_element_type.111
  40.0 3.3 reshape.408
  43.3 3.8 reshape.407
  47.1 2.4 copy.76
  50.3 1.5 slice_negate_fusion.2
  52.0 2.6 fusion.7
  56.7 1.2 copy-done.24
  58.7 1.3 copy.84
  59.9 3.0 reshape.409
  63.0 3.6 multiply_reduce_fusion.5
  66.6 1.1 fusion.58
  67.7 1.3 copy-done.73
  69.0 1.2 fusion.1
  70.7 1.7 multiply_reduce_fusion.11
  72.7 1.1 fusion.2
  73.9 1.8 multiply_reduce_fusion.1
  76.1 1.1 copy-done.13
  78.1 1.9 convolution_convert_fusion
  80.0 2.8 reshape.412
  82.8 3.4 fusion.33
  87.2 2.0 reshape.415
  89.2 5.1 fusion.21
  94.3 6.8 bitcast_multiply_fusion
  101.1 3.2 fusion.63
  106.5 1.4 fusion.9
  108.2 2.1 reshape.414
  110.5 2.0 reshape.413
  112.5 1.2 constant_dynamic-update-slice_fusion.2
  113.8 1.1 constant_dynamic-update-slice_fusion.1
  115.0 7.1 multiply_reduce_fusion.2
  123.4 1.0 copy-done.74
  124.4 1.1 fusion.3
  125.5 1.2 fusion.72
  126.8 4.0 fusion.59
  130.8 8.3 fusion.55
  139.1 1.1 broadcast_in_dim.28
  140.6 29.7 %concatenate.47 = f32[1280,5249]{1,0:T(8,128)} concatenate(f32[1280,3840]{1,0:T(8,128)} %fusion.55, f32[1280,1]{1,0:T(8,128)} %broadcast_in_dim.28, f32[1280,1280]{1,0:T(8,128)} %fusion.59, f32[1280,64]{1,0:T(8,128)S(1)} %copy-done.32, f32[1280,64]{1,0:T(8,128)S(1)} %fusion.73), dimensions={1} | concatenate | bytes 53749760 | tf_op jit(solution)/shard_map/concatenate | solution.py:80
  171.3 1.1 fusion.74
  172.5 5.0 fusion.37
  177.5 4.2 fusion.57
  181.7 4.3 fusion.40
  186.0 52.4 %concatenate.48 = f32[1280,3969]{0,1:T(8,128)} concatenate(f32[1280,128]{0,1:T(8,128)S(1)} %copy-done.31, f32[1280,1280]{0,1:T(8,128)} %fusion.40, f32[1280,1280]{0,1:T(8,128)} %fusion.57, f32[1280,1]{0,1:T(1,128)S(1)} %broadcast_in_dim.23, f32[1280,1280]{0,1:T(8,128)} %fusion.37), dimensions={1} | concatenate | bytes 40642560 | tf_op jit(solution)/shard_map/concatenate | solution.py:80
  238.4 22.3 %copy.106 = f32[1280,3969]{1,0:T(8,128)} copy(f32[1280,3969]{0,1:T(8,128)} %concatenate.48) | data formatting | bytes 40642560
  260.6 1.1 copy-done.29
  263.1 1.7 copy.92
  264.9 1.3 fusion.54
  267.7 1.0 multiply_add_fusion
  269.4 162.8 %reduce-scatter.5.cloned.1.call-done = f32[40,5249]{1,0:T(8,128)} async-done(((f32[1280,5249]{1,0:T(8,128)}), f32[40,5249]{1,0:T(8,128)}) %reduce-scatter.5.cloned.1.call-update) | async-done | bytes 839856 | tf_op jit(solution)/shard_map/reduce_scatter | solution.py:84
  432.3 1.7 slice.102
  434.0 1.9 slice.105
  435.9 1.4 slice_reduce_fusion
  437.3 1.5 slice_bitcast_fusion.1
  438.8 446.0 %reduce-scatter.7.cloned.1.call-done = f32[40,3969]{1,0:T(8,128)} async-done(((f32[1280,3969]{1,0:T(8,128)}), f32[40,3969]{1,0:T(8,128)}) %reduce-scatter.7.cloned.1.call-update) | async-done | bytes 635056
  886.2 1.3 slice.110
  887.5 2.0 slice_bitcast_fusion
  (203 shorter events, 30.5 us)
Async XLA Ops:
  7.2 59.4 %copy-start = (bf16[1280,1280]{1,0:T(8,128)(2,1)S(1)}, bf16[1280,1280]{1,0:T(8,128)(2,1)}, u32[]{:S(2)}) copy-start(bf16[1280,1280]{1,0:T(8,128)(2,1)} %param.24) | copy-start | bytes 9830404
  7.2 425.1 %reduce-scatter.5.cloned.1.call-start = ((), (), s32[]{:S(2)}) async-start(), calls=%async_computation.2 | async-start | bytes 28385280 | tf_op jit(solution)/shard_map/reduce_scatter | solution.py:84
  11.6 13.7 %copy-start.45 = (f32[16,16]{1,0:T(8,128)}, f32[16,16]{1,0:T(8,128)S(1)}, u32[]{:S(2)}) copy-start(f32[16,16]{1,0:T(8,128)S(1)} %get-tuple-element.98) | copy-start | bytes 3076
  12.6 6.7 copy-start.68
  12.7 16.2 %copy-start.33 = (f32[16,16,32]{2,1,0:T(8,128)}, f32[16,16,32]{2,1,0:T(8,128)S(1)}, u32[]{:S(2)}) copy-start(f32[16,16,32]{2,1,0:T(8,128)S(1)} %sub.110) | copy-start | bytes 98308
  14.4 7.6 copy-start.36
  25.3 3.7 copy-start.19
  25.3 3.7 copy-start.41
  25.3 5.8 copy-start.72
  29.0 2.1 copy-start.43
  29.4 4.5 copy-start.6
  29.9 3.9 copy-start.56
  34.8 1.7 copy-start.70
  34.8 1.7 copy-start.71
  36.7 15.3 %copy-start.51 = (f32[16,80]{1,0:T(8,128)}, f32[16,80]{1,0:T(8,128)S(1)}, u32[]{:S(2)}) copy-start(f32[16,80]{1,0:T(8,128)S(1)} %get-tuple-element.89) | copy-start | bytes 15364
  36.7 15.3 %copy-start.53 = (f32[16,80]{1,0:T(8,128)}, f32[16,80]{1,0:T(8,128)S(1)}, u32[]{:S(2)}) copy-start(f32[16,80]{1,0:T(8,128)S(1)} %get-tuple-element.90) | copy-start | bytes 15364
  47.1 2.4 copy-start.9
  50.2 1.6 copy-start.64
  50.2 1.6 copy-start.65
  50.3 1.6 copy-start.66
  50.3 1.7 copy-start.10
  55.9 2.7 copy-start.2
  55.9 2.0 copy-start.24
  63.0 3.7 copy-start.44
  66.6 9.1 %copy-start.4 = (f32[256,1280]{1,0:T(8,128)}, f32[256,1280]{1,0:T(8,128)S(1)}, u32[]{:S(2)}) copy-start(f32[256,1280]{1,0:T(8,128)S(1)} %get-tuple-element.104) | copy-start | bytes 3932164
  66.6 9.1 %copy-start.58 = (f32[256]{0:T(256)}, f32[256]{0:T(256)S(1)}, u32[]{:S(2)}) copy-start(f32[256]{0:T(256)S(1)} %get-tuple-element.94) | copy-start | bytes 3076
  66.6 2.4 copy-start.73
  69.0 3.7 copy-start.21
  69.0 1.6 copy-start.50
  69.0 1.6 copy-start.55
  69.0 1.6 copy-start.61
  69.0 1.6 copy-start.63
  70.3 2.1 copy-start.26
  72.7 3.0 copy-start.11
  73.9 1.8 copy-start.38
  75.7 2.4 copy-start.25
  82.8 3.4 copy-start.3
  89.2 5.1 copy-start.16
  89.2 5.1 copy-start.54
  101.1 3.2 copy-start.8
  104.3 1.6 copy-start.17
  104.3 2.2 copy-start.18
  104.3 2.2 copy-start.52
  110.5 4.4 copy-start.30
  112.5 2.4 copy-start.7
  112.5 2.4 copy-start.57
  115.0 7.1 copy-start.14
  115.0 7.1 copy-start.69
  122.1 2.3 copy-start.74
  125.5 14.7 %copy-start.28 = (bf16[256,1280]{1,0:T(8,128)(2,1)}, bf16[256,1280]{1,0:T(8,128)(2,1)S(1)}, u32[]{:S(2)}) copy-start(bf16[256,1280]{1,0:T(8,128)(2,1)S(1)} %fusion.3) | copy-start | bytes 1966084
  139.1 1.5 copy-start.32
  170.3 714.6 %reduce-scatter.7.cloned.1.call-start = ((), (), s32[]{:S(2)}) async-start(), calls=%async_computation.3 | async-start | bytes 21626880
  172.5 5.0 copy-start.5
  172.5 5.0 copy-start.39
  172.5 5.0 copy-start.59
  177.5 4.2 copy-start.12
  177.5 4.2 copy-start.22
  181.7 4.3 copy-start.31
  260.6 1.5 copy-start.42
  261.8 3.1 copy-start.34
  261.8 3.1 copy-start.37
  261.8 5.1 copy-start.48
  261.8 5.9 copy-start.46
  263.1 626.4 %copy-start.1 = (bf16[1280,1280]{1,0:T(8,128)(2,1)S(1)}, bf16[1280,1280]{1,0:T(8,128)(2,1)}, u32[]{:S(2)}) copy-start(bf16[1280,1280]{1,0:T(8,128)(2,1)} %param.24) | copy-start | bytes 9830404
  (13 other events, 13.7 us)
Sparse Core Ops, SparseCore 0:
  170.4 261.8 reduce-scatter.4
  434.7 450.1 reduce-scatter.6
where the time goes:
time: 907 us; the launch traced here: 897 us
  waiting for transfers between devices  609 us (67%)
  local copies, waits for them, and re-layouts  172 us (19%)
  matrix products  74.8 us (8%)
  other arithmetic  26.1 us (3%)
  between operations  15.4 us (2%)
    unnamed x3, waiting for transfers between devices  446 us
    reduce_scatter x1, waiting for transfers between devices, reduce_grads(): lax.psum_scatter(gradient_rows(pairs), ('wide', 'narrow'), scatter_dimens...  163 us
    concatenate x2, local copies, waits for them, and re-layouts, gradient_rows(): return jnp.concatenate(columns, axis=1)  82 us
    unnamed x154, local copies, waits for them, and re-layouts  38.2 us
    dot_general x8, matrix products, contract_rows(): lax.dot_general(left_side, right_side, (((0,), (0,)), ((), ())), preferre...  28.5 us
  transfers between devices with their start and end apart: 2, of which 2 were waited for; matrix products, arithmetic and copies ran while one was open for 12% of the time, Pallas kernels for 0%

commit v1 on v0

--- a/solution.py
+++ b/solution.py
@@ -1,6 +1,11 @@
+import functools
+import math
+
 import jax
 import jax.numpy as jnp
 from jax import lax
+from jax.experimental import pallas as pl
+from jax.experimental.pallas import tpu as pltpu
 from jax.sharding import PartitionSpec as P
 
 HEADS = 16
@@ -8,6 +13,7 @@
 
 epsilon = 1e-06
 masked_value = -1000000000.0
+AXES = ("wide", "narrow")
 
 
 def product(left_side, right_side):
@@ -70,31 +76,164 @@
     return (gain_terms, scale_inv * through - inputs * scale_inv**3 * inner_mean)
 
 
-def gradient_rows(pairs):
-    columns = []
-    for left_side, right_side in pairs:
-        if right_side is None:
-            columns.append(jnp.sum(left_side, axis=0)[:, None])
+def scatter_sum(array):
+    return lax.psum_scatter(array, AXES, scatter_dimension=0, tiled=True)
+
+
+class Layout:
+    def __init__(self, mesh_shape):
+        self.wide = mesh_shape["wide"]
+        self.narrow = mesh_shape["narrow"]
+        self.total = self.wide * self.narrow
+
+    def fits(self, rows):
+        return self.wide == 8 and self.narrow == 4 and rows % (16 * self.total // 4) == 0
+
+    def flip(self, bit):
+        return [(i, i ^ bit) for i in range(self.total)]
+
+    def middle(self):
+        swapped = (0, 2, 1, 3)
+        return [(i, (i & ~3) | swapped[i & 3]) for i in range(self.total)]
+
+    def position(self):
+        wide = lax.axis_index("wide")
+        narrow = lax.axis_index("narrow")
+        return {"y": wide // 4, "x": (wide // 2) % 2, "core": wide % 2, "z": narrow % 2}
+
+
+def to_other_core(layout, array):
+    return lax.ppermute(array.astype(jnp.float32), AXES, layout.flip(4))
+
+
+def gradient_kernel(groups_ref, *refs, pairs, group_rows, rows):
+    count = len(pairs)
+    inputs, (send_ref, keep_ref), scratch = refs[: 4 * count], refs[4 * count : 4 * count + 2], refs[4 * count + 2 :]
+    turned, chosen, joined = scratch[0], scratch[1 : 1 + count], scratch[1 + count :]
+    step = pl.program_id(0)
+
+    @pl.when(step == 0)
+    def _():
+        for at in range(count):
+            left_own, left_other, right_own, right_other = inputs[4 * at : 4 * at + 4]
+            turned[:, :rows] = left_own[...].astype(jnp.bfloat16).T
+            turned[:, rows:] = left_other[...].astype(jnp.bfloat16).T
+            for slot in range(4):
+                first = pl.multiple_of(groups_ref[slot] * group_rows, 32)
+                chosen[at][slot * group_rows : (slot + 1) * group_rows, :] = turned[pl.ds(first, group_rows), :]
+            joined[at][:rows, :] = right_own[...].astype(jnp.bfloat16)
+            joined[at][rows:, :] = right_other[...].astype(jnp.bfloat16)
+
+    def fill(out_ref, first):
+        for at in range(count):
+            begin, mask = pairs[at]
+            left_side = chosen[at][first : first + 2 * group_rows, :]
+            right_side = joined[at][...]
+            if mask is not None:
+                lane = lax.broadcasted_iota(jnp.int32, right_side.shape, 1)
+                inside = (lane >= mask[0]) & (lane < mask[1])
+                right_side = jnp.where(inside, right_side.astype(jnp.float32), 0.0).astype(jnp.bfloat16)
+            width = right_side.shape[1]
+            result = jnp.dot(left_side, right_side, preferred_element_type=jnp.float32)
+            result = result.reshape(2, group_rows, width)
+            if mask is not None and mask[0] > 0:
+                out_ref[:, :, begin : begin + width] += result
+            else:
+                out_ref[:, :, begin : begin + width] = result
+
+    @pl.when(step == 0)
+    def _():
+        fill(send_ref, 0)
+
+    @pl.when(step == 1)
+    def _():
+        fill(keep_ref, 2 * group_rows)
+
+
+def weight_gradient(groups, operands, pairs, group_rows):
+    rows, left_width = operands[0][0].shape
+    total = max(begin + ops[2].shape[1] for (begin, _), ops in zip(pairs, operands))
+    flat = [array for four in operands for array in four]
+    whole = lambda array: pl.BlockSpec(array.shape, lambda i, s: (0,) * array.ndim)
+    out_block = pl.BlockSpec((2, group_rows, total), lambda i, s: (0, 0, 0))
+    out_type = jax.ShapeDtypeStruct((2, group_rows, total), jnp.float32)
+    flops = sum(2 * 2 * rows * 4 * group_rows * ops[2].shape[1] for ops in operands)
+    moved = sum(array.size * array.dtype.itemsize for array in flat) + 4 * group_rows * total * 4
+    return pl.pallas_call(
+        functools.partial(gradient_kernel, pairs=pairs, group_rows=group_rows, rows=rows),
+        grid_spec=pltpu.PrefetchScalarGridSpec(
+            num_scalar_prefetch=1,
+            grid=(2,),
+            in_specs=[whole(array) for array in flat],
+            out_specs=[out_block, out_block],
+            scratch_shapes=[pltpu.VMEM((left_width, 2 * rows), jnp.bfloat16)]
+            + [pltpu.VMEM((4 * group_rows, 2 * rows), jnp.bfloat16) for _ in operands]
+            + [pltpu.VMEM((2 * rows, ops[2].shape[1]), jnp.bfloat16) for ops in operands],
+        ),
+        out_shape=[out_type, out_type],
+        compiler_params=pltpu.CompilerParams(vmem_limit_bytes=60 * 1024 * 1024),
+        cost_estimate=pl.CostEstimate(flops=flops, bytes_accessed=moved, transcendentals=0),
+    )(groups, *flat)
+
+
+def first_groups(place, axis):
+    y, x, core = place["y"], place["x"], place["core"]
+    if axis == "x":
+        order = [(0, 1 - x), (1, 1 - x), (0, x), (1, x)]
+    else:
+        order = [(1 - y, 0), (1 - y, 1), (y, 0), (y, 1)]
+    return jnp.stack([((a * 2 + b) * 2 + core) for a, b in order]).astype(jnp.int32)
+
+
+def pick(array, axis, index):
+    return lax.dynamic_index_in_dim(array, index, axis, keepdims=False)
+
+
+def sum_over_chips(layout, place, send, keep, order):
+    first = order[0]
+    group_rows, columns = send.shape[1:]
+    rows = group_rows // 4
+    held = keep + lax.ppermute(send, AXES, layout.flip({"x": 8, "y": 16}[first]))
+    held = held.reshape(2, 2, 2, rows, columns)
+    axes = ["y" if first == "x" else "x", "half", "part"]
+    for axis in order[1:]:
+        if axis == "z":
+            for name in ("half", "part"):
+                at = axes.index(name)
+                moved = lax.ppermute(pick(held, at, 1 - place["z"]), AXES, layout.flip(1))
+                held = pick(held, at, place["z"]) + moved
+                axes.remove(name)
+                if name == "half":
+                    held = lax.ppermute(held, AXES, layout.middle())
         else:
-            columns.append(contract_rows(left_side, right_side))
-    return jnp.concatenate(columns, axis=1)
-
-
-def reduce_grads(pairs):
-    summed = lax.psum_scatter(
-        gradient_rows(pairs), ("wide", "narrow"), scatter_dimension=0, tiled=True
-    )
+            at = axes.index(axis)
+            moved = lax.ppermute(pick(held, at, 1 - place[axis]), AXES, layout.flip({"x": 8, "y": 16}[axis]))
+            held = pick(held, at, place[axis]) + moved
+            axes.remove(axis)
+    return held
+
+
+def fast_sums(layout, wanted):
+    place = layout.position()
+    sent = {}
+
+    def other(array):
+        if id(array) not in sent:
+            sent[id(array)] = to_other_core(layout, array)
+        return sent[id(array)]
+
     results = []
-    begin = 0
-    for left_side, right_side in pairs:
-        span = 1 if right_side is None else right_side.shape[1]
-        piece = summed[:, begin : begin + span]
-        results.append(piece[:, 0] if right_side is None else piece)
-        begin = begin + span
-    return tuple(results)
+    for order, parts in wanted:
+        operands = [(left, other(left), right, other(right)) for left, right, _, _ in parts]
+        pairs = tuple((begin, lanes) for _, _, begin, lanes in parts)
+        group_rows = parts[0][0].shape[1] // 8
+        send, keep = weight_gradient(first_groups(place, order[0]), operands, pairs, group_rows)
+        results.append(sum_over_chips(layout, place, send, keep, order))
+    return results
 
 
 def per_device(
+    layout,
     series,
     flags,
     lengths,
@@ -202,17 +341,9 @@
     )
     normed_back = product_back(upper_back, grow_weight)
     second_terms, middle_norm = norm_back(resid_one, scale_two, gain_second, normed_back)
+    second_grad = scatter_sum(jnp.sum(second_terms, axis=0))
     middle_back = resid_back + middle_norm
     merge_back = middle_back.astype(jnp.bfloat16)
-    head_grad, shrink_shard, grow_grad, second_grad, merge_grad = reduce_grads(
-        (
-            (resid_low, head_back),
-            (branch_back, active),
-            (normed_two, upper_back),
-            (second_terms, None),
-            (mixed_heads, merge_back),
-        )
-    )
     mixed_back = product_back(merge_back, merge_weight).astype(jnp.bfloat16).reshape(shape_heads)
     probs_again = jnp.exp(score_block() - logsum)
     value_back = jnp.einsum(
@@ -246,17 +377,47 @@
     ).astype(jnp.bfloat16)
     first_back = product_back(joint_back, joint_weight)
     first_terms, embed_norm = norm_back(embedded, scale_one, gain_first, first_back)
+    first_grad = scatter_sum(jnp.sum(first_terms, axis=0))
     embed_low = (middle_back + embed_norm).astype(jnp.bfloat16)
     pre_back = (product_back(embed_low, mix_weight) * silu_slope(hidden_pre)).astype(jnp.bfloat16)
-    joint_grad, first_grad, mix_grad, skip_shard, lift_shard = reduce_grads(
-        (
-            (normed_one, joint_back),
-            (first_terms, None),
-            (hidden_act, embed_low),
-            (embed_low, tokens),
-            (pre_back, tokens),
+
+    if layout.fits(model_width):
+        width = active.shape[1]
+        half = joint_back.shape[1] // 2
+        tokens_twice = jnp.concatenate([tokens, tokens], axis=1)
+        across = tokens.shape[1]
+        shrink_rows, grow_head, merge_grad, joint_a, joint_b, mix_small = fast_sums(
+            layout,
+            [
+                ("xzy", [(branch_back, active, 0, None)]),
+                ("yzx", [(normed_two, upper_back, 0, None), (resid_low, head_back, width, None)]),
+                ("xyz", [(mixed_heads, merge_back, 0, None)]),
+                ("yxz", [(normed_one, joint_back[:, :half], 0, None)]),
+                ("xyz", [(normed_one, joint_back[:, half:], 0, None)]),
+                (
+                    "yzx",
+                    [
+                        (hidden_act, embed_low, 0, None),
+                        (pre_back, tokens_twice, model_width, (0, across)),
+                        (embed_low, tokens_twice, model_width, (across, 2 * across)),
+                    ],
+                ),
+            ],
         )
-    )
+        grow_grad, head_grad = grow_head[:, :width], grow_head[:, width:]
+        joint_grad = jnp.concatenate([joint_a, joint_b], axis=1)
+        mix_grad = mix_small[:, :model_width]
+        lift_rows = mix_small[:, model_width : model_width + across]
+        skip_rows = mix_small[:, model_width + across :]
+    else:
+        head_grad = scatter_sum(contract_rows(resid_low, head_back))
+        shrink_rows = scatter_sum(contract_rows(branch_back, active))
+        grow_grad = scatter_sum(contract_rows(normed_two, upper_back))
+        merge_grad = scatter_sum(contract_rows(mixed_heads, merge_back))
+        joint_grad = scatter_sum(contract_rows(normed_one, joint_back))
+        mix_grad = scatter_sum(contract_rows(hidden_act, embed_low))
+        lift_rows = scatter_sum(contract_rows(pre_back, tokens))
+        skip_rows = scatter_sum(contract_rows(embed_low, tokens))
     token_back = product_back(pre_back, lift_weight) + product_back(embed_low, skip_weight)
     scaled_back = token_back.reshape(series_count, patches, 2 * patch_len)[:, :, :patch_len]
     kept_back = scaled_back * kept_mask
@@ -278,50 +439,40 @@
     return (
         predictions,
         series_grad,
-        lift_shard.T,
+        lift_rows.T,
         mix_grad,
-        skip_shard.T,
+        skip_rows.T,
         first_grad,
         joint_grad,
         merge_grad,
         second_grad,
         grow_grad,
-        shrink_shard.T,
+        shrink_rows.T,
         head_grad,
     )
 
 
 def solution(mesh):
-    in_specs = (
-        P(("wide", "narrow"), None),
-        P(("wide", "narrow"), None),
-        P(("wide", "narrow")),
-        P(),
-        P(),
-        P(),
-        P(),
-        P(),
-        P(),
-        P(),
-        P(),
-        P(),
-        P(),
-        P(("wide", "narrow"), None, None),
-    )
+    both = P(AXES)
+    in_specs = (both, both, both) + (P(),) * 10 + (both,)
     out_specs = (
-        P(("wide", "narrow"), None, None),
-        P(("wide", "narrow"), None),
-        P(None, ("wide", "narrow")),
-        P(("wide", "narrow"), None),
-        P(None, ("wide", "narrow")),
-        P(("wide", "narrow")),
-        P(("wide", "narrow"), None),
-        P(("wide", "narrow"), None),
-        P(("wide", "narrow")),
-        P(("wide", "narrow"), None),
-        P(None, ("wide", "narrow")),
-        P(("wide", "narrow"), None),
+        P(AXES, None, None),
+        P(AXES, None),
+        P(None, AXES),
+        P(AXES, None),
+        P(None, AXES),
+        P(AXES),
+        P(AXES, None),
+        P(AXES, None),
+        P(AXES),
+        P(AXES, None),
+        P(None, AXES),
+        P(AXES, None),
     )
     return jax.shard_map(
-        per_device, mesh=mesh, in_specs=in_specs, out_specs=out_specs, check_vma=False
-    )
+        functools.partial(per_device, Layout(mesh.shape)),
+        mesh=mesh,
+        in_specs=in_specs,
+        out_specs=out_specs,
+        check_vma=False,
+    )

time: 907 us -> 536 us (0.59)
  waiting for transfers between devices: 609 us -> 105 us
  local copies, waits for them, and re-layouts: 172 us -> 60.9 us
  blocking collectives: 0 us -> 104 us
  starting transfers between devices: 0.08 us -> 102 us
  Pallas kernels: 0 us -> 43.1 us
  other arithmetic: 26.1 us -> 53.1 us
  matrix products: 74.8 us -> 55.4 us
  between operations: 15.4 us -> 2.42 us
    unnamed x3 -> x0, waiting for transfers between devices: 446 us -> none
    reduce_scatter x1 -> x0, waiting for transfers between devices: 163 us -> none  [reduce_grads(): lax.psum_scatter(gradient_rows(pairs), ('wide', 'narrow'), scatter_dimens...]
    ppermute x0 -> x45, waiting for transfers between devices: none -> 105 us  [the longest x12 56.2 us: sum_over_chips(): moved = lax.ppermute(pick(held, at, 1 - place['z']), AXES, layout.flip(1))]
    unnamed x0 -> x1, blocking collectives: none -> 104 us
    ppermute x0 -> x45, starting transfers between devices: none -> 102 us  [the longest x12 74.6 us: sum_over_chips(): moved = lax.ppermute(pick(held, at, 1 - place['z']), AXES, layout.flip(1))]
    concatenate x3 -> x0, local copies, waits for them, and re-layouts: 82.1 us -> none  [the longest x2 82 us: gradient_rows(): return jnp.concatenate(columns, axis=1)]
    pallas_call x0 -> x6, Pallas kernels: none -> 43.1 us  [weight_gradient(): pl.pallas_call(functools.partial(gradient_kernel, pairs=pairs, group_rows...]
    dot_general x8 -> x0, matrix products: 28.5 us -> none  [contract_rows(): lax.dot_general(left_side, right_side, (((0,), (0,)), ((), ())), preferre...]
  transfers between devices with their start and end apart: 2 -> 45, of which waited for: 2 -> 12; matrix products, arithmetic and copies ran while one was open for 12% -> 15% of each run, Pallas kernels for 0% -> 8%
where the time goes in v1:
time: 536 us; the launch traced here: 526 us
  waiting for transfers between devices  105 us (20%)
  blocking collectives  104 us (19%)
  starting transfers between devices  102 us (19%)
  local copies, waits for them, and re-layouts  60.9 us (11%)
  matrix products  55.4 us (10%)
  other arithmetic  53.1 us (10%)
  Pallas kernels  43.1 us (8%)
    unnamed x1, blocking collectives  104 us
    ppermute x12, starting transfers between devices, sum_over_chips(): moved = lax.ppermute(pick(held, at, 1 - place['z']), AXES, layout.flip(1))  74.6 us
    ppermute x12, waiting for transfers between devices, sum_over_chips(): moved = lax.ppermute(pick(held, at, 1 - place['z']), AXES, layout.flip(1))  56.2 us
    ppermute x6, waiting for transfers between devices, sum_over_chips(): lax.ppermute(pick(held, at, 1 - place[axis]), AXES, layout.flip({'x': 8,...  47.5 us
    pallas_call x6, Pallas kernels, weight_gradient(): pl.pallas_call(functools.partial(gradient_kernel, pairs=pairs, group_rows...  43.1 us
    dot_general x8, matrix products, product_back(): lax.dot_general(left_side, right_side, (((1,), (1,)), ((), ())), preferre...  19.7 us
    dot_general x8, matrix products, product(): return jnp.dot(left_side, right_side, preferred_element_type=jnp.float32)  17.6 us
    unnamed x204, local copies, waits for them, and re-layouts  12.4 us
  transfers between devices with their start and end apart: 45, of which 12 were waited for; matrix products, arithmetic and copies ran while one was open for 15% of the time, Pallas kernels for 8%

profile of v1, /device:TPU:0, one launch (start us, length us, event | category | flops | bytes accessed | tf_op | source)
XLA Modules:
  0.0 525.9 jit_solution(17316368558493383934)
XLA Ops:
  20.8 3.1 fusion.69
  24.7 3.1 fusion.80
  30.7 2.7 fusion.81
  33.5 1.7 fusion.71
  36.1 3.3 reshape.425
  39.5 3.6 copy.65
  43.0 3.3 reshape.426
  46.4 3.7 copy.68
  50.3 3.5 convert_element_type.156
  53.8 5.1 slice_negate_fusion.2
  59.1 2.6 fusion.7
  67.1 3.3 reshape.427.refs_0_
  70.4 3.6 multiply_reduce_fusion.5
  75.3 2.2 fusion.60
  77.7 2.1 fusion.79
  83.9 2.2 fusion.78
  87.8 1.8 multiply_reduce_fusion.1
  89.6 2.0 fusion.63
  92.5 1.9 convolution_convert_fusion
  94.4 2.7 reshape.430
  98.1 3.4 fusion.39
  101.5 5.0 fusion.24
  106.6 6.6 %bitcast_multiply_fusion.2 = (f32[16,16,16,80]{3,1,2,0:T(8,128)}, f32[16,16,16,80]{3,1,2,0:T(8,128)}, f32[16,16,80,16]{2,3,1,0:T(8,128)}) fusion(f32[16,80]{1,0:T(8,128)S(1)} %copy-done.70, f32[16,16,80,16]{2,3,1,0:T(8,128)} %fusion.24, bf16[16,16,16,80]{3,1,2,0:T(8,128)(2,1)S(1)} %copy-done.12, f32[16,16,16,16]{2,3,1,0:T(8,128)} %fusion.39, ...), kind=kOutput, calls=%fused_computation.26 | convolution fusion | flops 11603983 | bytes 6444032 | tf_op jit(solution)/shard_map/bhqk,bkhe->bqhe/dot_general | solution.py:361
  113.2 3.2 fusion.72
  118.6 2.3 fusion.8
  124.4 2.0 reshape.432
  128.0 2.0 reshape.433
  130.2 8.0 %multiply_reduce_fusion.2 = (f32[1280]{0:T(1024)}, f32[256]{0:T(256)S(1)}, f32[256,1280]{1,0:T(8,128)S(1)}) fusion(f32[256,1280]{1,0:T(8,128)S(1)} %copy-done.5, f32[256]{0:T(256)S(1)} %copy-done.83, f32[1280]{0:T(1024)S(1)} %copy-done.73, bf16[1280,3840]{1,0:T(8,128)(2,1)} %param.21, bf16[256,1280]{1,0:T(8,128)(2,1)} %reshape.433, ...), kind=kOutput, calls=%fused_computation.49 | convolution fusion | flops 2524445184 | bytes 14430208 | tf_op jit(solution)/shard_map/dot_general | solution.py:24
  144.2 2.5 fusion.77
  147.2 2.7 fusion.64
  153.8 6.2 %shard_map.234 = (f32[2,160,1280]{2,1,0:T(8,128)}, f32[2,160,1280]{2,1,0:T(8,128)}) custom-call(s32[4]{0:T(128)} %pad_add_fusion.1.groups_ref, bf16[256,1280]{1,0:T(8,128)(2,1)} %copy-done.32, f32[256,1280]{1,0:T(8,128)} %collective-permute-done.38.refs_1_, bf16[256,1280]{1,0:T(8,128)(2,1)} %copy-done.31, f32[256,1280]{1,0:T(8,128)} %collective-permute-done.39.refs_3_), custom_call_target="tpu_custom_call" | custom-call | flops 838860800 | bytes 7208960 | tf_op jit(solution)/shard_map/pallas_call | solution.py:162
  160.4 2.7 collective-permute-start.40
  164.1 6.1 %shard_map.232 = (f32[2,160,1280]{2,1,0:T(8,128)}, f32[2,160,1280]{2,1,0:T(8,128)}) custom-call(s32[4]{0:T(128)} %pad_add_fusion.1.groups_ref, bf16[256,1280]{1,0:T(8,128)(2,1)} %reshape.427.refs_0_, f32[256,1280]{1,0:T(8,128)} %collective-permute-done.22.refs_1_, bf16[256,1280]{1,0:T(8,128)(2,1)} %copy-done.30, f32[256,1280]{1,0:T(8,128)} %copy-done.44), custom_call_target="tpu_custom_call" | custom-call | flops 838860800 | bytes 7208960 | tf_op jit(solution)/shard_map/pallas_call | solution.py:162
  170.4 7.2 %shard_map.233 = (f32[2,160,1408]{2,1,0:T(8,128)}, f32[2,160,1408]{2,1,0:T(8,128)}) custom-call(s32[4]{0:T(128)} %pad_add_fusion.groups_ref, bf16[256,1280]{1,0:T(8,128)(2,1)} %copy-done.29, f32[256,1280]{1,0:T(8,128)} %copy-done.47, bf16[256,1280]{1,0:T(8,128)(2,1)} %copy-done.54, f32[256,1280]{1,0:T(8,128)} %collective-permute-done.30.refs_3_, ...), custom_call_target="tpu_custom_call" | custom-call | flops 922746880 | bytes 9699328 | tf_op jit(solution)/shard_map/pallas_call | solution.py:162
  177.6 2.0 collective-permute-start.33
  180.0 8.4 %shard_map.229 = (f32[2,160,1408]{2,1,0:T(8,128)}, f32[2,160,1408]{2,1,0:T(8,128)}) custom-call(s32[4]{0:T(128)} %pad_add_fusion.groups_ref, bf16[256,1280]{1,0:T(8,128)(2,1)} %copy-done.53, f32[256,1280]{1,0:T(8,128)} %collective-permute-done.refs_1_, bf16[256,1280]{1,0:T(8,128)(2,1)} %copy-done.9, f32[256,1280]{1,0:T(8,128)} %copy-done.22, ...), custom_call_target="tpu_custom_call" | custom-call | flops 1006632960 | bytes 11862016 | tf_op jit(solution)/shard_map/pallas_call | solution.py:162
  188.7 103.7 %all-reduce.2 = (f32[1280]{0:T(1024)S(1)}, f32[1280]{0:T(1024)S(1)}) all-reduce(f32[1280]{0:T(1024)S(1)} %copy-done.89, f32[1280]{0:T(1024)S(1)} %copy-done.88), channel_id=2, replica_groups=mesh['wide'=8,'narrow'=4] {'wide','narrow'}, use_global_device_ids=true, to_apply=%region_18.19.clone | all-reduce | flops 2560 | bytes 20480
  294.5 7.6 %shard_map.230 = (f32[2,160,1920]{2,1,0:T(8,128)}, f32[2,160,1920]{2,1,0:T(8,128)}) custom-call(s32[4]{0:T(128)} %pad_add_fusion.groups_ref, bf16[256,1280]{1,0:T(8,128)(2,1)} %copy-done.19, f32[256,1280]{1,0:T(8,128)} %copy-done.21, bf16[256,1920]{1,0:T(8,128)(2,1)} %get-tuple-element.60.refs_2_, f32[256,1920]{1,0:T(8,128)} %collective-permute-done.10.refs_3_), custom_call_target="tpu_custom_call" | custom-call | flops 1258291200 | bytes 9830400 | tf_op jit(solution)/shard_map/pallas_call | solution.py:162
  302.1 2.3 collective-permute-start.11
  306.6 7.6 %shard_map.231 = (f32[2,160,1920]{2,1,0:T(8,128)}, f32[2,160,1920]{2,1,0:T(8,128)}) custom-call(s32[4]{0:T(128)} %pad_add_fusion.1.groups_ref, bf16[256,1280]{1,0:T(8,128)(2,1)} %copy-done.19, f32[256,1280]{1,0:T(8,128)} %copy-done.21, bf16[256,1920]{1,0:T(8,128)(2,1)} %get-tuple-element.86.refs_2_, f32[256,1920]{1,0:T(8,128)} %collective-permute-done.16.refs_3_), custom_call_target="tpu_custom_call" | custom-call | flops 1258291200 | bytes 9830400 | tf_op jit(solution)/shard_map/pallas_call | solution.py:162
  314.7 1.7 add.357
  318.1 1.7 add.361
  321.6 1.7 add.333
  323.4 4.1 collective-permute-done.41
  329.1 45.0 %collective-permute-done.25 = f32[2,2,40,1280]{3,2,1,0:T(8,128)S(1)} collective-permute-done((f32[2,2,40,1280]{3,2,1,0:T(8,128)S(1)}, f32[2,2,40,1280]{3,2,1,0:T(8,128)S(1)}, u32[]{:S(2)}, u32[]{:S(2)}) %collective-permute-start.25) | collective-permute-done | bytes 819232 | tf_op jit(solution)/shard_map/ppermute | solution.py:210
  375.0 2.4 collective-permute-start.26
  378.5 6.1 %collective-permute-done.26 = f32[2,40,1280]{2,1,0:T(8,128)S(1)} collective-permute-done((f32[2,40,1280]{2,1,0:T(8,128)S(1)}, f32[2,40,1280]{2,1,0:T(8,128)S(1)}, u32[]{:S(2)}, u32[]{:S(2)}) %collective-permute-start.26) | collective-permute-done | bytes 409632 | tf_op jit(solution)/shard_map/ppermute | solution.py:203
  386.0 2.1 add.343
  391.8 50.7 %collective-permute-start.28 = (f32[40,1280]{1,0:T(8,128)S(1)}, f32[40,1280]{1,0:T(8,128)S(1)}, u32[]{:S(2)}, u32[]{:S(2)}) collective-permute-start(f32[40,1280]{1,0:T(8,128)S(1)} %dynamic-slice_bitcast_fusion.17), channel_id=1, source_target_pairs={{0,1},{1,0},{2,3},{3,2},{4,5},{5,4},{6,7},{7,6},{8,9},{9,8},{10,11... | collective-permute-start | bytes 614408 | tf_op jit(solution)/shard_map/ppermute | solution.py:203
  442.6 5.7 %collective-permute-done.28 = f32[40,1280]{1,0:T(8,128)S(1)} collective-permute-done((f32[40,1280]{1,0:T(8,128)S(1)}, f32[40,1280]{1,0:T(8,128)S(1)}, u32[]{:S(2)}, u32[]{:S(2)}) %collective-permute-start.28) | collective-permute-done | bytes 204832 | tf_op jit(solution)/shard_map/ppermute | solution.py:203
  448.2 2.3 collective-permute-start.43
  451.3 9.6 %collective-permute-done.43 = f32[2,40,1280]{2,1,0:T(8,128)S(1)} collective-permute-done((f32[2,40,1280]{2,1,0:T(8,128)S(1)}, f32[2,40,1280]{2,1,0:T(8,128)S(1)}, u32[]{:S(2)}, u32[]{:S(2)}) %collective-permute-start.43) | collective-permute-done | bytes 409632 | tf_op jit(solution)/shard_map/ppermute | solution.py:203
  462.2 2.1 collective-permute-start.7
  464.3 2.5 collective-permute-done.44
  467.5 2.0 collective-permute-done.36
  469.6 2.6 collective-permute-start.37
  472.2 2.2 collective-permute-done.7
  474.4 4.0 collective-permute-start.8
  478.7 2.4 collective-permute-start.13
  481.4 13.4 %collective-permute-done.13 = f32[2,40,1920]{2,1,0:T(8,128)S(1)} collective-permute-done((f32[2,40,1920]{2,1,0:T(8,128)S(1)}, f32[2,40,1920]{2,1,0:T(8,128)S(1)}, u32[]{:S(2)}, u32[]{:S(2)}) %collective-permute-start.13) | collective-permute-done | bytes 614432 | tf_op jit(solution)/shard_map/ppermute | solution.py:203
  495.6 8.4 %collective-permute-done.19 = f32[2,40,1920]{2,1,0:T(8,128)S(1)} collective-permute-done((f32[2,40,1920]{2,1,0:T(8,128)S(1)}, f32[2,40,1920]{2,1,0:T(8,128)S(1)}, u32[]{:S(2)}, u32[]{:S(2)}) %collective-permute-start.19) | collective-permute-done | bytes 614432 | tf_op jit(solution)/shard_map/ppermute | solution.py:203
  504.9 8.2 %collective-permute-start.15 = (f32[40,1920]{1,0:T(8,128)S(1)}, f32[40,1920]{1,0:T(8,128)S(1)}, u32[]{:S(2)}, u32[]{:S(2)}) collective-permute-start(f32[40,1920]{1,0:T(8,128)S(1)} %dynamic-slice_bitcast_fusion.13), channel_id=1, source_target_pairs={{0,1},{1,0},{2,3},{3,2},{4,5},{5,4},{6,7},{7,6},{8,9},{9,8},{10,11... | collective-permute-start | bytes 921608 | tf_op jit(solution)/shard_map/ppermute | solution.py:203
  515.8 3.9 collective-permute-start.21
  519.8 4.8 collective-permute-done.21
  (378 shorter events, 85.0 us)
Async XLA Ops:
  0.6 74.7 %copy-start = (bf16[1280,1280]{1,0:T(8,128)(2,1)S(1)}, bf16[1280,1280]{1,0:T(8,128)(2,1)}, u32[]{:S(2)}) copy-start(bf16[1280,1280]{1,0:T(8,128)(2,1)} %param.24) | copy-start | bytes 9830404
  5.4 18.4 %copy-start.50 = (f32[16,16,32]{2,1,0:T(8,128)}, f32[16,16,32]{2,1,0:T(8,128)S(1)}, u32[]{:S(2)}) copy-start(f32[16,16,32]{2,1,0:T(8,128)S(1)} %reshape.424) | copy-start | bytes 98308
  20.8 10.0 %copy-start.98 = (bf16[1280,3840]{1,0:T(8,128)(2,1)S(1)}, bf16[1280,3840]{1,0:T(8,128)(2,1)}, u32[]{:S(2)}) copy-start(bf16[1280,3840]{1,0:T(8,128)(2,1)} %param.21) | copy-start | bytes 29491204
  50.2 8.8 %copy-start.67 = (f32[16,80]{1,0:T(8,128)}, f32[16,80]{1,0:T(8,128)S(1)}, u32[]{:S(2)}) copy-start(f32[16,80]{1,0:T(8,128)S(1)} %get-tuple-element.99) | copy-start | bytes 15364
  83.4 57.1 %collective-permute-start.38 = (f32[256,1280]{1,0:T(8,128)}, f32[256,1280]{1,0:T(8,128)}, u32[]{:S(2)}, u32[]{:S(2)}) collective-permute-start(f32[256,1280]{1,0:T(8,128)} %get-tuple-element.52), channel_id=1, source_target_pairs={{0,4},{1,5},{2,6},{3,7},{4,0},{5,1},{6,2},{7,3},{8,12},{9,13},{10,... | collective-permute-start | bytes 3932168 | tf_op jit(solution)/shard_map/ppermute | solution.py:106
  83.9 58.6 %collective-permute-start.39 = (f32[256,1280]{1,0:T(8,128)}, f32[256,1280]{1,0:T(8,128)}, u32[]{:S(2)}, u32[]{:S(2)}) collective-permute-start(f32[256,1280]{1,0:T(8,128)} %get-tuple-element.50), channel_id=1, source_target_pairs={{0,4},{1,5},{2,6},{3,7},{4,0},{5,1},{6,2},{7,3},{8,12},{9,13},{10,... | collective-permute-start | bytes 3932168 | tf_op jit(solution)/shard_map/ppermute | solution.py:106
  86.1 60.5 %collective-permute-start.30 = (f32[256,1280]{1,0:T(8,128)}, f32[256,1280]{1,0:T(8,128)}, u32[]{:S(2)}, u32[]{:S(2)}) collective-permute-start(f32[256,1280]{1,0:T(8,128)} %get-tuple-element.123), channel_id=1, source_target_pairs={{0,4},{1,5},{2,6},{3,7},{4,0},{5,1},{6,2},{7,3},{8,12},{9,13},{10,... | collective-permute-start | bytes 3932168 | tf_op jit(solution)/shard_map/ppermute | solution.py:106
  86.6 60.2 %collective-permute-start.31 = (f32[256,1280]{1,0:T(8,128)}, f32[256,1280]{1,0:T(8,128)}, u32[]{:S(2)}, u32[]{:S(2)}) collective-permute-start(f32[256,1280]{1,0:T(8,128)} %get-tuple-element.125), channel_id=1, source_target_pairs={{0,4},{1,5},{2,6},{3,7},{4,0},{5,1},{6,2},{7,3},{8,12},{9,13},{10,... | collective-permute-start | bytes 3932168 | tf_op jit(solution)/shard_map/ppermute | solution.py:106
  87.3 51.6 %collective-permute-start.32 = (f32[256,128]{1,0:T(8,128)}, f32[256,128]{1,0:T(8,128)}, u32[]{:S(2)}, u32[]{:S(2)}) collective-permute-start(f32[256,128]{1,0:T(8,128)} %bitcast_convert_fusion), channel_id=1, source_target_pairs={{0,4},{1,5},{2,6},{3,7},{4,0},{5,1},{6,2},{7,3},{8,12},{9,13},{10,... | collective-permute-start | bytes 393224 | tf_op jit(solution)/shard_map/ppermute | solution.py:106
  130.1 10.2 %copy-start.45 = (f32[256,1280]{1,0:T(8,128)S(1)}, f32[256,1280]{1,0:T(8,128)}, u32[]{:S(2)}) copy-start(f32[256,1280]{1,0:T(8,128)} %get-tuple-element.54) | copy-start | bytes 3932164
  130.1 10.4 %copy-start.43 = (f32[256,1280]{1,0:T(8,128)S(1)}, f32[256,1280]{1,0:T(8,128)}, u32[]{:S(2)}) copy-start(f32[256,1280]{1,0:T(8,128)} %get-tuple-element.56) | copy-start | bytes 3932164
  130.1 10.7 %copy-start.23 = (f32[256,1280]{1,0:T(8,128)S(1)}, f32[256,1280]{1,0:T(8,128)}, u32[]{:S(2)}) copy-start(f32[256,1280]{1,0:T(8,128)} %get-tuple-element.58) | copy-start | bytes 3932164
  130.1 10.7 %copy-start.74 = (f32[1280]{0:T(1024)S(1)}, f32[1280]{0:T(1024)}, u32[]{:S(2)}) copy-start(f32[1280]{0:T(1024)} %param.20) | copy-start | bytes 15364
  130.2 10.7 %copy-start.84 = (f32[256]{0:T(256)S(1)}, f32[256]{0:T(256)}, u32[]{:S(2)}) copy-start(f32[256]{0:T(256)} %copy-done.82) | copy-start | bytes 3076
  130.2 10.7 %copy-start.91 = (f32[256]{0:T(256)S(1)}, f32[256]{0:T(256)}, u32[]{:S(2)}) copy-start(f32[256]{0:T(256)} %get-tuple-element.101) | copy-start | bytes 3076
  139.0 1.3 collective-permute-start.3
  140.3 9.5 %collective-permute-start.29 = (f32[256,1280]{1,0:T(8,128)S(1)}, f32[256,1280]{1,0:T(8,128)S(1)}, u32[]{:S(2)}, u32[]{:S(2)}) collective-permute-start(f32[256,1280]{1,0:T(8,128)S(1)} %copy-done.45), channel_id=1, source_target_pairs={{0,4},{1,5},{2,6},{3,7},{4,0},{5,1},{6,2},{7,3},{8,12},{9,13},{10,... | collective-permute-start | bytes 3932168 | tf_op jit(solution)/shard_map/ppermute | solution.py:106
  140.5 9.5 %collective-permute-start.23 = (f32[256,1280]{1,0:T(8,128)S(1)}, f32[256,1280]{1,0:T(8,128)S(1)}, u32[]{:S(2)}, u32[]{:S(2)}) collective-permute-start(f32[256,1280]{1,0:T(8,128)S(1)} %copy-done.43), channel_id=1, source_target_pairs={{0,4},{1,5},{2,6},{3,7},{4,0},{5,1},{6,2},{7,3},{8,12},{9,13},{10,... | collective-permute-start | bytes 3932168 | tf_op jit(solution)/shard_map/ppermute | solution.py:106
  142.3 20.7 %copy-start.9 = (bf16[256,1280]{1,0:T(8,128)(2,1)}, bf16[256,1280]{1,0:T(8,128)(2,1)S(1)}, u32[]{:S(2)}) copy-start(bf16[256,1280]{1,0:T(8,128)(2,1)S(1)} %get-tuple-element.68.refs_2_.refs_8_) | copy-start | bytes 1966084
  142.5 9.1 %collective-permute-start.22 = (f32[256,1280]{1,0:T(8,128)S(1)}, f32[256,1280]{1,0:T(8,128)}, u32[]{:S(2)}, u32[]{:S(2)}) collective-permute-start(f32[256,1280]{1,0:T(8,128)S(1)} %convert_element_type.183), channel_id=1, source_target_pairs={{0,4},{1,5},{2,6},{3,7},{4,0},{5,1},{6,2},{7,3},{8,12},{9,13},{10,... | collective-permute-start | bytes 3932168 | tf_op jit(solution)/shard_map/ppermute | solution.py:106
  146.7 13.4 %collective-permute-start.9 = (f32[256,1280]{1,0:T(8,128)}, f32[256,1280]{1,0:T(8,128)S(1)}, u32[]{:S(2)}, u32[]{:S(2)}) collective-permute-start(f32[256,1280]{1,0:T(8,128)} %get-tuple-element.63), channel_id=1, source_target_pairs={{0,4},{1,5},{2,6},{3,7},{4,0},{5,1},{6,2},{7,3},{8,12},{9,13},{10,... | collective-permute-start | bytes 3932168 | tf_op jit(solution)/shard_map/ppermute | solution.py:106
  146.8 13.6 %collective-permute-start.2 = (f32[256,1280]{1,0:T(8,128)}, f32[256,1280]{1,0:T(8,128)}, u32[]{:S(2)}, u32[]{:S(2)}) collective-permute-start(f32[256,1280]{1,0:T(8,128)} %get-tuple-element.121), channel_id=1, source_target_pairs={{0,4},{1,5},{2,6},{3,7},{4,0},{5,1},{6,2},{7,3},{8,12},{9,13},{10,... | collective-permute-start | bytes 3932168 | tf_op jit(solution)/shard_map/ppermute | solution.py:106
  149.8 38.6 %collective-permute-start.10 = (f32[256,1920]{1,0:T(8,128)}, f32[256,1920]{1,0:T(8,128)}, u32[]{:S(2)}, u32[]{:S(2)}) collective-permute-start(f32[256,1920]{1,0:T(8,128)} %get-tuple-element.59), channel_id=1, source_target_pairs={{0,4},{1,5},{2,6},{3,7},{4,0},{5,1},{6,2},{7,3},{8,12},{9,13},{10,... | collective-permute-start | bytes 5898248 | tf_op jit(solution)/shard_map/ppermute | solution.py:106
  151.3 19.0 %collective-permute-start.1 = (f32[256,1280]{1,0:T(8,128)}, f32[256,1280]{1,0:T(8,128)S(1)}, u32[]{:S(2)}, u32[]{:S(2)}) collective-permute-start(f32[256,1280]{1,0:T(8,128)} %get-tuple-element.67), channel_id=1, source_target_pairs={{0,4},{1,5},{2,6},{3,7},{4,0},{5,1},{6,2},{7,3},{8,12},{9,13},{10,... | collective-permute-start | bytes 3932168 | tf_op jit(solution)/shard_map/ppermute | solution.py:106
  151.6 26.0 %collective-permute-start = (f32[256,1280]{1,0:T(8,128)}, f32[256,1280]{1,0:T(8,128)}, u32[]{:S(2)}, u32[]{:S(2)}) collective-permute-start(f32[256,1280]{1,0:T(8,128)} %get-tuple-element.69), channel_id=1, source_target_pairs={{0,4},{1,5},{2,6},{3,7},{4,0},{5,1},{6,2},{7,3},{8,12},{9,13},{10,... | collective-permute-start | bytes 3932168 | tf_op jit(solution)/shard_map/ppermute | solution.py:106
  153.8 9.3 %copy-start.56 = (bf16[64,1280]{1,0:T(8,128)(2,1)S(1)}, bf16[64,1280]{1,0:T(8,128)(2,1)}, u32[]{:S(2)}) copy-start(bf16[64,1280]{1,0:T(8,128)(2,1)} %param.19) | copy-start | bytes 491524
  160.1 10.2 %copy-start.21 = (f32[256,1280]{1,0:T(8,128)}, f32[256,1280]{1,0:T(8,128)S(1)}, u32[]{:S(2)}) copy-start(f32[256,1280]{1,0:T(8,128)S(1)} %collective-permute-done.9.refs_1_) | copy-start | bytes 3932164
  160.1 146.0 %collective-permute-start.16 = (f32[256,1920]{1,0:T(8,128)}, f32[256,1920]{1,0:T(8,128)}, u32[]{:S(2)}, u32[]{:S(2)}) collective-permute-start(f32[256,1920]{1,0:T(8,128)} %get-tuple-element.85), channel_id=1, source_target_pairs={{0,4},{1,5},{2,6},{3,7},{4,0},{5,1},{6,2},{7,3},{8,12},{9,13},{10,... | collective-permute-start | bytes 5898248 | tf_op jit(solution)/shard_map/ppermute | solution.py:106
  160.4 141.7 %collective-permute-start.40 = (f32[2,160,1280]{2,1,0:T(8,128)}, f32[2,160,1280]{2,1,0:T(8,128)}, u32[]{:S(2)}, u32[]{:S(2)}) collective-permute-start(f32[2,160,1280]{2,1,0:T(8,128)} %get-tuple-element.35), channel_id=1, source_target_pairs={{0,8},{1,9},{2,10},{3,11},{4,12},{5,13},{6,14},{7,15},{8,0},{9,1},... | collective-permute-start | bytes 4915208 | tf_op jit(solution)/shard_map/ppermute | solution.py:196
  170.3 9.3 %copy-start.51 = (f32[16,16,32]{2,1,0:T(8,128)S(1)}, f32[16,16,32]{2,1,0:T(8,128)}, u32[]{:S(2)}) copy-start(f32[16,16,32]{2,1,0:T(8,128)} %copy-done.50) | copy-start | bytes 98308
  170.3 9.3 %copy-start.78 = (f32[16]{0:T(128)S(1)}, f32[16]{0:T(128)}, u32[]{:S(2)}) copy-start(f32[16]{0:T(128)} %copy-done.76) | copy-start | bytes 196
  170.3 9.2 %copy-start.81 = (f32[16]{0:T(128)S(1)}, f32[16]{0:T(128)}, u32[]{:S(2)}) copy-start(f32[16]{0:T(128)} %copy-done.79) | copy-start | bytes 196
  170.3 143.8 %collective-permute-start.24 = (f32[2,160,1280]{2,1,0:T(8,128)}, f32[2,160,1280]{2,1,0:T(8,128)}, u32[]{:S(2)}, u32[]{:S(2)}) collective-permute-start(f32[2,160,1280]{2,1,0:T(8,128)} %get-tuple-element.31), channel_id=1, source_target_pairs={{0,8},{1,9},{2,10},{3,11},{4,12},{5,13},{6,14},{7,15},{8,0},{9,1},... | collective-permute-start | bytes 4915208 | tf_op jit(solution)/shard_map/ppermute | solution.py:196
  177.6 139.0 %collective-permute-start.33 = (f32[2,160,1408]{2,1,0:T(8,128)}, f32[2,160,1408]{2,1,0:T(8,128)}, u32[]{:S(2)}, u32[]{:S(2)}) collective-permute-start(f32[2,160,1408]{2,1,0:T(8,128)} %get-tuple-element.33), channel_id=1, source_target_pairs={{0,16},{1,17},{2,18},{3,19},{4,20},{5,21},{6,22},{7,23},{8,24},{9,... | collective-permute-start | bytes 5406728 | tf_op jit(solution)/shard_map/ppermute | solution.py:196
  180.0 113.6 %copy-start.65 = (f32[16,32]{1,0:T(8,128)S(1)}, f32[16,32]{1,0:T(8,128)}, u32[]{:S(2)}) copy-start(f32[16,32]{1,0:T(8,128)} %copy-done.64) | copy-start | bytes 6148
  188.4 131.5 %collective-permute-start.4 = (f32[2,160,1408]{2,1,0:T(8,128)}, f32[2,160,1408]{2,1,0:T(8,128)}, u32[]{:S(2)}, u32[]{:S(2)}) collective-permute-start(f32[2,160,1408]{2,1,0:T(8,128)} %get-tuple-element.25), channel_id=1, source_target_pairs={{0,16},{1,17},{2,18},{3,19},{4,20},{5,21},{6,22},{7,23},{8,24},{9,... | collective-permute-start | bytes 5406728 | tf_op jit(solution)/shard_map/ppermute | solution.py:196
  294.5 9.9 %copy-start.41 = (f32[2,160,1280]{2,1,0:T(8,128)S(1)}, f32[2,160,1280]{2,1,0:T(8,128)}, u32[]{:S(2)}) copy-start(f32[2,160,1280]{2,1,0:T(8,128)} %get-tuple-element.34) | copy-start | bytes 4915204
  302.1 83.2 %collective-permute-start.11 = (f32[2,160,1920]{2,1,0:T(8,128)}, f32[2,160,1920]{2,1,0:T(8,128)}, u32[]{:S(2)}, u32[]{:S(2)}) collective-permute-start(f32[2,160,1920]{2,1,0:T(8,128)} %get-tuple-element.27), channel_id=1, source_target_pairs={{0,16},{1,17},{2,18},{3,19},{4,20},{5,21},{6,22},{7,23},{8,24},{9,... | collective-permute-start | bytes 7372808 | tf_op jit(solution)/shard_map/ppermute | solution.py:196
  306.1 21.4 %collective-permute-start.41 = (f32[2,2,40,1280]{3,2,1,0:T(8,128)S(1)}, f32[2,2,40,1280]{3,2,1,0:T(8,128)}, u32[]{:S(2)}, u32[]{:S(2)}) collective-permute-start(f32[2,2,40,1280]{3,2,1,0:T(8,128)S(1)} %dynamic-slice_bitcast_fusion.4), channel_id=1, source_target_pairs={{0,1},{1,0},{2,3},{3,2},{4,5},{5,4},{6,7},{7,6},{8,9},{9,8},{10,11... | collective-permute-start | bytes 2457608 | tf_op jit(solution)/shard_map/ppermute | solution.py:203
  314.1 74.1 %collective-permute-start.17 = (f32[2,160,1920]{2,1,0:T(8,128)}, f32[2,160,1920]{2,1,0:T(8,128)S(1)}, u32[]{:S(2)}, u32[]{:S(2)}) collective-permute-start(f32[2,160,1920]{2,1,0:T(8,128)} %get-tuple-element.29), channel_id=1, source_target_pairs={{0,8},{1,9},{2,10},{3,11},{4,12},{5,13},{6,14},{7,15},{8,0},{9,1},... | collective-permute-start | bytes 7372808 | tf_op jit(solution)/shard_map/ppermute | solution.py:196
  316.6 57.6 %collective-permute-start.25 = (f32[2,2,40,1280]{3,2,1,0:T(8,128)S(1)}, f32[2,2,40,1280]{3,2,1,0:T(8,128)S(1)}, u32[]{:S(2)}, u32[]{:S(2)}) collective-permute-start(f32[2,2,40,1280]{3,2,1,0:T(8,128)S(1)} %dynamic-slice_bitcast_fusion.5), channel_id=1, source_target_pairs={{0,16},{1,17},{2,18},{3,19},{4,20},{5,21},{6,22},{7,23},{8,24},{9,... | collective-permute-start | bytes 2457608 | tf_op jit(solution)/shard_map/ppermute | solution.py:210
  319.9 55.1 %collective-permute-start.34 = (f32[2,2,40,1408]{3,2,1,0:T(8,128)S(1)}, f32[2,2,40,1408]{3,2,1,0:T(8,128)S(1)}, u32[]{:S(2)}, u32[]{:S(2)}) collective-permute-start(f32[2,2,40,1408]{3,2,1,0:T(8,128)S(1)} %dynamic-slice_bitcast_fusion.2), channel_id=1, source_target_pairs={{0,1},{1,0},{2,3},{3,2},{4,5},{5,4},{6,7},{7,6},{8,9},{9,8},{10,11... | collective-permute-start | bytes 2703368 | tf_op jit(solution)/shard_map/ppermute | solution.py:203
  327.4 50.1 %collective-permute-start.5 = (f32[2,2,40,1408]{3,2,1,0:T(8,128)S(1)}, f32[2,2,40,1408]{3,2,1,0:T(8,128)S(1)}, u32[]{:S(2)}, u32[]{:S(2)}) collective-permute-start(f32[2,2,40,1408]{3,2,1,0:T(8,128)S(1)} %dynamic-slice_bitcast_fusion.3), channel_id=1, source_target_pairs={{0,1},{1,0},{2,3},{3,2},{4,5},{5,4},{6,7},{7,6},{8,9},{9,8},{10,11... | collective-permute-start | bytes 2703368 | tf_op jit(solution)/shard_map/ppermute | solution.py:203
  374.1 17.7 %collective-permute-start.42 = (f32[2,2,40,1280]{3,2,1,0:T(8,128)S(1)}, f32[2,2,40,1280]{3,2,1,0:T(8,128)S(1)}, u32[]{:S(2)}, u32[]{:S(2)}) collective-permute-start(f32[2,2,40,1280]{3,2,1,0:T(8,128)S(1)} %bitcast_add_fusion.4), channel_id=1, source_target_pairs={{0,0},{1,2},{2,1},{3,3},{4,4},{5,6},{6,5},{7,7},{8,8},{9,10},{10,9... | collective-permute-start | bytes 2457608 | tf_op jit(solution)/shard_map/ppermute | solution.py:207
  375.0 9.5 %collective-permute-start.26 = (f32[2,40,1280]{2,1,0:T(8,128)S(1)}, f32[2,40,1280]{2,1,0:T(8,128)S(1)}, u32[]{:S(2)}, u32[]{:S(2)}) collective-permute-start(f32[2,40,1280]{2,1,0:T(8,128)S(1)} %dynamic-slice_bitcast_fusion.11), channel_id=1, source_target_pairs={{0,1},{1,0},{2,3},{3,2},{4,5},{5,4},{6,7},{7,6},{8,9},{9,8},{10,11... | collective-permute-start | bytes 1228808 | tf_op jit(solution)/shard_map/ppermute | solution.py:203
  377.5 73.7 %collective-permute-start.35 = (f32[2,2,40,1408]{3,2,1,0:T(8,128)S(1)}, f32[2,2,40,1408]{3,2,1,0:T(8,128)S(1)}, u32[]{:S(2)}, u32[]{:S(2)}) collective-permute-start(f32[2,2,40,1408]{3,2,1,0:T(8,128)S(1)} %bitcast_add_fusion.2), channel_id=1, source_target_pairs={{0,0},{1,2},{2,1},{3,3},{4,4},{5,6},{6,5},{7,7},{8,8},{9,10},{10,9... | collective-permute-start | bytes 2703368 | tf_op jit(solution)/shard_map/ppermute | solution.py:207
  384.5 77.6 %collective-permute-start.6 = (f32[2,2,40,1408]{3,2,1,0:T(8,128)S(1)}, f32[2,2,40,1408]{3,2,1,0:T(8,128)S(1)}, u32[]{:S(2)}, u32[]{:S(2)}) collective-permute-start(f32[2,2,40,1408]{3,2,1,0:T(8,128)S(1)} %bitcast_add_fusion.3), channel_id=1, source_target_pairs={{0,0},{1,2},{2,1},{3,3},{4,4},{5,6},{6,5},{7,7},{8,8},{9,10},{10,9... | collective-permute-start | bytes 2703368 | tf_op jit(solution)/shard_map/ppermute | solution.py:207
  385.3 4.8 collective-permute-start.27
  388.2 90.3 %collective-permute-start.12 = (f32[2,2,40,1920]{3,2,1,0:T(8,128)S(1)}, f32[2,2,40,1920]{3,2,1,0:T(8,128)S(1)}, u32[]{:S(2)}, u32[]{:S(2)}) collective-permute-start(f32[2,2,40,1920]{3,2,1,0:T(8,128)S(1)} %dynamic-slice_bitcast_fusion.1), channel_id=1, source_target_pairs={{0,8},{1,9},{2,10},{3,11},{4,12},{5,13},{6,14},{7,15},{8,0},{9,1},... | collective-permute-start | bytes 3686408 | tf_op jit(solution)/shard_map/ppermute | solution.py:210
  390.1 90.9 %collective-permute-start.18 = (f32[2,2,40,1920]{3,2,1,0:T(8,128)S(1)}, f32[2,2,40,1920]{3,2,1,0:T(8,128)S(1)}, u32[]{:S(2)}, u32[]{:S(2)}) collective-permute-start(f32[2,2,40,1920]{3,2,1,0:T(8,128)S(1)} %dynamic-slice_bitcast_fusion), channel_id=1, source_target_pairs={{0,16},{1,17},{2,18},{3,19},{4,20},{5,21},{6,22},{7,23},{8,24},{9,... | collective-permute-start | bytes 3686408 | tf_op jit(solution)/shard_map/ppermute | solution.py:210
  391.8 56.4 %collective-permute-start.28 = (f32[40,1280]{1,0:T(8,128)S(1)}, f32[40,1280]{1,0:T(8,128)S(1)}, u32[]{:S(2)}, u32[]{:S(2)}) collective-permute-start(f32[40,1280]{1,0:T(8,128)S(1)} %dynamic-slice_bitcast_fusion.17), channel_id=1, source_target_pairs={{0,1},{1,0},{2,3},{3,2},{4,5},{5,4},{6,7},{7,6},{8,9},{9,8},{10,11... | collective-permute-start | bytes 614408 | tf_op jit(solution)/shard_map/ppermute | solution.py:203
  448.2 12.6 %collective-permute-start.43 = (f32[2,40,1280]{2,1,0:T(8,128)S(1)}, f32[2,40,1280]{2,1,0:T(8,128)S(1)}, u32[]{:S(2)}, u32[]{:S(2)}) collective-permute-start(f32[2,40,1280]{2,1,0:T(8,128)S(1)} %dynamic-slice_bitcast_fusion.10), channel_id=1, source_target_pairs={{0,1},{1,0},{2,3},{3,2},{4,5},{5,4},{6,7},{7,6},{8,9},{9,8},{10,11... | collective-permute-start | bytes 1228808 | tf_op jit(solution)/shard_map/ppermute | solution.py:203
  451.2 18.3 %collective-permute-start.36 = (f32[2,40,1408]{2,1,0:T(8,128)S(1)}, f32[2,40,1408]{2,1,0:T(8,128)S(1)}, u32[]{:S(2)}, u32[]{:S(2)}) collective-permute-start(f32[2,40,1408]{2,1,0:T(8,128)S(1)} %dynamic-slice_bitcast_fusion.8), channel_id=1, source_target_pairs={{0,1},{1,0},{2,3},{3,2},{4,5},{5,4},{6,7},{7,6},{8,9},{9,8},{10,11... | collective-permute-start | bytes 1351688 | tf_op jit(solution)/shard_map/ppermute | solution.py:203
  460.9 5.8 %collective-permute-start.44 = (f32[40,1280]{1,0:T(8,128)S(1)}, f32[40,1280]{1,0:T(8,128)S(1)}, u32[]{:S(2)}, u32[]{:S(2)}) collective-permute-start(f32[40,1280]{1,0:T(8,128)S(1)} %dynamic-slice_bitcast_fusion.16), channel_id=1, source_target_pairs={{0,16},{1,17},{2,18},{3,19},{4,20},{5,21},{6,22},{7,23},{8,24},{9,... | collective-permute-start | bytes 614408 | tf_op jit(solution)/shard_map/ppermute | solution.py:210
  462.2 12.1 %collective-permute-start.7 = (f32[2,40,1408]{2,1,0:T(8,128)S(1)}, f32[2,40,1408]{2,1,0:T(8,128)S(1)}, u32[]{:S(2)}, u32[]{:S(2)}) collective-permute-start(f32[2,40,1408]{2,1,0:T(8,128)S(1)} %dynamic-slice_bitcast_fusion.9), channel_id=1, source_target_pairs={{0,1},{1,0},{2,3},{3,2},{4,5},{5,4},{6,7},{7,6},{8,9},{9,8},{10,11... | collective-permute-start | bytes 1351688 | tf_op jit(solution)/shard_map/ppermute | solution.py:203
  469.6 11.8 %collective-permute-start.37 = (f32[40,1408]{1,0:T(8,128)S(1)}, f32[40,1408]{1,0:T(8,128)S(1)}, u32[]{:S(2)}, u32[]{:S(2)}) collective-permute-start(f32[40,1408]{1,0:T(8,128)S(1)} %dynamic-slice_bitcast_fusion.14), channel_id=1, source_target_pairs={{0,8},{1,9},{2,10},{3,11},{4,12},{5,13},{6,14},{7,15},{8,0},{9,1},... | collective-permute-start | bytes 675848 | tf_op jit(solution)/shard_map/ppermute | solution.py:210
  474.4 30.4 %collective-permute-start.8 = (f32[40,1408]{1,0:T(8,128)S(1)}, f32[40,1408]{1,0:T(8,128)S(1)}, u32[]{:S(2)}, u32[]{:S(2)}) collective-permute-start(f32[40,1408]{1,0:T(8,128)S(1)} %dynamic-slice_bitcast_fusion.15), channel_id=1, source_target_pairs={{0,8},{1,9},{2,10},{3,11},{4,12},{5,13},{6,14},{7,15},{8,0},{9,1},... | collective-permute-start | bytes 675848 | tf_op jit(solution)/shard_map/ppermute | solution.py:210
  478.7 16.1 %collective-permute-start.13 = (f32[2,40,1920]{2,1,0:T(8,128)S(1)}, f32[2,40,1920]{2,1,0:T(8,128)S(1)}, u32[]{:S(2)}, u32[]{:S(2)}) collective-permute-start(f32[2,40,1920]{2,1,0:T(8,128)S(1)} %dynamic-slice_bitcast_fusion.7), channel_id=1, source_target_pairs={{0,1},{1,0},{2,3},{3,2},{4,5},{5,4},{6,7},{7,6},{8,9},{9,8},{10,11... | collective-permute-start | bytes 1843208 | tf_op jit(solution)/shard_map/ppermute | solution.py:203
  481.3 22.7 %collective-permute-start.19 = (f32[2,40,1920]{2,1,0:T(8,128)S(1)}, f32[2,40,1920]{2,1,0:T(8,128)S(1)}, u32[]{:S(2)}, u32[]{:S(2)}) collective-permute-start(f32[2,40,1920]{2,1,0:T(8,128)S(1)} %dynamic-slice_bitcast_fusion.6), channel_id=1, source_target_pairs={{0,1},{1,0},{2,3},{3,2},{4,5},{5,4},{6,7},{7,6},{8,9},{9,8},{10,11... | collective-permute-start | bytes 1843208 | tf_op jit(solution)/shard_map/ppermute | solution.py:203
  494.9 10.0 %collective-permute-start.14 = (f32[2,40,1920]{2,1,0:T(8,128)S(1)}, f32[2,40,1920]{2,1,0:T(8,128)S(1)}, u32[]{:S(2)}, u32[]{:S(2)}) collective-permute-start(f32[2,40,1920]{2,1,0:T(8,128)S(1)} %bitcast_add_fusion.7), channel_id=1, source_target_pairs={{0,0},{1,2},{2,1},{3,3},{4,4},{5,6},{6,5},{7,7},{8,8},{9,10},{10,9... | collective-permute-start | bytes 1843208 | tf_op jit(solution)/shard_map/ppermute | solution.py:207
  504.1 11.7 %collective-permute-start.20 = (f32[2,40,1920]{2,1,0:T(8,128)S(1)}, f32[2,40,1920]{2,1,0:T(8,128)S(1)}, u32[]{:S(2)}, u32[]{:S(2)}) collective-permute-start(f32[2,40,1920]{2,1,0:T(8,128)S(1)} %bitcast_add_fusion.6), channel_id=1, source_target_pairs={{0,0},{1,2},{2,1},{3,3},{4,4},{5,6},{6,5},{7,7},{8,8},{9,10},{10,9... | collective-permute-start | bytes 1843208 | tf_op jit(solution)/shard_map/ppermute | solution.py:207
  504.9 14.8 %collective-permute-start.15 = (f32[40,1920]{1,0:T(8,128)S(1)}, f32[40,1920]{1,0:T(8,128)S(1)}, u32[]{:S(2)}, u32[]{:S(2)}) collective-permute-start(f32[40,1920]{1,0:T(8,128)S(1)} %dynamic-slice_bitcast_fusion.13), channel_id=1, source_target_pairs={{0,1},{1,0},{2,3},{3,2},{4,5},{5,4},{6,7},{7,6},{8,9},{9,8},{10,11... | collective-permute-start | bytes 921608 | tf_op jit(solution)/shard_map/ppermute | solution.py:203
  514.5 10.9 %copy-start.1 = (bf16[1280,1280]{1,0:T(8,128)(2,1)S(1)}, bf16[1280,1280]{1,0:T(8,128)(2,1)}, u32[]{:S(2)}) copy-start(bf16[1280,1280]{1,0:T(8,128)(2,1)} %param.24) | copy-start | bytes 9830404
  515.8 8.7 %collective-permute-start.21 = (f32[40,1920]{1,0:T(8,128)S(1)}, f32[40,1920]{1,0:T(8,128)S(1)}, u32[]{:S(2)}, u32[]{:S(2)}) collective-permute-start(f32[40,1920]{1,0:T(8,128)S(1)} %dynamic-slice_bitcast_fusion.12), channel_id=1, source_target_pairs={{0,1},{1,0},{2,3},{3,2},{4,5},{5,4},{6,7},{7,6},{8,9},{9,8},{10,11... | collective-permute-start | bytes 921608 | tf_op jit(solution)/shard_map/ppermute | solution.py:203
  (82 other events, 312.3 us)

commit v2 on v1

v2 whole, which is shorter than its diff:
```python
import functools

import jax
import jax.numpy as jnp
import numpy as np
from jax import lax
from jax.experimental import pallas as pl
from jax.experimental.pallas import tpu as pltpu
from jax.sharding import PartitionSpec as P

HEADS = 16
BLOCK = 128

epsilon = 1e-06
masked_value = -1000000000.0
AXES = ("wide", "narrow")


def rotary_tables(patches, head_dim, count):
    exponent = np.arange(head_dim // 2, dtype=np.float32) * np.float32(2.0 / head_dim)
    frequency = np.float32(10000.0) ** (-exponent)
    angles = frequency[:, None] * np.arange(patches, dtype=np.float32)[None, :]
    angles = np.tile(np.concatenate([angles, angles], axis=0), (1, count))
    return jnp.asarray(np.cos(angles)), jnp.asarray(np.sin(angles))


def dot_plain(left_side, right_side):
    return jnp.dot(left_side, right_side, preferred_element_type=jnp.float32)


def dot_over(left_side, right_side, left_axis, right_axis):
    return lax.dot_general(
        left_side,
        right_side,
        (((left_axis,), (right_axis,)), ((), ())),
        preferred_element_type=jnp.float32,
    )


def dot_exact(left_side, right_side):
    return jnp.dot(
        left_side, right_side, preferred_element_type=jnp.float32, precision=lax.Precision.HIGHEST
    )


def logistic(values):
    return 1.0 / (1.0 + jnp.exp(-values))


def quotient(values, by):
    return lax.shift_right_logical(values, jnp.int32(by.bit_length() - 1))


def remainder(values, by):
    return values & (by - 1)


def iota(shape, axis):
    return lax.broadcasted_iota(jnp.int32, shape, axis)


def series_statistics(lengths_ref, series_ref, flags_ref, patch_len):
    count, points = series_ref.shape
    patches = points // patch_len
    values = series_ref[...]
    kept = 1.0 - flags_ref[...].astype(jnp.float32)
    starts = jnp.zeros((count, 1), jnp.int32)
    row = iota((count, 1), 0)
    for at in range(count):
        starts = jnp.where(row == at, patches - lengths_ref[at], starts)
    hot = (quotient(iota((count, points), 1), patch_len) == starts).astype(jnp.float32)
    hot_kept = hot * kept
    kept_count = jnp.maximum(jnp.sum(hot_kept, axis=1, keepdims=True), 1.0)
    center = jnp.sum(hot_kept * values, axis=1, keepdims=True) / kept_count
    shifted = values - center
    spread = jnp.sum(hot_kept * shifted * shifted, axis=1, keepdims=True) / kept_count
    sigma = jnp.sqrt(jnp.maximum(spread, 1.0))
    return kept, starts, hot_kept, kept_count, center, shifted, spread, sigma


def belongs(rows, count, patches, kind):
    return (quotient(iota((rows, count), 0), patches) == iota((rows, count), 1)).astype(kind)


def belongs_back(rows, count, patches, kind):
    return (quotient(iota((count, rows), 1), patches) == iota((count, rows), 0)).astype(kind)


def own_patch(rows, points, patches, patch_len):
    return quotient(iota((rows, points), 1), patch_len) == remainder(iota((rows, points), 0), patches)


def turn_half(values):
    half = values.shape[0] // 2
    return jnp.concatenate([-values[half:], values[:half]], axis=0)


def turn_half_back(values):
    half = values.shape[0] // 2
    return jnp.concatenate([values[half:], -values[:half]], axis=0)


def split_rows(place_ref, turned, other_ref, own_ref, first, units):
    core = place_ref[0]
    unit = turned.shape[0] // units
    for at in range(units // 2):
        mine = pl.multiple_of((2 * at + core) * unit, 16)
        theirs = pl.multiple_of((2 * at + 1 - core) * unit, 16)
        own_ref[at * unit : (at + 1) * unit, :] = turned[pl.ds(mine, unit), :].astype(jnp.float32)
        other_ref[first + at * unit : first + (at + 1) * unit, :] = turned[pl.ds(theirs, unit), :].astype(jnp.float32)


def put_tiles(ref, first, values):
    rows, width = values.shape
    for at in range(width // rows):
        ref[first + at * rows : first + (at + 1) * rows, :] = values[:, at * rows : (at + 1) * rows].astype(jnp.float32)


UNITS = 8


def front_kernel(
    heads,
    lengths_ref,
    place_ref,
    series_ref,
    flags_ref,
    cotangent_ref,
    gain_first_ref,
    gain_second_ref,
    cosine_ref,
    sine_ref,
    lift_hbm,
    mix_hbm,
    skip_hbm,
    joint_hbm,
    merge_hbm,
    grow_hbm,
    shrink_hbm,
    head_hbm,
    predictions_ref,
    tokens_out,
    logsum_out,
    sigma_sum_out,
    center_sum_out,
    second_out,
    embedded_hbm,
    middle_hbm,
    turned_hbm,
    early_send_hbm,
    early_own_hbm,
    shrink_send_hbm,
    shrink_own_hbm,
    grow_send_hbm,
    grow_own_hbm,
    merge_send_hbm,
    merge_own_hbm,
    lift_ref,
    mix_ref,
    skip_ref,
    joint_ref,
    merge_ref,
    grow_ref,
    shrink_ref,
    head_ref,
    embedded_ref,
    middle_ref,
    joint_turned,
    turned_ref,
    mixed_turned,
    allowed_ref,
    resid_ref,
    upper_ref,
    back_ref,
    flip_ref,
    early_send,
    early_own,
    shrink_send,
    shrink_own,
    grow_send,
    grow_own,
    merge_send,
    merge_own,
    load_sem,
    store_sem,
):
    rows, width = embedded_ref.shape
    count, points = series_ref.shape
    patches = rows // count
    patch_len = points // patches
    head_dim = width // heads
    half_rows = width // 2
    loads = [
        pltpu.make_async_copy(lift_hbm, lift_ref, load_sem.at[0]),
        pltpu.make_async_copy(skip_hbm, skip_ref, load_sem.at[1]),
        pltpu.make_async_copy(mix_hbm, mix_ref, load_sem.at[2]),
    ]
    for at in range(3):
        loads.append(
            pltpu.make_async_copy(joint_hbm.at[:, pl.ds(at * width, width)], joint_ref.at[at], load_sem.at[3 + at])
        )
    for at, (source, target) in enumerate(
        ((merge_hbm, merge_ref), (head_hbm, head_ref), (shrink_hbm, shrink_ref), (grow_hbm, grow_ref))
    ):
        loads.append(pltpu.make_async_copy(source, target, load_sem.at[6 + at]))
    for copy in loads:
        copy.start()
    stores = []

    def store(source, target):
        copy = pltpu.make_async_copy(source, target, store_sem.at[len(stores)])
        copy.start()
        stores.append(copy)

    kept, starts, _, _, center, shifted, _, sigma = series_statistics(lengths_ref, series_ref, flags_ref, patch_len)
    scaled = (shifted / sigma * kept).astype(jnp.bfloat16)
    flag_values = flags_ref[...].astype(jnp.float32).astype(jnp.bfloat16)
    spread_out = belongs(rows, count, patches, jnp.bfloat16)
    inside = own_patch(rows, points, patches, patch_len)
    lane = iota((points, 2 * patch_len), 1)
    point = remainder(iota((points, 2 * patch_len), 0), patch_len)
    fold_left = (lane == point).astype(jnp.bfloat16)
    fold_right = (lane == point + patch_len).astype(jnp.bfloat16)
    left = jnp.where(inside, dot_plain(spread_out, scaled), 0.0).astype(jnp.bfloat16)
    right = jnp.where(inside, dot_plain(spread_out, flag_values), 0.0).astype(jnp.bfloat16)
    tokens = (dot_plain(left, fold_left) + dot_plain(right, fold_right)).astype(jnp.bfloat16)
    tokens_out[...] = tokens
    wide = cotangent_ref.shape[1]
    spread_exact = belongs(rows, count, patches, jnp.float32)
    sigma_rows = dot_exact(spread_exact, jnp.broadcast_to(sigma, (count, wide)))
    center_rows = dot_exact(spread_exact, jnp.broadcast_to(center, (count, wide)))
    starts_rows = dot_exact(spread_exact, jnp.broadcast_to(starts.astype(jnp.float32), (count, wide)))
    patch_row = remainder(iota((rows, wide), 0), patches).astype(jnp.float32)
    valid = (patch_row >= starts_rows - 0.5).astype(jnp.float32)
    block = allowed_ref.shape[1]
    key_at = remainder(iota((rows, block), 0), block)
    query_at = iota((rows, block), 1)
    key_pos, query_pos = remainder(key_at, patches), remainder(query_at, patches)
    allowed_ref[...] = (
        (quotient(key_at, patches) == quotient(query_at, patches))
        & (key_pos <= query_pos)
        & ((key_pos.astype(jnp.float32) >= starts_rows[:, :1] - 0.5) | (key_pos == query_pos))
    ).astype(jnp.float32)

    loads[0].wait()
    hidden_pre = dot_plain(tokens, lift_ref[...])
    hidden_act = (hidden_pre * logistic(hidden_pre)).astype(jnp.bfloat16)
    flip_ref[...] = hidden_act.T
    split_rows(place_ref, flip_ref, early_send, early_own.at[pl.ds(half_rows, half_rows)], half_rows, UNITS)
    loads[1].wait()
    loads[2].wait()
    embedded = dot_plain(hidden_act, mix_ref[...]) + dot_plain(tokens, skip_ref[...])
    embedded_ref[...] = embedded
    store(embedded_ref, embedded_hbm)
    scale_one = lax.rsqrt(jnp.mean(embedded * embedded, axis=1, keepdims=True) + epsilon)
    normed_one = (embedded * scale_one * gain_first_ref[...]).astype(jnp.bfloat16)
    for at in range(3):
        loads[3 + at].wait()
        tile = rows
        for part in range(width // tile):
            result = dot_plain(normed_one, joint_ref[at, :, part * tile : (part + 1) * tile])
            joint_turned[at * width + part * tile : at * width + (part + 1) * tile, :] = result.T
    flip_ref[...] = normed_one.T
    split_rows(place_ref, flip_ref, early_send, early_own.at[pl.ds(0, half_rows)], 0, UNITS)
    store(early_send, early_send_hbm)
    store(early_own, early_own_hbm)

    scale = head_dim ** (-0.5)
    cosine, sine = cosine_ref[...], sine_ref[...]

    def one_head(head, _):
        begin = pl.multiple_of(head * head_dim, 16)
        query = joint_turned[pl.ds(begin, head_dim), :]
        key = joint_turned[pl.ds(width + begin, head_dim), :]
        value = joint_turned[pl.ds(2 * width + begin, head_dim), :].astype(jnp.bfloat16)
        query = (query * cosine + turn_half(query) * sine).astype(jnp.bfloat16)
        key = (key * cosine + turn_half(key) * sine).astype(jnp.bfloat16)
        turned_ref[pl.ds(begin, head_dim), :] = query
        turned_ref[pl.ds(width + begin, head_dim), :] = key
        turned_ref[pl.ds(2 * width + begin, head_dim), :] = value
        mixed, sums = [], []
        for at in range(rows // block):
            span = slice(at * block, (at + 1) * block)
            scores = dot_over(key[:, span], query[:, span], 0, 0) * scale
            scores = jnp.where(allowed_ref[span, :] > 0.5, scores, masked_value)
            top = jnp.max(scores, axis=0, keepdims=True)
            raised = jnp.exp(scores - top)
            total = jnp.sum(raised, axis=0, keepdims=True)
            sums.append(top + jnp.log(total))
            probs = (raised / total).astype(jnp.bfloat16)
            mixed.append(dot_plain(value[:, span], probs))
        logsum_out[pl.ds(head, 1), :] = jnp.concatenate(sums, axis=1)
        mixed_turned[pl.ds(begin, head_dim), :] = jnp.concatenate(mixed, axis=1).astype(jnp.bfloat16)
        return 0

    lax.fori_loop(0, heads, one_head, 0, unroll=2)
    store(turned_ref, turned_hbm)
    split_rows(place_ref, mixed_turned, merge_send, merge_own, 0, UNITS)
    store(merge_own, merge_own_hbm)
    mixed = mixed_turned[...].T
    loads[6].wait()
    resid_one = embedded_ref[...] + dot_plain(mixed, merge_ref[...])
    resid_ref[...] = resid_one
    scale_two = lax.rsqrt(jnp.mean(resid_one * resid_one, axis=1, keepdims=True) + epsilon)
    normed_two = (resid_one * scale_two * gain_second_ref[...]).astype(jnp.bfloat16)
    flip_ref[...] = normed_two.T
    split_rows(place_ref, flip_ref, grow_send, grow_own.at[pl.ds(0, half_rows)], 0, UNITS)

    outer = cotangent_ref[...] * valid
    head_back = (outer * sigma_rows).astype(jnp.bfloat16)
    loads[7].wait()
    resid_back = dot_over(head_back, head_ref[...], 1, 1)
    back_ref[...] = resid_back
    branch_back = resid_back.astype(jnp.bfloat16)
    flip_ref[...] = branch_back.T
    split_rows(place_ref, flip_ref, shrink_send, shrink_own, 0, UNITS)
    store(shrink_own, shrink_own_hbm)

    loads[9].wait()
    upper_pre = dot_plain(normed_two, grow_ref[...])
    upper_ref[...] = upper_pre
    active = (upper_pre * logistic(upper_pre)).astype(jnp.bfloat16)
    put_tiles(shrink_send, half_rows, active)
    store(shrink_send, shrink_send_hbm)
    loads[8].wait()
    upper_pre = upper_ref[...]
    gate = logistic(upper_pre)
    slope = gate * (1.0 + upper_pre * (1.0 - gate))
    upper_back = (dot_over(branch_back, shrink_ref[...], 1, 1) * slope).astype(jnp.bfloat16)
    put_tiles(grow_send, half_rows, upper_back)
    resid_low = (resid_ref[...] + dot_plain(active, shrink_ref[...])).astype(jnp.bfloat16)
    flip_ref[...] = resid_low.T
    split_rows(place_ref, flip_ref, grow_send, grow_own.at[pl.ds(half_rows, half_rows)], half_rows + width, UNITS)
    grow_send[2 * width : 2 * width + wide, :] = head_back.astype(jnp.float32).T
    store(grow_send, grow_send_hbm)
    store(grow_own, grow_own_hbm)

    normed_back = dot_over(upper_back, grow_ref[...], 1, 1)
    resid_one = resid_ref[...]
    second_out[...] = jnp.sum(normed_back * resid_one * scale_two, axis=0, keepdims=True)
    through = normed_back * gain_second_ref[...]
    inner = jnp.mean(through * resid_one, axis=1, keepdims=True)
    middle = back_ref[...] + scale_two * through - resid_one * (scale_two * scale_two * scale_two * inner)
    middle_ref[...] = middle
    store(middle_ref, middle_hbm)
    put_tiles(merge_send, half_rows, middle.astype(jnp.bfloat16))
    store(merge_send, merge_send_hbm)

    head_out = dot_plain(resid_low, head_ref[...])
    predictions_ref[...] = valid * (head_out * sigma_rows + center_rows)
    gather = belongs_back(rows, count, patches, jnp.float32)
    sigma_sum_out[...] = dot_exact(gather, outer * head_out)
    center_sum_out[...] = dot_exact(gather, outer)
    for copy in stores:
        copy.wait()


def front(place, lengths, series, flags, cotangent, tables, weights, heads):
    lift, mix, skip, gain_first, joint, merge, gain_second, grow, shrink, head = weights
    rows, horizon = cotangent.shape
    width = mix.shape[0]
    half = width // 2
    count = series.shape[0]
    f32, bf16 = jnp.float32, jnp.bfloat16
    vmem = pl.BlockSpec(memory_space=pltpu.VMEM)
    smem = pl.BlockSpec(memory_space=pltpu.SMEM)
    hbm = pl.BlockSpec(memory_space=pl.ANY)
    shape = jax.ShapeDtypeStruct
    packs = [
        (2 * half, rows),
        (2 * half, rows),
        (half + width, rows),
        (half, rows),
        (2 * width + horizon, rows),
        (2 * half, rows),
        (half + width, rows),
        (half, rows),
    ]
    outs = [
        shape((rows, horizon), f32),
        shape((rows, lift.shape[0]), bf16),
        shape((heads, rows), f32),
        shape((count, horizon), f32),
        shape((count, horizon), f32),
        shape((1, width), f32),
        shape((rows, width), f32),
        shape((rows, width), f32),
        shape((3 * width, rows), bf16),
    ] + [shape(pack, f32) for pack in packs]
    scratch = [
        pltpu.VMEM(lift.shape, bf16),
        pltpu.VMEM(mix.shape, bf16),
        pltpu.VMEM(skip.shape, bf16),
        pltpu.VMEM((3, width, width), bf16),
        pltpu.VMEM(merge.shape, bf16),
        pltpu.VMEM(grow.shape, bf16),
        pltpu.VMEM(shrink.shape, bf16),
        pltpu.VMEM(head.shape, bf16),
        pltpu.VMEM((rows, width), f32),
        pltpu.VMEM((rows, width), f32),
        pltpu.VMEM((3 * width, rows), f32),
        pltpu.VMEM((3 * width, rows), bf16),
        pltpu.VMEM((width, rows), bf16),
        pltpu.VMEM((rows, BLOCK), f32),
        pltpu.VMEM((rows, width), f32),
        pltpu.VMEM((rows, width), f32),
        pltpu.VMEM((rows, width), f32),
        pltpu.VMEM((width, rows), bf16),
    ] + [pltpu.VMEM(pack, f32) for pack in packs]
    scratch += [pltpu.SemaphoreType.DMA((10,)), pltpu.SemaphoreType.DMA((11,))]
    return pl.pallas_call(
        functools.partial(front_kernel, heads),
        out_shape=outs,
        in_specs=[smem, smem] + [vmem] * 7 + [hbm] * 8,
        out_specs=[vmem] * 6 + [hbm] * 11,
        scratch_shapes=scratch,
        compiler_params=pltpu.CompilerParams(vmem_limit_bytes=62 * 1024 * 1024),
        cost_estimate=pl.CostEstimate(flops=9_000_000_000, bytes_accessed=45_000_000, transcendentals=2_000_000),
    )(
        lengths,
        place,
        series,
        flags,
        cotangent,
        gain_first.reshape(1, width),
        gain_second.reshape(1, width),
        *tables,
        lift,
        mix,
        skip,
        joint,
        merge,
        grow,
        shrink,
        head,
    )


def back_kernel(
    heads,
    lengths_ref,
    place_ref,
    series_ref,
    flags_ref,
    gain_first_ref,
    cosine_ref,
    sine_ref,
    tokens_ref,
    logsum_ref,
    sigma_sum_ref,
    center_sum_ref,
    second_ref,
    middle_ref,
    turned_ref,
    embedded_hbm,
    lift_hbm,
    mix_hbm,
    skip_hbm,
    joint_hbm,
    merge_hbm,
    series_grad_ref,
    joint_send_hbm,
    mix_send_hbm,
    mix_own_hbm,
    vector_send_hbm,
    vector_own_hbm,
    lift_ref,
    mix_ref,
    skip_ref,
    joint_ref,
    merge_ref,
    embedded_ref,
    mixed_turned,
    joint_turned,
    first_ref,
    allowed_ref,
    flip_ref,
    joint_send,
    mix_send,
    mix_own,
    vector_send,
    vector_own,
    vector_flip,
    load_sem,
    store_sem,
):
    rows, width = embedded_ref.shape
    count, points = series_ref.shape
    patches = rows // count
    patch_len = points // patches
    head_dim = width // heads
    half_rows = width // 2
    loads = [
        pltpu.make_async_copy(source, target, load_sem.at[at])
        for at, (source, target) in enumerate(
            (
                (merge_hbm, merge_ref),
                (joint_hbm, joint_ref),
                (embedded_hbm, embedded_ref),
                (mix_hbm, mix_ref),
                (lift_hbm, lift_ref),
                (skip_hbm, skip_ref),
            )
        )
    ]
    for copy in loads:
        copy.start()
    stores = []

    def store(source, target):
        copy = pltpu.make_async_copy(source, target, store_sem.at[len(stores)])
        copy.start()
        stores.append(copy)

    kept, starts, hot_kept, kept_count, center, shifted, spread, sigma = series_statistics(
        lengths_ref, series_ref, flags_ref, patch_len
    )
    block = allowed_ref.shape[1]
    spread_exact = belongs(rows, count, patches, jnp.float32)
    starts_rows = dot_exact(spread_exact, jnp.broadcast_to(starts.astype(jnp.float32), (count, block)))
    key_at = remainder(iota((rows, block), 0), block)
    query_at = iota((rows, block), 1)
    key_pos, query_pos = remainder(key_at, patches), remainder(query_at, patches)
    allowed_ref[...] = (
        (quotient(key_at, patches) == quotient(query_at, patches))
        & (key_pos <= query_pos)
        & ((key_pos.astype(jnp.float32) >= starts_rows - 0.5) | (key_pos == query_pos))
    ).astype(jnp.float32)
    scale = head_dim ** (-0.5)
    cosine, sine = cosine_ref[...], sine_ref[...]
    loads[0].wait()
    mixed_turned[...] = dot_over(merge_ref[...], middle_ref[...].astype(jnp.bfloat16), 1, 1).astype(jnp.bfloat16)

    def unrotate(gradient):
        return gradient * cosine + turn_half_back(gradient * sine)

    def one_head(head, _):
        begin = pl.multiple_of(head * head_dim, 16)
        query = turned_ref[pl.ds(begin, head_dim), :]
        key = turned_ref[pl.ds(width + begin, head_dim), :]
        value = turned_ref[pl.ds(2 * width + begin, head_dim), :]
        upstream = mixed_turned[pl.ds(begin, head_dim), :]
        logsum = logsum_ref[pl.ds(head, 1), :]
        query_parts, key_parts, value_parts = [], [], []
        for at in range(rows // block):
            span = slice(at * block, (at + 1) * block)
            query_in, key_in, value_in, up = query[:, span], key[:, span], value[:, span], upstream[:, span]
            scores = dot_over(key_in, query_in, 0, 0) * scale
            scores = jnp.where(allowed_ref[span, :] > 0.5, scores, masked_value)
            probs = jnp.exp(scores - logsum[:, span])
            value_parts.append(dot_over(up, probs.astype(jnp.bfloat16), 1, 1))
            probs_back = dot_over(value_in, up, 0, 0)
            inner = jnp.sum(probs * probs_back, axis=0, keepdims=True)
            scores_back = (probs * (probs_back - inner) * scale).astype(jnp.bfloat16)
            query_parts.append(dot_plain(key_in, scores_back))
            key_parts.append(dot_over(query_in, scores_back, 1, 1))
        for at, parts in enumerate((query_parts, key_parts, value_parts)):
            result = jnp.concatenate(parts, axis=1)
            if at < 2:
                result = unrotate(result)
            result = result.astype(jnp.bfloat16)
            joint_turned[pl.ds(at * width + begin, head_dim), :] = result
            joint_send[pl.ds(at * width + begin, head_dim), :] = result.astype(jnp.float32)
        return 0

    lax.fori_loop(0, heads, one_head, 0, unroll=2)
    store(joint_send, joint_send_hbm)
    loads[1].wait()
    tile = rows
    for part in range(width // tile):
        span = slice(part * tile, (part + 1) * tile)
        first_ref[:, span] = dot_plain(joint_ref[span, :], joint_turned[...]).T
    loads[2].wait()
    embedded = embedded_ref[...]
    first_back = first_ref[...]
    scale_one = lax.rsqrt(jnp.mean(embedded * embedded, axis=1, keepdims=True) + epsilon)
    first_sum = jnp.sum(first_back * embedded * scale_one, axis=0, keepdims=True)
    through = first_back * gain_first_ref[...]
    inner = jnp.mean(through * embedded, axis=1, keepdims=True)
    embed_low = (
        middle_ref[...] + scale_one * through - embedded * (scale_one * scale_one * scale_one * inner)
    ).astype(jnp.bfloat16)
    put_tiles(mix_send, 0, embed_low)
    flip_ref[...] = embed_low.T
    split_rows(place_ref, flip_ref, mix_send, mix_own.at[pl.ds(0, half_rows)], width, UNITS)
    tokens = tokens_ref[...]
    loads[4].wait()
    hidden_pre = dot_plain(tokens, lift_ref[...])
    gate = logistic(hidden_pre)
    slope = gate * (1.0 + hidden_pre * (1.0 - gate))
    loads[3].wait()
    pre_back = (dot_over(embed_low, mix_ref[...], 1, 1) * slope).astype(jnp.bfloat16)
    flip_ref[...] = pre_back.T
    split_rows(place_ref, flip_ref, mix_send, mix_own.at[pl.ds(half_rows, half_rows)], width + half_rows, UNITS)
    mix_send[2 * width : 2 * width + 2 * patch_len, :] = tokens.astype(jnp.float32).T
    store(mix_send, mix_send_hbm)
    store(mix_own, mix_own_hbm)

    lanes = vector_send.shape[1]
    row = iota((lanes, width), 0)
    both = jnp.where(row == 0, second_ref[...], jnp.where(row == 1, first_sum, 0.0))
    vector_flip[...] = both.T
    core = place_ref[0]
    unit = width // UNITS
    for at in range(UNITS // 2):
        mine = pl.multiple_of((2 * at + core) * unit, 16)
        theirs = pl.multiple_of((2 * at + 1 - core) * unit, 16)
        vector_own[at * unit : (at + 1) * unit, :] = vector_flip[pl.ds(mine, unit), :]
        vector_send[at * unit : (at + 1) * unit, :] = vector_flip[pl.ds(theirs, unit), :]
    store(vector_send, vector_send_hbm)
    store(vector_own, vector_own_hbm)

    loads[5].wait()
    token_back = dot_over(pre_back, lift_ref[...], 1, 1) + dot_over(embed_low, skip_ref[...], 1, 1)
    lane = remainder(iota((2 * patch_len, points), 1), patch_len)
    unfold = (lane == iota((2 * patch_len, points), 0)).astype(jnp.float32)
    inside = own_patch(rows, points, patches, patch_len)
    spread_back_rows = jnp.where(inside, dot_exact(token_back, unfold), 0.0)
    scaled_back = dot_exact(belongs_back(rows, count, patches, jnp.float32), spread_back_rows)
    kept_back = scaled_back * kept
    point_back = kept_back / sigma
    sigma_back = jnp.sum(sigma_sum_ref[...], axis=1, keepdims=True)
    center_back = jnp.sum(center_sum_ref[...], axis=1, keepdims=True)
    center_total = center_back - jnp.sum(point_back, axis=1, keepdims=True)
    sigma_total = sigma_back - jnp.sum(kept_back * shifted, axis=1, keepdims=True) / (sigma * sigma)
    spread_grad = jnp.where(spread > 1.0, sigma_total * 0.5 / sigma, 0.0)
    offset_sum = jnp.sum(hot_kept * 2.0 * shifted, axis=1, keepdims=True)
    center_all = center_total - spread_grad * offset_sum / kept_count
    series_grad_ref[...] = point_back + hot_kept * (center_all + 2.0 * shifted * spread_grad) / kept_count
    for copy in stores:
        copy.wait()


def back(place, lengths, series, flags, tables, weights, kept_values, heads):
    lift, mix, skip, gain_first, joint, merge = weights
    tokens, logsum, sigma_sum, center_sum, second_sum, embedded, middle, turned = kept_values
    rows, width = embedded.shape
    half = width // 2
    f32, bf16 = jnp.float32, jnp.bfloat16
    vmem = pl.BlockSpec(memory_space=pltpu.VMEM)
    smem = pl.BlockSpec(memory_space=pltpu.SMEM)
    hbm = pl.BlockSpec(memory_space=pl.ANY)
    shape = jax.ShapeDtypeStruct
    packs = [
        (3 * width, rows),
        (2 * width + lift.shape[0], rows),
        (2 * half, rows),
        (half, BLOCK),
        (half, BLOCK),
    ]
    scratch = [
        pltpu.VMEM(lift.shape, bf16),
        pltpu.VMEM(mix.shape, bf16),
        pltpu.VMEM(skip.shape, bf16),
        pltpu.VMEM(joint.shape, bf16),
        pltpu.VMEM(merge.shape, bf16),
        pltpu.VMEM((rows, width), f32),
        pltpu.VMEM((width, rows), bf16),
        pltpu.VMEM((3 * width, rows), bf16),
        pltpu.VMEM((rows, width), f32),
        pltpu.VMEM((rows, BLOCK), f32),
        pltpu.VMEM((width, rows), bf16),
    ] + [pltpu.VMEM(pack, f32) for pack in packs]
    scratch += [pltpu.VMEM((width, BLOCK), f32), pltpu.SemaphoreType.DMA((6,)), pltpu.SemaphoreType.DMA((5,))]
    return pl.pallas_call(
        functools.partial(back_kernel, heads),
        out_shape=[shape(series.shape, f32)] + [shape(pack, f32) for pack in packs],
        in_specs=[smem, smem] + [vmem] * 12 + [hbm] * 6,
        out_specs=[vmem] + [hbm] * 5,
        scratch_shapes=scratch,
        compiler_params=pltpu.CompilerParams(vmem_limit_bytes=62 * 1024 * 1024),
        cost_estimate=pl.CostEstimate(flops=6_000_000_000, bytes_accessed=35_000_000, transcendentals=1_000_000),
    )(
        lengths,
        place,
        series,
        flags,
        gain_first.reshape(1, width),
        *tables,
        tokens,
        logsum,
        sigma_sum,
        center_sum,
        second_sum,
        middle,
        turned,
        embedded,
        lift,
        mix,
        skip,
        joint,
        merge,
    )


def gradient_kernel(groups_ref, *refs, terms, inputs, unit):
    arrays, (send_ref, keep_ref), scratch = refs[:inputs], refs[inputs : inputs + 2], refs[inputs + 2 :]
    step = pl.program_id(0)
    matrices = [term for term in terms if term[7] != "sum"]

    @pl.when(step == 0)
    def _():
        for at, (own, own_row, other, other_row, near, far, row, kind, width, _) in enumerate(matrices):
            left, right = scratch[2 * at], scratch[2 * at + 1]
            rows = left.shape[1] // 2
            for slot in range(4):
                first = groups_ref[slot] * unit
                mine = pl.multiple_of(own_row + first, 16)
                theirs = pl.multiple_of(other_row + first, 16)
                span = slice(slot * unit, (slot + 1) * unit)
                left[span, :rows] = arrays[own][pl.ds(mine, unit), :].astype(jnp.bfloat16)
                left[span, rows:] = arrays[other][pl.ds(theirs, unit), :].astype(jnp.bfloat16)
            for place, source in ((0, near), (rows, far)):
                if kind == "tiles":
                    for tile in range(width // rows):
                        begin = row + tile * rows
                        right[place : place + rows, tile * rows : (tile + 1) * rows] = arrays[source][
                            begin : begin + rows, :
                        ].astype(jnp.bfloat16)
                elif kind == "turned":
                    right[:, place : place + rows] = arrays[source][row : row + width, :].astype(jnp.bfloat16)
                else:
                    filled = arrays[source][row : row + width, :].astype(jnp.bfloat16)
                    blank = jnp.zeros_like(filled)
                    stacked = (filled, blank) if kind == "low" else (blank, filled)
                    right[:, place : place + rows] = jnp.concatenate(stacked, axis=0)

    def fill(out_ref, slots):
        for at, (_, _, _, _, _, _, _, kind, width, begin) in enumerate(matrices):
            left = scratch[2 * at][slots[0] * unit : (slots[-1] + 1) * unit, :]
            right = scratch[2 * at + 1][...]
            if kind == "tiles":
                result = dot_plain(left, right)
            else:
                result = dot_over(left, right, 1, 1)
            result = result.reshape(len(slots), unit, result.shape[1])
            if kind == "high":
                out_ref[:, :, begin : begin + result.shape[2]] += result
            else:
                out_ref[:, :, begin : begin + result.shape[2]] = result
        for own, _, other, _, _, _, _, kind, width, begin in terms:
            if kind == "sum":
                for place, slot in enumerate(slots):
                    first = pl.multiple_of(groups_ref[slot] * unit, 16)
                    out_ref[place, :, begin : begin + width] = (
                        arrays[own][pl.ds(first, unit), :] + arrays[other][pl.ds(first, unit), :]
                    )

    @pl.when(step == 0)
    def _():
        fill(send_ref, (0, 1))

    @pl.when(step == 1)
    def _():
        fill(keep_ref, (2, 3))


def weight_gradient(groups, arrays, terms, unit, columns):
    rows = arrays[0][0].shape[1]
    blocks = [
        pl.BlockSpec((height, array.shape[1]), lambda i, s, at=at: (at, 0), pipeline_mode=pl.Buffered(1))
        for array, height, at in arrays
    ]
    out_block = pl.BlockSpec((2, unit, columns), lambda i, s: (0, 0, 0))
    out_type = jax.ShapeDtypeStruct((2, unit, columns), jnp.float32)
    scratch = []
    for term in terms:
        kind, width = term[7], term[8]
        if kind == "sum":
            continue
        scratch.append(pltpu.VMEM((4 * unit, 2 * rows), jnp.bfloat16))
        if kind == "tiles":
            scratch.append(pltpu.VMEM((2 * rows, width), jnp.bfloat16))
        else:
            scratch.append(pltpu.VMEM((width if kind == "turned" else 2 * width, 2 * rows), jnp.bfloat16))
    moved = sum(height * array.shape[1] * 4 for array, height, _ in arrays) + 4 * unit * columns * 4
    return pl.pallas_call(
        functools.partial(gradient_kernel, terms=terms, inputs=len(arrays), unit=unit),
        grid_spec=pltpu.PrefetchScalarGridSpec(
            num_scalar_prefetch=1,
            grid=(2,),
            in_specs=blocks,
            out_specs=[out_block, out_block],
            scratch_shapes=scratch,
        ),
        out_shape=[out_type, out_type],
        compiler_params=pltpu.CompilerParams(vmem_limit_bytes=50 * 1024 * 1024),
        cost_estimate=pl.CostEstimate(
            flops=2 * 2 * rows * 4 * unit * columns, bytes_accessed=moved, transcendentals=0
        ),
    )(groups, *(array for array, _, _ in arrays))


class Layout:
    def __init__(self, mesh_shape):
        self.wide = mesh_shape["wide"]
        self.narrow = mesh_shape["narrow"]
        self.total = self.wide * self.narrow
        self.paired = self.wide == 8 and self.narrow == 4

    def flip(self, bit):
        return [(i, i ^ bit) for i in range(self.total)]

    def middle(self):
        swapped = (0, 2, 1, 3)
        return [(i, (i & ~3) | swapped[i & 3]) for i in range(self.total)]

    def position(self):
        wide = lax.axis_index("wide")
        narrow = lax.axis_index("narrow")
        return {"y": wide // 4, "x": (wide // 2) % 2, "core": wide % 2, "z": narrow % 2}


def first_groups(place, axis):
    y, x = place["y"], place["x"]
    if axis == "x":
        order = [1 - x, 2 + 1 - x, x, 2 + x]
    else:
        order = [2 * (1 - y), 2 * (1 - y) + 1, 2 * y, 2 * y + 1]
    return jnp.stack(order).astype(jnp.int32)


def pick(array, axis, index):
    return lax.dynamic_index_in_dim(array, index, axis, keepdims=False)


def sum_over_chips(layout, place, send, keep, order):
    first = order[0]
    unit, columns = send.shape[1:]
    rows = unit // 4
    held = keep + lax.ppermute(send, AXES, layout.flip({"x": 8, "y": 16}[first]))
    held = held.reshape(2, 2, 2, rows, columns)
    axes = ["y" if first == "x" else "x", "half", "part"]
    for axis in order[1:]:
        if axis == "z":
            for name in ("half", "part"):
                at = axes.index(name)
                moved = lax.ppermute(pick(held, at, 1 - place["z"]), AXES, layout.flip(1))
                held = pick(held, at, place["z"]) + moved
                axes.remove(name)
                if name == "half":
                    held = lax.ppermute(held, AXES, layout.middle())
        else:
            at = axes.index(axis)
            moved = lax.ppermute(pick(held, at, 1 - place[axis]), AXES, layout.flip({"x": 8, "y": 16}[axis]))
            held = pick(held, at, place[axis]) + moved
            axes.remove(axis)
    return held


def whole_rows(own, other):
    unit = own.shape[0] // (UNITS // 2)
    pair = jnp.stack([own.reshape(-1, unit, own.shape[1]), other.reshape(-1, unit, own.shape[1])], axis=1)
    return pair.reshape(2 * own.shape[0], own.shape[1])


def whole_tiles(tiles, rows):
    return jnp.concatenate([tiles[at : at + rows] for at in range(0, tiles.shape[0], rows)], axis=1)


def per_device(
    layout,
    series,
    flags,
    lengths,
    lift_weight,
    mix_weight,
    skip_weight,
    gain_first,
    joint_weight,
    merge_weight,
    gain_second,
    grow_weight,
    shrink_weight,
    head_weight,
    cotangent,
):
    count = series.shape[0]
    patches, horizon = cotangent.shape[1:]
    width = mix_weight.shape[0]
    hidden = shrink_weight.shape[0]
    rows = count * patches
    half = width // 2
    tables = rotary_tables(patches, width // HEADS, count)
    place = layout.position()
    core = place["core"] if layout.paired else jnp.zeros_like(place["core"])
    core = jnp.reshape(core, (1,)).astype(jnp.int32)
    weights = (
        lift_weight,
        mix_weight,
        skip_weight,
        gain_first,
        joint_weight,
        merge_weight,
        gain_second,
        grow_weight,
        shrink_weight,
        head_weight,
    )
    (
        predictions,
        tokens,
        logsum,
        sigma_sum,
        center_sum,
        second_sum,
        embedded,
        middle,
        turned,
        early_send,
        early_own,
        shrink_send,
        shrink_own,
        grow_send,
        grow_own,
        merge_send,
        merge_own,
    ) = front(core, lengths, series, flags, cotangent.reshape(rows, horizon), tables, weights, HEADS)
    series_grad, joint_send, mix_send, mix_own, vector_send, vector_own = back(
        core,
        lengths,
        series,
        flags,
        tables,
        (lift_weight, mix_weight, skip_weight, gain_first, joint_weight, merge_weight),
        (tokens, logsum, sigma_sum, center_sum, second_sum, embedded, middle, turned),
        HEADS,
    )
    across = lift_weight.shape[0]
    joint_width = joint_weight.shape[1]
    if layout.paired:
        swap = lambda array: lax.ppermute(array, AXES, layout.flip(4))
        unit = width // UNITS
        whole = lambda array: (array, array.shape[0], 0)
        shrink_got, grow_got, merge_got, early_got = swap(shrink_send), swap(grow_send), swap(merge_send), swap(early_send)
        joint_got, mix_got, vector_got = swap(joint_send), swap(mix_send), swap(vector_send)

        def piece(order, arrays, terms, columns):
            send, keep = weight_gradient(first_groups(place, order[0]), arrays, terms, unit, columns)
            return sum_over_chips(layout, place, send, keep, order)

        shrink_rows = piece(
            "xzy",
            [whole(shrink_own), whole(shrink_send), whole(shrink_got)],
            ((0, 0, 2, 0, 1, 2, half, "tiles", hidden, 0),),
            hidden,
        )
        grow_head = piece(
            "yzx",
            [whole(grow_own), whole(grow_send), whole(grow_got)],
            (
                (0, 0, 2, 0, 1, 2, half, "tiles", hidden, 0),
                (0, half, 2, half + hidden, 1, 2, width + hidden, "turned", horizon, hidden),
            ),
            hidden + horizon,
        )
        merge_grad = piece(
            "xyz",
            [whole(merge_own), whole(merge_send), whole(merge_got)],
            ((0, 0, 2, 0, 1, 2, half, "tiles", width, 0),),
            width,
        )
        span = joint_width // 2
        joint_parts = [
            piece(
                order,
                [(early_own, half, 0), (early_got, half, 0), (joint_send, span, at), (joint_got, span, at)],
                ((0, 0, 1, 0, 2, 3, 0, "turned", span, 0),),
                span,
            )
            for at, order in enumerate(("yxz", "xyz"))
        ]
        mix_small = piece(
            "yzx",
            [
                (early_own, half, 1),
                (early_got, half, 1),
                whole(mix_own),
                whole(mix_send),
                whole(mix_got),
                whole(vector_own),
                whole(vector_got),
            ],
            (
                (0, 0, 1, 0, 3, 4, 0, "tiles", width, 0),
                (2, half, 4, width + half, 3, 4, 2 * width, "low", across, width),
                (2, 0, 4, width, 3, 4, 2 * width, "high", across, width),
                (5, 0, 6, 0, 0, 0, 0, "sum", BLOCK, width + 2 * across),
            ),
            width + 2 * across + BLOCK,
        )
        grow_grad, head_grad = grow_head[:, :hidden], grow_head[:, hidden:]
        joint_grad = jnp.concatenate(joint_parts, axis=1)
        mix_grad = mix_small[:, :width]
        lift_rows = mix_small[:, width : width + across]
        skip_rows = mix_small[:, width + across : width + 2 * across]
        second_grad = mix_small[:, width + 2 * across]
        first_grad = mix_small[:, width + 2 * across + 1]
    else:
        scatter = lambda left, right: lax.psum_scatter(
            dot_plain(left.astype(jnp.bfloat16), right.astype(jnp.bfloat16)), AXES, scatter_dimension=0, tiled=True
        )
        branch_back = whole_rows(shrink_own, shrink_send[:half])
        normed_two = whole_rows(grow_own[:half], grow_send[:half])
        resid_low = whole_rows(grow_own[half:], grow_send[half + hidden : width + hidden])
        mixed = whole_rows(merge_own, merge_send[:half])
        normed_one = whole_rows(early_own[:half], early_send[:half])
        hidden_act = whole_rows(early_own[half:], early_send[half:])
        embed_low = whole_rows(mix_own[:half], mix_send[width : width + half])
        pre_back = whole_rows(mix_own[half:], mix_send[width + half : 2 * width])
        shrink_rows = scatter(branch_back, whole_tiles(shrink_send[half:], rows))
        grow_grad = scatter(normed_two, whole_tiles(grow_send[half : half + hidden], rows))
        head_grad = scatter(resid_low, grow_send[width + hidden :].T)
        merge_grad = scatter(mixed, whole_tiles(merge_send[half:], rows))
        joint_grad = scatter(normed_one, joint_send.T)
        mix_grad = scatter(hidden_act, whole_tiles(mix_send[:width], rows))
        lift_rows = scatter(pre_back, tokens)
        skip_rows = scatter(embed_low, tokens)
        sums = lax.psum_scatter(whole_rows(vector_own, vector_send), AXES, scatter_dimension=0, tiled=True)
        second_grad, first_grad = sums[:, 0], sums[:, 1]
    return (
        predictions.reshape(count, patches, horizon),
        series_grad,
        lift_rows.T,
        mix_grad,
        skip_rows.T,
        first_grad,
        joint_grad,
        merge_grad,
        second_grad,
        grow_grad,
        shrink_rows.T,
        head_grad,
    )


def solution(mesh):
    both = P(AXES)
    in_specs = (both, both, both) + (P(),) * 10 + (both,)
    out_specs = (
        P(AXES, None, None),
        P(AXES, None),
        P(None, AXES),
        P(AXES, None),
        P(None, AXES),
        P(AXES),
        P(AXES, None),
        P(AXES, None),
        P(AXES),
        P(AXES, None),
        P(None, AXES),
        P(AXES, None),
    )
    return jax.shard_map(
        functools.partial(per_device, Layout(mesh.shape)),
        mesh=mesh,
        in_specs=in_specs,
        out_specs=out_specs,
        check_vma=False,
    )
```

time: 536 us -> 337 us (0.63); the launches traced: 526 us -> 337 us
  blocking collectives: 104 us -> 0 us
  waiting for transfers between devices: 105 us -> 167 us
  matrix products: 55.4 us -> 0 us
  starting transfers between devices: 102 us -> 55.8 us
  local copies, waits for them, and re-layouts: 60.9 us -> 15.8 us
  Pallas kernels: 43.1 us -> 83.6 us
  other arithmetic: 53.1 us -> 13.1 us
    unnamed x1 -> x0, blocking collectives: 104 us -> none
    ppermute x6, waiting for transfers between devices: 0.02 us -> 63 us  [sum_over_chips(): lax.ppermute(send, AXES, layout.flip({'x': 8, 'y': 16}[first]))]
    dot_general x22 -> x0, matrix products: 55.4 us -> none  [the longest x8 19.7 us: product_back(): lax.dot_general(left_side, right_side, (((1,), (1,)), ((), ())), preferre...]
    ppermute x12, starting transfers between devices: 74.6 us -> 31.6 us  [sum_over_chips(): moved = lax.ppermute(pick(held, at, 1 - place['z']), AXES, layout.flip(1))]
    pallas_call x6 -> x8, Pallas kernels: 43.1 us -> 83.6 us  [the longest x6 37.6 us: weight_gradient(): pl.pallas_call(functools.partial(gradient_kernel, terms=terms, inputs=len...]
    reshape x12 -> x2, local copies, waits for them, and re-layouts: 28.2 us -> 2.59 us  [the longest x1 1.29 us: front(): gain_first.reshape(1, width)]
    convert_element_type x10 -> x0, other arithmetic: 13.4 us -> none  [the longest x8 10.2 us: to_other_core(): return lax.ppermute(array.astype(jnp.float32), AXES, layout.flip(4))]
    another operation x5 -> x2, other arithmetic: 6.03 us -> 0.15 us  [first_groups(): return jnp.stack(order).astype(jnp.int32)]
  transfers between devices with their start and end apart: 45 -> 37, of which waited for: 12 -> 16; matrix products, arithmetic and copies ran while one was open for 15% -> 5% of each run, Pallas kernels for 8% -> 18%
where the time goes in v2:
time: 337 us
  waiting for transfers between devices  167 us (50%)
  Pallas kernels  83.6 us (25%)
  starting transfers between devices  55.8 us (17%)
  local copies, waits for them, and re-layouts  15.8 us (5%)
  other arithmetic  13.1 us (4%)
    ppermute x6, waiting for transfers between devices, sum_over_chips(): lax.ppermute(send, AXES, layout.flip({'x': 8, 'y': 16}[first]))  63 us
    ppermute x12, waiting for transfers between devices, sum_over_chips(): moved = lax.ppermute(pick(held, at, 1 - place['z']), AXES, layout.flip(1))  55.9 us
    ppermute x6, waiting for transfers between devices, sum_over_chips(): lax.ppermute(pick(held, at, 1 - place[axis]), AXES, layout.flip({'x': 8,...  43.3 us
    pallas_call x6, Pallas kernels, weight_gradient(): pl.pallas_call(functools.partial(gradient_kernel, terms=terms, inputs=len...  37.6 us
    ppermute x12, starting transfers between devices, sum_over_chips(): moved = lax.ppermute(pick(held, at, 1 - place['z']), AXES, layout.flip(1))  31.6 us
    pallas_call x1, Pallas kernels, front(): pl.pallas_call(functools.partial(front_kernel, heads), out_shape=outs, in...  23.4 us
    pallas_call x1, Pallas kernels, back(): pl.pallas_call(functools.partial(back_kernel, heads), out_shape=[shape(se...  22.6 us
    ppermute x6, starting transfers between devices, sum_over_chips(): lax.ppermute(pick(held, at, 1 - place[axis]), AXES, layout.flip({'x': 8,...  8.38 us
  transfers between devices with their start and end apart: 37, of which 16 were waited for; matrix products, arithmetic and copies ran while one was open for 5% of the time, Pallas kernels for 18%

profile of v2, /device:TPU:0, one launch (start us, length us, event | category | flops | bytes accessed | tf_op | source)
XLA Modules:
  0.0 336.7 jit_solution(2141114673589662916)
XLA Ops:
  0.7 1.3 reshape.60.gain_first_ref
  1.9 1.3 reshape.61.gain_second_ref
  3.2 23.4 %shard_map.247 = (f32[256,128]{1,0:T(8,128)}, bf16[256,64]{1,0:T(8,128)(2,1)}, f32[16,256]{1,0:T(8,128)}, f32[16,128]{1,0:T(8,128)}, f32[16,128]{1,0:T(8,128)}, ...) custom-call(s32[16]{0:T(128)} %lengths_ref.3, ...), custom_call_target="tpu_custom_call" | custom-call | flops 8999999488 | bytes 45000000 | tf_op jit(solution)/shard_map/pallas_call | solution.py:411
  27.7 5.2 %collective-permute-done.19.refs_2_ = f32[1920,256]{1,0:T(8,128)S(1)} collective-permute-done((f32[1920,256]{1,0:T(8,128)}, f32[1920,256]{1,0:T(8,128)S(1)}, u32[]{:S(2)}, u32[]{:S(2)}) %collective-permute-start.19) | collective-permute-done | bytes 1966112 | tf_op jit(solution)/shard_map/ppermute | solution.py:932
  33.0 1.3 copy-done.10
  34.2 1.1 copy-done.4
  35.3 5.1 %shard_map.252 = (f32[2,160,1280]{2,1,0:T(8,128)}, f32[2,160,1280]{2,1,0:T(8,128)S(1)}) custom-call(s32[4]{0:T(128)S(1)} %pad_add_fusion.1.groups_ref, f32[640,256]{1,0:T(8,128)S(1)} %copy-done.4, f32[1920,256]{1,0:T(8,128)} %get-tuple-element.71.refs_1_, f32[1920,256]{1,0:T(8,128)} %copy-done.10), custom_call_target="tpu_custom_call" | custom-call | flops 838860800 | bytes 7864320 | tf_op jit(solution)/shard_map/pallas_call | solution.py:777
  40.4 1.2 copy-done.1
  41.6 2.9 collective-permute-start.20
  44.5 22.6 %shard_map.248 = (f32[16,512]{1,0:T(8,128)}, f32[3840,256]{1,0:T(8,128)}, f32[2624,256]{1,0:T(8,128)}, f32[1280,256]{1,0:T(8,128)}, f32[640,128]{1,0:T(8,128)}, /*index=5*/f32[640,128]{1,0:T(8,128)}) custom-call(s32[16]{0:T(128)} %lengths_ref.3, s32[1]{0:T(128)} %bitcast.place_ref, f32[16,512]{1,0:T(8,128)} %series_ref.3, s32[16,512]{1,0:T(8,128)} %flags_ref.3, ...), custom_call_target="tpu_custom_call" | custom-call | flops 6000000000 | bytes 35000000 | tf_op jit(solution)/shard_map/pallas_call | solution.py:665
  67.6 1.1 copy-done.3
  68.7 5.1 %shard_map.254 = (f32[2,160,1280]{2,1,0:T(8,128)}, f32[2,160,1280]{2,1,0:T(8,128)S(1)}) custom-call(s32[4]{0:T(128)S(1)} %pad_add_fusion.1.groups_ref, f32[640,256]{1,0:T(8,128)S(1)} %copy-done.3, f32[1920,256]{1,0:T(8,128)} %get-tuple-element.79.refs_1_, f32[1920,256]{1,0:T(8,128)} %collective-permute-done.31.refs_2_), custom_call_target="tpu_custom_call" | custom-call | flops 838860800 | bytes 7864320 | tf_op jit(solution)/shard_map/pallas_call | solution.py:777
  73.9 7.5 %collective-permute-done.20 = f32[2,160,1280]{2,1,0:T(8,128)} collective-permute-done((f32[2,160,1280]{2,1,0:T(8,128)}, f32[2,160,1280]{2,1,0:T(8,128)}, u32[]{:S(2)}, u32[]{:S(2)}) %collective-permute-start.20) | collective-permute-done | bytes 1638432 | tf_op jit(solution)/shard_map/ppermute | solution.py:831
  81.4 2.1 add.185
  83.5 1.2 copy-done.6
  84.7 1.0 dynamic-slice_bitcast_fusion.5
  85.7 2.1 collective-permute-start.21
  87.9 1.3 copy-done.2
  89.2 6.5 %shard_map.253 = (f32[2,160,1408]{2,1,0:T(8,128)}, f32[2,160,1408]{2,1,0:T(8,128)}) custom-call(s32[4]{0:T(128)S(1)} %pad_add_fusion.groups_ref, f32[1280,256]{1,0:T(8,128)S(1)} %copy-done.2, f32[2688,256]{1,0:T(8,128)} %get-tuple-element.75.refs_1_, f32[2688,256]{1,0:T(8,128)} %collective-permute-done.25.refs_2_), custom_call_target="tpu_custom_call" | custom-call | flops 922746880 | bytes 10420224 | tf_op jit(solution)/shard_map/pallas_call | solution.py:777
  95.7 20.3 %collective-permute-done.32 = f32[2,160,1280]{2,1,0:T(8,128)} collective-permute-done((f32[2,160,1280]{2,1,0:T(8,128)}, f32[2,160,1280]{2,1,0:T(8,128)}, u32[]{:S(2)}, u32[]{:S(2)}) %collective-permute-start.32) | collective-permute-done | bytes 1638432 | tf_op jit(solution)/shard_map/ppermute | solution.py:831
  116.0 1.8 collective-permute-start.26
  117.8 1.6 add.193
  119.5 1.6 collective-permute-start.33
  121.2 7.2 %shard_map.249 = (f32[2,160,1536]{2,1,0:T(8,128)}, f32[2,160,1536]{2,1,0:T(8,128)}) custom-call(s32[4]{0:T(128)S(1)} %pad_add_fusion.groups_ref, f32[1280,256]{1,0:T(8,128)S(1)} %copy-done, f32[1280,256]{1,0:T(8,128)S(1)} %collective-permute-done.refs_1_, f32[1280,256]{1,0:T(8,128)} %get-tuple-element.59.refs_2_, f32[2624,256]{1,0:T(8,128)} %get-tuple-element.60.refs_3_, ...), custom_call_target="tpu_custom_call" | custom-call | flops 1006632960 | bytes 12582912 | tf_op jit(solution)/shard_map/pallas_call | solution.py:777
  128.9 1.2 bitcast_add_fusion.5
  130.2 1.2 collective-permute-start.22
  131.4 9.3 %collective-permute-done.33 = f32[2,2,40,1280]{3,2,1,0:T(8,128)S(1)} collective-permute-done((f32[2,2,40,1280]{3,2,1,0:T(8,128)S(1)}, f32[2,2,40,1280]{3,2,1,0:T(8,128)S(1)}, u32[]{:S(2)}, u32[]{:S(2)}) %collective-permute-start.33) | collective-permute-done | bytes 819232 | tf_op jit(solution)/shard_map/ppermute | solution.py:838
  140.8 1.0 bitcast_add_fusion.4
  141.8 1.8 collective-permute-start.34
  143.6 15.0 %collective-permute-done.26 = f32[2,160,1408]{2,1,0:T(8,128)} collective-permute-done((f32[2,160,1408]{2,1,0:T(8,128)}, f32[2,160,1408]{2,1,0:T(8,128)}, u32[]{:S(2)}, u32[]{:S(2)}) %collective-permute-start.26) | collective-permute-done | bytes 1802272 | tf_op jit(solution)/shard_map/ppermute | solution.py:831
  158.6 1.7 add.189
  160.4 1.9 collective-permute-start.27
  162.3 1.4 collective-permute-start.23
  163.7 6.9 %shard_map.251 = (f32[2,160,1920]{2,1,0:T(8,128)}, f32[2,160,1920]{2,1,0:T(8,128)}) custom-call(s32[4]{0:T(128)S(1)} %pad_add_fusion.1.groups_ref, f32[1280,256]{1,0:T(8,128)S(1)} %copy-done, f32[1280,256]{1,0:T(8,128)S(1)} %collective-permute-done.refs_1_, f32[3840,256]{1,0:T(8,128)} %get-tuple-element.65.refs_2_, f32[3840,256]{1,0:T(8,128)} %collective-permute-done.8.refs_3_), custom_call_target="tpu_custom_call" | custom-call | flops 1258291200 | bytes 10158080 | tf_op jit(solution)/shard_map/pallas_call | solution.py:777
  170.7 1.5 collective-permute-start.14
  172.2 6.8 %shard_map.250 = (f32[2,160,1920]{2,1,0:T(8,128)}, f32[2,160,1920]{2,1,0:T(8,128)}) custom-call(s32[4]{0:T(128)S(1)} %pad_add_fusion.groups_ref, f32[1280,256]{1,0:T(8,128)S(1)} %copy-done, f32[1280,256]{1,0:T(8,128)S(1)} %collective-permute-done.refs_1_, f32[3840,256]{1,0:T(8,128)} %get-tuple-element.65.refs_2_, f32[3840,256]{1,0:T(8,128)} %collective-permute-done.8.refs_3_), custom_call_target="tpu_custom_call" | custom-call | flops 1258291200 | bytes 10158080 | tf_op jit(solution)/shard_map/pallas_call | solution.py:777
  179.0 20.2 %collective-permute-done.3 = f32[2,160,1536]{2,1,0:T(8,128)S(1)} collective-permute-done((f32[2,160,1536]{2,1,0:T(8,128)}, f32[2,160,1536]{2,1,0:T(8,128)S(1)}, u32[]{:S(2)}, u32[]{:S(2)}) %collective-permute-start.3) | collective-permute-done | bytes 1966112 | tf_op jit(solution)/shard_map/ppermute | solution.py:831
  199.2 1.5 collective-permute-start.9
  201.1 1.6 collective-permute-start.4
  202.7 0.9 dynamic-slice_bitcast_fusion.17
  204.2 1.6 collective-permute-start.35
  206.0 19.9 %collective-permute-done.4 = f32[2,2,40,1536]{3,2,1,0:T(8,128)S(1)} collective-permute-done((f32[2,2,40,1536]{3,2,1,0:T(8,128)S(1)}, f32[2,2,40,1536]{3,2,1,0:T(8,128)S(1)}, u32[]{:S(2)}, u32[]{:S(2)}) %collective-permute-start.4) | collective-permute-done | bytes 983072 | tf_op jit(solution)/shard_map/ppermute | solution.py:838
  226.7 9.4 %collective-permute-done.35 = f32[2,40,1280]{2,1,0:T(8,128)S(1)} collective-permute-done((f32[2,40,1280]{2,1,0:T(8,128)S(1)}, f32[2,40,1280]{2,1,0:T(8,128)S(1)}, u32[]{:S(2)}, u32[]{:S(2)}) %collective-permute-start.35) | collective-permute-done | bytes 409632 | tf_op jit(solution)/shard_map/ppermute | solution.py:838
  236.1 0.7 collective-permute-start.5
  236.9 1.0 collective-permute-start.36
  237.9 1.6 bitcast_add_fusion.17
  239.5 18.3 %collective-permute-done.36 = f32[40,1280]{1,0:T(8,128)S(1)} collective-permute-done((f32[40,1280]{1,0:T(8,128)S(1)}, f32[40,1280]{1,0:T(8,128)S(1)}, u32[]{:S(2)}, u32[]{:S(2)}) %collective-permute-start.36) | collective-permute-done | bytes 204832 | tf_op jit(solution)/shard_map/ppermute | solution.py:845
  257.8 0.7 fusion
  258.5 1.2 collective-permute-start.29
  260.2 1.6 collective-permute-start.15
  262.1 4.5 %collective-permute-start.6 = (f32[2,40,1536]{2,1,0:T(8,128)S(1)}, f32[2,40,1536]{2,1,0:T(8,128)S(1)}, u32[]{:S(2)}, u32[]{:S(2)}) collective-permute-start(f32[2,40,1536]{2,1,0:T(8,128)S(1)} %dynamic-slice_bitcast_fusion.8), channel_id=1, source_target_pairs={{0,1},{1,0},{2,3},{3,2},{4,5},{5,4},{6,7},{7,6},{8,9},{9,8},{10,11... | collective-permute-start | bytes 1474568 | tf_op jit(solution)/shard_map/ppermute | solution.py:838
  266.6 5.2 %collective-permute-done.29 = f32[2,40,1408]{2,1,0:T(8,128)S(1)} collective-permute-done((f32[2,40,1408]{2,1,0:T(8,128)S(1)}, f32[2,40,1408]{2,1,0:T(8,128)S(1)}, u32[]{:S(2)}, u32[]{:S(2)}) %collective-permute-start.29) | collective-permute-done | bytes 450592 | tf_op jit(solution)/shard_map/ppermute | solution.py:838
  271.9 1.1 collective-permute-start.30
  273.2 1.0 collective-permute-start.10
  274.2 6.3 %collective-permute-done.30 = f32[40,1408]{1,0:T(8,128)S(1)} collective-permute-done((f32[40,1408]{1,0:T(8,128)S(1)}, f32[40,1408]{1,0:T(8,128)S(1)}, u32[]{:S(2)}, u32[]{:S(2)}) %collective-permute-start.30) | collective-permute-done | bytes 225312 | tf_op jit(solution)/shard_map/ppermute | solution.py:845
  281.9 4.5 %collective-permute-done.15 = f32[2,2,40,1920]{3,2,1,0:T(8,128)S(1)} collective-permute-done((f32[2,2,40,1920]{3,2,1,0:T(8,128)S(1)}, f32[2,2,40,1920]{3,2,1,0:T(8,128)S(1)}, u32[]{:S(2)}, u32[]{:S(2)}) %collective-permute-start.15) | collective-permute-done | bytes 1228832 | tf_op jit(solution)/shard_map/ppermute | solution.py:845
  286.6 1.3 collective-permute-start.16
  287.9 14.2 %collective-permute-done.10 = f32[2,2,40,1920]{3,2,1,0:T(8,128)S(1)} collective-permute-done((f32[2,2,40,1920]{3,2,1,0:T(8,128)S(1)}, f32[2,2,40,1920]{3,2,1,0:T(8,128)S(1)}, u32[]{:S(2)}, u32[]{:S(2)}) %collective-permute-start.10) | collective-permute-done | bytes 1228832 | tf_op jit(solution)/shard_map/ppermute | solution.py:845
  302.9 1.6 collective-permute-start.7
  305.2 7.3 %collective-permute-done.11 = f32[2,40,1920]{2,1,0:T(8,128)S(1)} collective-permute-done((f32[2,40,1920]{2,1,0:T(8,128)S(1)}, f32[2,40,1920]{2,1,0:T(8,128)S(1)}, u32[]{:S(2)}, u32[]{:S(2)}) %collective-permute-start.11) | collective-permute-done | bytes 614432 | tf_op jit(solution)/shard_map/ppermute | solution.py:838
  314.8 9.0 %collective-permute-start.18 = (f32[40,1920]{1,0:T(8,128)S(1)}, f32[40,1920]{1,0:T(8,128)S(1)}, u32[]{:S(2)}, u32[]{:S(2)}) collective-permute-start(f32[40,1920]{1,0:T(8,128)S(1)} %dynamic-slice_bitcast_fusion.12), channel_id=1, source_target_pairs={{0,1},{1,0},{2,3},{3,2},{4,5},{5,4},{6,7},{7,6},{8,9},{9,8},{10,11... | collective-permute-start | bytes 921608 | tf_op jit(solution)/shard_map/ppermute | solution.py:838
  324.5 6.4 %collective-permute-start.13 = (f32[40,1920]{1,0:T(8,128)S(1)}, f32[40,1920]{1,0:T(8,128)S(1)}, u32[]{:S(2)}, u32[]{:S(2)}) collective-permute-start(f32[40,1920]{1,0:T(8,128)S(1)} %dynamic-slice_bitcast_fusion.13), channel_id=1, source_target_pairs={{0,1},{1,0},{2,3},{3,2},{4,5},{5,4},{6,7},{7,6},{8,9},{9,8},{10,11... | collective-permute-start | bytes 921608 | tf_op jit(solution)/shard_map/ppermute | solution.py:838
  331.4 4.4 %collective-permute-done.13 = f32[40,1920]{1,0:T(8,128)S(1)} collective-permute-done((f32[40,1920]{1,0:T(8,128)S(1)}, f32[40,1920]{1,0:T(8,128)S(1)}, u32[]{:S(2)}, u32[]{:S(2)}) %collective-permute-start.13) | collective-permute-done | bytes 307232 | tf_op jit(solution)/shard_map/ppermute | solution.py:838
  335.8 0.9 pad_maximum_fusion
  (96 shorter events, 12.1 us)
Async XLA Ops:
  26.6 6.4 %collective-permute-start.19 = (f32[1920,256]{1,0:T(8,128)}, f32[1920,256]{1,0:T(8,128)S(1)}, u32[]{:S(2)}, u32[]{:S(2)}) collective-permute-start(f32[1920,256]{1,0:T(8,128)} %get-tuple-element.71.refs_1_), channel_id=1, source_target_pairs={{0,4},{1,5},{2,6},{3,7},{4,0},{5,1},{6,2},{7,3},{8,12},{9,13},{10,... | collective-permute-start | bytes 5898248 | tf_op jit(solution)/shard_map/ppermute | solution.py:932
  27.1 40.5 %collective-permute-start.31 = (f32[1920,256]{1,0:T(8,128)}, f32[1920,256]{1,0:T(8,128)}, u32[]{:S(2)}, u32[]{:S(2)}) collective-permute-start(f32[1920,256]{1,0:T(8,128)} %get-tuple-element.79.refs_1_), channel_id=1, source_target_pairs={{0,4},{1,5},{2,6},{3,7},{4,0},{5,1},{6,2},{7,3},{8,12},{9,13},{10,... | collective-permute-start | bytes 5898248 | tf_op jit(solution)/shard_map/ppermute | solution.py:932
  27.2 58.5 %collective-permute-start.25 = (f32[2688,256]{1,0:T(8,128)}, f32[2688,256]{1,0:T(8,128)}, u32[]{:S(2)}, u32[]{:S(2)}) collective-permute-start(f32[2688,256]{1,0:T(8,128)} %get-tuple-element.75.refs_1_), channel_id=1, source_target_pairs={{0,4},{1,5},{2,6},{3,7},{4,0},{5,1},{6,2},{7,3},{8,12},{9,13},{10,... | collective-permute-start | bytes 8257544 | tf_op jit(solution)/shard_map/ppermute | solution.py:932
  33.0 1.3 copy-start.10
  34.2 1.1 copy-start.4
  40.4 1.2 copy-start.1
  41.6 39.8 %collective-permute-start.20 = (f32[2,160,1280]{2,1,0:T(8,128)}, f32[2,160,1280]{2,1,0:T(8,128)}, u32[]{:S(2)}, u32[]{:S(2)}) collective-permute-start(f32[2,160,1280]{2,1,0:T(8,128)} %get-tuple-element.73), channel_id=1, source_target_pairs={{0,8},{1,9},{2,10},{3,11},{4,12},{5,13},{6,14},{7,15},{8,0},{9,1},... | collective-permute-start | bytes 4915208 | tf_op jit(solution)/shard_map/ppermute | solution.py:831
  67.1 54.1 %collective-permute-start.1 = (f32[2624,256]{1,0:T(8,128)}, f32[2624,256]{1,0:T(8,128)}, u32[]{:S(2)}, u32[]{:S(2)}) collective-permute-start(f32[2624,256]{1,0:T(8,128)} %get-tuple-element.60.refs_3_), channel_id=1, source_target_pairs={{0,4},{1,5},{2,6},{3,7},{4,0},{5,1},{6,2},{7,3},{8,12},{9,13},{10,... | collective-permute-start | bytes 8060936 | tf_op jit(solution)/shard_map/ppermute | solution.py:932
  67.1 6.7 %collective-permute-start.2 = (f32[640,128]{1,0:T(8,128)}, f32[640,128]{1,0:T(8,128)S(1)}, u32[]{:S(2)}, u32[]{:S(2)}) collective-permute-start(f32[640,128]{1,0:T(8,128)} %get-tuple-element.62), channel_id=1, source_target_pairs={{0,4},{1,5},{2,6},{3,7},{4,0},{5,1},{6,2},{7,3},{8,12},{9,13},{10,... | collective-permute-start | bytes 983048 | tf_op jit(solution)/shard_map/ppermute | solution.py:932
  67.6 1.1 copy-start.3
  73.8 42.2 %collective-permute-start.32 = (f32[2,160,1280]{2,1,0:T(8,128)}, f32[2,160,1280]{2,1,0:T(8,128)}, u32[]{:S(2)}, u32[]{:S(2)}) collective-permute-start(f32[2,160,1280]{2,1,0:T(8,128)} %get-tuple-element.81), channel_id=1, source_target_pairs={{0,8},{1,9},{2,10},{3,11},{4,12},{5,13},{6,14},{7,15},{8,0},{9,1},... | collective-permute-start | bytes 4915208 | tf_op jit(solution)/shard_map/ppermute | solution.py:831
  73.8 89.9 %collective-permute-start.8 = (f32[3840,256]{1,0:T(8,128)}, f32[3840,256]{1,0:T(8,128)}, u32[]{:S(2)}, u32[]{:S(2)}) collective-permute-start(f32[3840,256]{1,0:T(8,128)} %get-tuple-element.65.refs_2_), channel_id=1, source_target_pairs={{0,4},{1,5},{2,6},{3,7},{4,0},{5,1},{6,2},{7,3},{8,12},{9,13},{10,... | collective-permute-start | bytes 11796488 | tf_op jit(solution)/shard_map/ppermute | solution.py:932
  81.4 38.1 %collective-permute-start = (f32[1280,256]{1,0:T(8,128)}, f32[1280,256]{1,0:T(8,128)S(1)}, u32[]{:S(2)}, u32[]{:S(2)}) collective-permute-start(f32[1280,256]{1,0:T(8,128)} %get-tuple-element.58), channel_id=1, source_target_pairs={{0,4},{1,5},{2,6},{3,7},{4,0},{5,1},{6,2},{7,3},{8,12},{9,13},{10,... | collective-permute-start | bytes 3932168 | tf_op jit(solution)/shard_map/ppermute | solution.py:932
  83.5 1.2 copy-start.6
  85.7 43.2 %collective-permute-start.21 = (f32[2,2,40,1280]{3,2,1,0:T(8,128)}, f32[2,2,40,1280]{3,2,1,0:T(8,128)}, u32[]{:S(2)}, u32[]{:S(2)}) collective-permute-start(f32[2,2,40,1280]{3,2,1,0:T(8,128)} %dynamic-slice_bitcast_fusion.5), channel_id=1, source_target_pairs={{0,16},{1,17},{2,18},{3,19},{4,20},{5,21},{6,22},{7,23},{8,24},{9,... | collective-permute-start | bytes 2457608 | tf_op jit(solution)/shard_map/ppermute | solution.py:845
  87.9 1.3 copy-start.2
  116.0 42.5 %collective-permute-start.26 = (f32[2,160,1408]{2,1,0:T(8,128)}, f32[2,160,1408]{2,1,0:T(8,128)}, u32[]{:S(2)}, u32[]{:S(2)}) collective-permute-start(f32[2,160,1408]{2,1,0:T(8,128)} %get-tuple-element.77), channel_id=1, source_target_pairs={{0,16},{1,17},{2,18},{3,19},{4,20},{5,21},{6,22},{7,23},{8,24},{9,... | collective-permute-start | bytes 5406728 | tf_op jit(solution)/shard_map/ppermute | solution.py:831
  119.4 1.7 copy-start
  119.4 1.7 copy-start.5
  119.5 21.2 %collective-permute-start.33 = (f32[2,2,40,1280]{3,2,1,0:T(8,128)S(1)}, f32[2,2,40,1280]{3,2,1,0:T(8,128)S(1)}, u32[]{:S(2)}, u32[]{:S(2)}) collective-permute-start(f32[2,2,40,1280]{3,2,1,0:T(8,128)S(1)} %dynamic-slice_bitcast_fusion.4), channel_id=1, source_target_pairs={{0,1},{1,0},{2,3},{3,2},{4,5},{5,4},{6,7},{7,6},{8,9},{9,8},{10,11... | collective-permute-start | bytes 2457608 | tf_op jit(solution)/shard_map/ppermute | solution.py:838
  121.2 7.7 %copy-start.7 = (f32[2,160,1280]{2,1,0:T(8,128)S(1)}, f32[2,160,1280]{2,1,0:T(8,128)}, u32[]{:S(2)}) copy-start(f32[2,160,1280]{2,1,0:T(8,128)} %copy-done.6) | copy-start | bytes 4915204
  128.4 70.8 %collective-permute-start.3 = (f32[2,160,1536]{2,1,0:T(8,128)}, f32[2,160,1536]{2,1,0:T(8,128)S(1)}, u32[]{:S(2)}, u32[]{:S(2)}) collective-permute-start(f32[2,160,1536]{2,1,0:T(8,128)} %get-tuple-element.64), channel_id=1, source_target_pairs={{0,16},{1,17},{2,18},{3,19},{4,20},{5,21},{6,22},{7,23},{8,24},{9,... | collective-permute-start | bytes 5898248 | tf_op jit(solution)/shard_map/ppermute | solution.py:831
  130.1 28.4 %copy-start.12 = (f32[2,160,1408]{2,1,0:T(8,128)S(1)}, f32[2,160,1408]{2,1,0:T(8,128)}, u32[]{:S(2)}) copy-start(f32[2,160,1408]{2,1,0:T(8,128)} %get-tuple-element.76) | copy-start | bytes 5406724
  130.2 32.1 %collective-permute-start.22 = (f32[2,40,1280]{2,1,0:T(8,128)S(1)}, f32[2,40,1280]{2,1,0:T(8,128)S(1)}, u32[]{:S(2)}, u32[]{:S(2)}) collective-permute-start(f32[2,40,1280]{2,1,0:T(8,128)S(1)} %dynamic-slice_bitcast_fusion.11), channel_id=1, source_target_pairs={{0,1},{1,0},{2,3},{3,2},{4,5},{5,4},{6,7},{7,6},{8,9},{9,8},{10,11... | collective-permute-start | bytes 1228808 | tf_op jit(solution)/shard_map/ppermute | solution.py:838
  141.8 61.9 %collective-permute-start.34 = (f32[2,2,40,1280]{3,2,1,0:T(8,128)}, f32[2,2,40,1280]{3,2,1,0:T(8,128)S(1)}, u32[]{:S(2)}, u32[]{:S(2)}) collective-permute-start(f32[2,2,40,1280]{3,2,1,0:T(8,128)} %bitcast_add_fusion.4), channel_id=1, source_target_pairs={{0,0},{1,2},{2,1},{3,3},{4,4},{5,6},{6,5},{7,7},{8,8},{9,10},{10,9... | collective-permute-start | bytes 2457608 | tf_op jit(solution)/shard_map/ppermute | solution.py:842
  160.4 43.9 %collective-permute-start.27 = (f32[2,2,40,1408]{3,2,1,0:T(8,128)S(1)}, f32[2,2,40,1408]{3,2,1,0:T(8,128)S(1)}, u32[]{:S(2)}, u32[]{:S(2)}) collective-permute-start(f32[2,2,40,1408]{3,2,1,0:T(8,128)S(1)} %dynamic-slice_bitcast_fusion.3), channel_id=1, source_target_pairs={{0,1},{1,0},{2,3},{3,2},{4,5},{5,4},{6,7},{7,6},{8,9},{9,8},{10,11... | collective-permute-start | bytes 2703368 | tf_op jit(solution)/shard_map/ppermute | solution.py:838
  162.3 38.8 %collective-permute-start.23 = (f32[2,40,1280]{2,1,0:T(8,128)S(1)}, f32[2,40,1280]{2,1,0:T(8,128)}, u32[]{:S(2)}, u32[]{:S(2)}) collective-permute-start(f32[2,40,1280]{2,1,0:T(8,128)S(1)} %bitcast_add_fusion.11), channel_id=1, source_target_pairs={{0,0},{1,2},{2,1},{3,3},{4,4},{5,6},{6,5},{7,7},{8,8},{9,10},{10,9... | collective-permute-start | bytes 1228808 | tf_op jit(solution)/shard_map/ppermute | solution.py:842
  170.7 30.0 %copy-start.11 = (f32[2,160,1536]{2,1,0:T(8,128)S(1)}, f32[2,160,1536]{2,1,0:T(8,128)}, u32[]{:S(2)}) copy-start(f32[2,160,1536]{2,1,0:T(8,128)} %get-tuple-element.63) | copy-start | bytes 5898244
  170.7 89.1 %collective-permute-start.14 = (f32[2,160,1920]{2,1,0:T(8,128)}, f32[2,160,1920]{2,1,0:T(8,128)S(1)}, u32[]{:S(2)}, u32[]{:S(2)}) collective-permute-start(f32[2,160,1920]{2,1,0:T(8,128)} %get-tuple-element.69), channel_id=1, source_target_pairs={{0,8},{1,9},{2,10},{3,11},{4,12},{5,13},{6,14},{7,15},{8,0},{9,1},... | collective-permute-start | bytes 7372808 | tf_op jit(solution)/shard_map/ppermute | solution.py:831
  199.2 62.6 %collective-permute-start.9 = (f32[2,160,1920]{2,1,0:T(8,128)}, f32[2,160,1920]{2,1,0:T(8,128)S(1)}, u32[]{:S(2)}, u32[]{:S(2)}) collective-permute-start(f32[2,160,1920]{2,1,0:T(8,128)} %get-tuple-element.67), channel_id=1, source_target_pairs={{0,16},{1,17},{2,18},{3,19},{4,20},{5,21},{6,22},{7,23},{8,24},{9,... | collective-permute-start | bytes 7372808 | tf_op jit(solution)/shard_map/ppermute | solution.py:831
  201.1 24.8 %collective-permute-start.4 = (f32[2,2,40,1536]{3,2,1,0:T(8,128)S(1)}, f32[2,2,40,1536]{3,2,1,0:T(8,128)S(1)}, u32[]{:S(2)}, u32[]{:S(2)}) collective-permute-start(f32[2,2,40,1536]{3,2,1,0:T(8,128)S(1)} %dynamic-slice_bitcast_fusion.2), channel_id=1, source_target_pairs={{0,1},{1,0},{2,3},{3,2},{4,5},{5,4},{6,7},{7,6},{8,9},{9,8},{10,11... | collective-permute-start | bytes 2949128 | tf_op jit(solution)/shard_map/ppermute | solution.py:838
  203.7 33.2 %collective-permute-start.24 = (f32[40,1280]{1,0:T(8,128)S(1)}, f32[40,1280]{1,0:T(8,128)S(1)}, u32[]{:S(2)}, u32[]{:S(2)}) collective-permute-start(f32[40,1280]{1,0:T(8,128)S(1)} %dynamic-slice_bitcast_fusion.17), channel_id=1, source_target_pairs={{0,1},{1,0},{2,3},{3,2},{4,5},{5,4},{6,7},{7,6},{8,9},{9,8},{10,11... | collective-permute-start | bytes 614408 | tf_op jit(solution)/shard_map/ppermute | solution.py:838
  204.2 31.8 %collective-permute-start.35 = (f32[2,40,1280]{2,1,0:T(8,128)S(1)}, f32[2,40,1280]{2,1,0:T(8,128)S(1)}, u32[]{:S(2)}, u32[]{:S(2)}) collective-permute-start(f32[2,40,1280]{2,1,0:T(8,128)S(1)} %dynamic-slice_bitcast_fusion.10), channel_id=1, source_target_pairs={{0,1},{1,0},{2,3},{3,2},{4,5},{5,4},{6,7},{7,6},{8,9},{9,8},{10,11... | collective-permute-start | bytes 1228808 | tf_op jit(solution)/shard_map/ppermute | solution.py:838
  225.8 32.6 %collective-permute-start.28 = (f32[2,2,40,1408]{3,2,1,0:T(8,128)S(1)}, f32[2,2,40,1408]{3,2,1,0:T(8,128)S(1)}, u32[]{:S(2)}, u32[]{:S(2)}) collective-permute-start(f32[2,2,40,1408]{3,2,1,0:T(8,128)S(1)} %bitcast_add_fusion.3), channel_id=1, source_target_pairs={{0,0},{1,2},{2,1},{3,3},{4,4},{5,6},{6,5},{7,7},{8,8},{9,10},{10,9... | collective-permute-start | bytes 2703368 | tf_op jit(solution)/shard_map/ppermute | solution.py:842
  226.7 33.1 %copy-start.9 = (f32[2,160,1920]{2,1,0:T(8,128)S(1)}, f32[2,160,1920]{2,1,0:T(8,128)}, u32[]{:S(2)}) copy-start(f32[2,160,1920]{2,1,0:T(8,128)} %get-tuple-element.68) | copy-start | bytes 7372804
  236.1 26.0 %collective-permute-start.5 = (f32[2,2,40,1536]{3,2,1,0:T(8,128)S(1)}, f32[2,2,40,1536]{3,2,1,0:T(8,128)S(1)}, u32[]{:S(2)}, u32[]{:S(2)}) collective-permute-start(f32[2,2,40,1536]{3,2,1,0:T(8,128)S(1)} %bitcast_add_fusion.2), channel_id=1, source_target_pairs={{0,0},{1,2},{2,1},{3,3},{4,4},{5,6},{6,5},{7,7},{8,8},{9,10},{10,9... | collective-permute-start | bytes 2949128 | tf_op jit(solution)/shard_map/ppermute | solution.py:842
  236.9 20.9 %collective-permute-start.36 = (f32[40,1280]{1,0:T(8,128)S(1)}, f32[40,1280]{1,0:T(8,128)S(1)}, u32[]{:S(2)}, u32[]{:S(2)}) collective-permute-start(f32[40,1280]{1,0:T(8,128)S(1)} %dynamic-slice_bitcast_fusion.16), channel_id=1, source_target_pairs={{0,16},{1,17},{2,18},{3,19},{4,20},{5,21},{6,22},{7,23},{8,24},{9,... | collective-permute-start | bytes 614408 | tf_op jit(solution)/shard_map/ppermute | solution.py:845
  258.5 13.3 %collective-permute-start.29 = (f32[2,40,1408]{2,1,0:T(8,128)S(1)}, f32[2,40,1408]{2,1,0:T(8,128)S(1)}, u32[]{:S(2)}, u32[]{:S(2)}) collective-permute-start(f32[2,40,1408]{2,1,0:T(8,128)S(1)} %dynamic-slice_bitcast_fusion.9), channel_id=1, source_target_pairs={{0,1},{1,0},{2,3},{3,2},{4,5},{5,4},{6,7},{7,6},{8,9},{9,8},{10,11... | collective-permute-start | bytes 1351688 | tf_op jit(solution)/shard_map/ppermute | solution.py:838
  260.1 1.7 copy-start.8
  260.2 26.2 %collective-permute-start.15 = (f32[2,2,40,1920]{3,2,1,0:T(8,128)S(1)}, f32[2,2,40,1920]{3,2,1,0:T(8,128)S(1)}, u32[]{:S(2)}, u32[]{:S(2)}) collective-permute-start(f32[2,2,40,1920]{3,2,1,0:T(8,128)S(1)} %dynamic-slice_bitcast_fusion), channel_id=1, source_target_pairs={{0,16},{1,17},{2,18},{3,19},{4,20},{5,21},{6,22},{7,23},{8,24},{9,... | collective-permute-start | bytes 3686408 | tf_op jit(solution)/shard_map/ppermute | solution.py:845
  262.1 19.7 %collective-permute-start.6 = (f32[2,40,1536]{2,1,0:T(8,128)S(1)}, f32[2,40,1536]{2,1,0:T(8,128)S(1)}, u32[]{:S(2)}, u32[]{:S(2)}) collective-permute-start(f32[2,40,1536]{2,1,0:T(8,128)S(1)} %dynamic-slice_bitcast_fusion.8), channel_id=1, source_target_pairs={{0,1},{1,0},{2,3},{3,2},{4,5},{5,4},{6,7},{7,6},{8,9},{9,8},{10,11... | collective-permute-start | bytes 1474568 | tf_op jit(solution)/shard_map/ppermute | solution.py:838
  271.9 8.5 %collective-permute-start.30 = (f32[40,1408]{1,0:T(8,128)S(1)}, f32[40,1408]{1,0:T(8,128)S(1)}, u32[]{:S(2)}, u32[]{:S(2)}) collective-permute-start(f32[40,1408]{1,0:T(8,128)S(1)} %dynamic-slice_bitcast_fusion.15), channel_id=1, source_target_pairs={{0,8},{1,9},{2,10},{3,11},{4,12},{5,13},{6,14},{7,15},{8,0},{9,1},... | collective-permute-start | bytes 675848 | tf_op jit(solution)/shard_map/ppermute | solution.py:845
  273.2 28.9 %collective-permute-start.10 = (f32[2,2,40,1920]{3,2,1,0:T(8,128)S(1)}, f32[2,2,40,1920]{3,2,1,0:T(8,128)S(1)}, u32[]{:S(2)}, u32[]{:S(2)}) collective-permute-start(f32[2,2,40,1920]{3,2,1,0:T(8,128)S(1)} %dynamic-slice_bitcast_fusion.1), channel_id=1, source_target_pairs={{0,8},{1,9},{2,10},{3,11},{4,12},{5,13},{6,14},{7,15},{8,0},{9,1},... | collective-permute-start | bytes 3686408 | tf_op jit(solution)/shard_map/ppermute | solution.py:845
  286.6 17.9 %collective-permute-start.16 = (f32[2,40,1920]{2,1,0:T(8,128)S(1)}, f32[2,40,1920]{2,1,0:T(8,128)S(1)}, u32[]{:S(2)}, u32[]{:S(2)}) collective-permute-start(f32[2,40,1920]{2,1,0:T(8,128)S(1)} %dynamic-slice_bitcast_fusion.6), channel_id=1, source_target_pairs={{0,1},{1,0},{2,3},{3,2},{4,5},{5,4},{6,7},{7,6},{8,9},{9,8},{10,11... | collective-permute-start | bytes 1843208 | tf_op jit(solution)/shard_map/ppermute | solution.py:838
  302.3 10.2 %collective-permute-start.11 = (f32[2,40,1920]{2,1,0:T(8,128)S(1)}, f32[2,40,1920]{2,1,0:T(8,128)S(1)}, u32[]{:S(2)}, u32[]{:S(2)}) collective-permute-start(f32[2,40,1920]{2,1,0:T(8,128)S(1)} %dynamic-slice_bitcast_fusion.7), channel_id=1, source_target_pairs={{0,1},{1,0},{2,3},{3,2},{4,5},{5,4},{6,7},{7,6},{8,9},{9,8},{10,11... | collective-permute-start | bytes 1843208 | tf_op jit(solution)/shard_map/ppermute | solution.py:838
  302.9 10.4 %collective-permute-start.7 = (f32[40,1536]{1,0:T(8,128)S(1)}, f32[40,1536]{1,0:T(8,128)S(1)}, u32[]{:S(2)}, u32[]{:S(2)}) collective-permute-start(f32[40,1536]{1,0:T(8,128)S(1)} %dynamic-slice_bitcast_fusion.14), channel_id=1, source_target_pairs={{0,8},{1,9},{2,10},{3,11},{4,12},{5,13},{6,14},{7,15},{8,0},{9,1},... | collective-permute-start | bytes 737288 | tf_op jit(solution)/shard_map/ppermute | solution.py:845
  304.5 10.2 %collective-permute-start.17 = (f32[2,40,1920]{2,1,0:T(8,128)S(1)}, f32[2,40,1920]{2,1,0:T(8,128)S(1)}, u32[]{:S(2)}, u32[]{:S(2)}) collective-permute-start(f32[2,40,1920]{2,1,0:T(8,128)S(1)} %bitcast_add_fusion.6), channel_id=1, source_target_pairs={{0,0},{1,2},{2,1},{3,3},{4,4},{5,6},{6,5},{7,7},{8,8},{9,10},{10,9... | collective-permute-start | bytes 1843208 | tf_op jit(solution)/shard_map/ppermute | solution.py:842
  312.6 11.9 %collective-permute-start.12 = (f32[2,40,1920]{2,1,0:T(8,128)S(1)}, f32[2,40,1920]{2,1,0:T(8,128)S(1)}, u32[]{:S(2)}, u32[]{:S(2)}) collective-permute-start(f32[2,40,1920]{2,1,0:T(8,128)S(1)} %bitcast_add_fusion.7), channel_id=1, source_target_pairs={{0,0},{1,2},{2,1},{3,3},{4,4},{5,6},{6,5},{7,7},{8,8},{9,10},{10,9... | collective-permute-start | bytes 1843208 | tf_op jit(solution)/shard_map/ppermute | solution.py:842
  314.8 16.6 %collective-permute-start.18 = (f32[40,1920]{1,0:T(8,128)S(1)}, f32[40,1920]{1,0:T(8,128)S(1)}, u32[]{:S(2)}, u32[]{:S(2)}) collective-permute-start(f32[40,1920]{1,0:T(8,128)S(1)} %dynamic-slice_bitcast_fusion.12), channel_id=1, source_target_pairs={{0,1},{1,0},{2,3},{3,2},{4,5},{5,4},{6,7},{7,6},{8,9},{9,8},{10,11... | collective-permute-start | bytes 921608 | tf_op jit(solution)/shard_map/ppermute | solution.py:838
  324.5 11.3 %collective-permute-start.13 = (f32[40,1920]{1,0:T(8,128)S(1)}, f32[40,1920]{1,0:T(8,128)S(1)}, u32[]{:S(2)}, u32[]{:S(2)}) collective-permute-start(f32[40,1920]{1,0:T(8,128)S(1)} %dynamic-slice_bitcast_fusion.13), channel_id=1, source_target_pairs={{0,1},{1,0},{2,3},{3,2},{4,5},{5,4},{6,7},{7,6},{8,9},{9,8},{10,11... | collective-permute-start | bytes 921608 | tf_op jit(solution)/shard_map/ppermute | solution.py:838

commit v3 on v2

v3 whole, which is shorter than its diff:
```python
import functools
import math

import jax
import jax.numpy as jnp
import numpy as np
from jax import lax
from jax.experimental import pallas as pl
from jax.experimental.pallas import tpu as pltpu
from jax.sharding import PartitionSpec as P

HEADS = 16
BLOCK = 128

epsilon = 1e-06
masked_value = -1000000000.0
AXES = ("wide", "narrow")


def rotary_tables(patches, head_dim, count):
    exponent = np.arange(head_dim // 2, dtype=np.float32) * np.float32(2.0 / head_dim)
    frequency = np.float32(10000.0) ** (-exponent)
    angles = frequency[:, None] * np.arange(patches, dtype=np.float32)[None, :]
    angles = np.tile(np.concatenate([angles, angles], axis=0), (1, count))
    return jnp.asarray(np.cos(angles)), jnp.asarray(np.sin(angles))


TILE_BYTES = 409600
ORDERS = {"A": "azb", "B": "azb", "C": "azb", "D1": "azb", "D2": "abz", "D3": "abz", "E": "abz"}
PROGRAM = (
    "A", "B", "K", "A", "C", "D3", "B", "E", "A", "C", "B", "D3", "A", "C", "E", "B", "A", "D3", "B", "A", "D1", "C", "E", "B", "D2", "D3", "C", "D1", "E", "D3", "D2", "C", "E", "D1", "D3", "D2", "E", "D2", "D1", "D2", "D1", "D2", "D1",
)


def dot_plain(left_side, right_side):
    return jnp.dot(left_side, right_side, preferred_element_type=jnp.float32)


def dot_over(left_side, right_side, left_axis, right_axis):
    return lax.dot_general(
        left_side,
        right_side,
        (((left_axis,), (right_axis,)), ((), ())),
        preferred_element_type=jnp.float32,
    )


def dot_exact(left_side, right_side):
    return jnp.dot(
        left_side, right_side, preferred_element_type=jnp.float32, precision=lax.Precision.HIGHEST
    )


def logistic(values):
    return 1.0 / (1.0 + jnp.exp(-values))


def quotient(values, by):
    return lax.shift_right_logical(values, jnp.int32(by.bit_length() - 1))


def remainder(values, by):
    return values & (by - 1)


def iota(shape, axis):
    return lax.broadcasted_iota(jnp.int32, shape, axis)


def series_statistics(lengths_ref, series_ref, flags_ref, patch_len):
    count, points = series_ref.shape
    patches = points // patch_len
    values = series_ref[...]
    kept = 1.0 - flags_ref[...].astype(jnp.float32)
    starts = jnp.zeros((count, 1), jnp.int32)
    row = iota((count, 1), 0)
    for at in range(count):
        starts = jnp.where(row == at, patches - lengths_ref[at], starts)
    hot = (quotient(iota((count, points), 1), patch_len) == starts).astype(jnp.float32)
    hot_kept = hot * kept
    kept_count = jnp.maximum(jnp.sum(hot_kept, axis=1, keepdims=True), 1.0)
    center = jnp.sum(hot_kept * values, axis=1, keepdims=True) / kept_count
    shifted = values - center
    spread = jnp.sum(hot_kept * shifted * shifted, axis=1, keepdims=True) / kept_count
    sigma = jnp.sqrt(jnp.maximum(spread, 1.0))
    return kept, starts, hot_kept, kept_count, center, shifted, spread, sigma


def belongs(rows, count, patches, kind):
    return (quotient(iota((rows, count), 0), patches) == iota((rows, count), 1)).astype(kind)


def belongs_back(rows, count, patches, kind):
    return (quotient(iota((count, rows), 1), patches) == iota((count, rows), 0)).astype(kind)


def own_patch(rows, points, patches, patch_len):
    return quotient(iota((rows, points), 1), patch_len) == remainder(iota((rows, points), 0), patches)


def turn_half(values):
    half = values.shape[0] // 2
    return jnp.concatenate([-values[half:], values[:half]], axis=0)


def turn_half_back(values):
    half = values.shape[0] // 2
    return jnp.concatenate([values[half:], -values[:half]], axis=0)


def split_rows(place_ref, turned, other_ref, own_ref, first, units):
    core = place_ref[0]
    unit = turned.shape[0] // units
    for at in range(units // 2):
        mine = pl.multiple_of((2 * at + core) * unit, 16)
        theirs = pl.multiple_of((2 * at + 1 - core) * unit, 16)
        own_ref[at * unit : (at + 1) * unit, :] = turned[pl.ds(mine, unit), :].astype(jnp.float32)
        other_ref[first + at * unit : first + (at + 1) * unit, :] = turned[pl.ds(theirs, unit), :].astype(jnp.float32)


def put_tiles(ref, first, values):
    rows, width = values.shape
    for at in range(width // rows):
        ref[first + at * rows : first + (at + 1) * rows, :] = values[:, at * rows : (at + 1) * rows].astype(jnp.float32)


UNITS = 8
TOKEN = jax.ShapeDtypeStruct((8, 128), jnp.float32)


def COST(microseconds):
    return pl.CostEstimate(flops=int(microseconds * 11500000000.0), bytes_accessed=0, transcendentals=0)


OWN = ("branch", "normed_two", "resid", "mixed", "normed_one", "hidden")


def stack_rows(*heights):
    places, at = {}, 0
    for name, height in heights:
        places[name] = at
        at += height
    places["end"] = at
    return places


def later_rows(width, horizon):
    half = width // 2
    return stack_rows(("normed_two", half), ("upper", width), ("resid", half), ("head", horizon))


def rest_rows(width):
    half = width // 2
    return stack_rows(
        ("mixed", half),
        ("middle", width),
        ("normed_one", half),
        ("hidden", half),
    )


def last_rows(width, patch_len, rows):
    half = width // 2
    return stack_rows(
        ("embed_tiles", width),
        ("embed", half),
        ("pre", half),
        ("tokens", 2 * patch_len),
        ("sums", 8 * width // rows),
    )


def front_kernel(
    heads,
    lengths_ref,
    place_ref,
    series_ref,
    flags_ref,
    cotangent_ref,
    gain_first_ref,
    gain_second_ref,
    cosine_ref,
    sine_ref,
    lift_hbm,
    mix_hbm,
    skip_hbm,
    joint_hbm,
    merge_hbm,
    grow_hbm,
    shrink_hbm,
    head_hbm,
    token_ref,
    predictions_ref,
    tokens_out,
    logsum_out,
    sigma_sum_out,
    center_sum_out,
    second_out,
    embedded_hbm,
    middle_hbm,
    turned_hbm,
    own_hbm,
    soon_hbm,
    later_hbm,
    rest_hbm,
    lift_ref,
    mix_ref,
    skip_ref,
    joint_ref,
    merge_ref,
    grow_ref,
    shrink_ref,
    head_ref,
    embedded_ref,
    middle_ref,
    joint_turned,
    turned_ref,
    mixed_turned,
    allowed_ref,
    resid_ref,
    upper_ref,
    back_ref,
    flip_ref,
    own,
    soon,
    later,
    rest,
    load_sem,
    store_sem,
):
    rows, width = embedded_ref.shape
    count, points = series_ref.shape
    patches = rows // count
    patch_len = points // patches
    head_dim = width // heads
    half_rows = width // 2
    wide = cotangent_ref.shape[1]
    token_ref[...] = jnp.zeros_like(token_ref)
    loads = [
        pltpu.make_async_copy(lift_hbm, lift_ref, load_sem.at[0]),
        pltpu.make_async_copy(skip_hbm, skip_ref, load_sem.at[1]),
        pltpu.make_async_copy(mix_hbm, mix_ref, load_sem.at[2]),
    ]
    for at in range(3):
        loads.append(
            pltpu.make_async_copy(joint_hbm.at[:, pl.ds(at * width, width)], joint_ref.at[at], load_sem.at[3 + at])
        )
    for at, (source, target) in enumerate(
        ((merge_hbm, merge_ref), (head_hbm, head_ref), (shrink_hbm, shrink_ref), (grow_hbm, grow_ref))
    ):
        loads.append(pltpu.make_async_copy(source, target, load_sem.at[6 + at]))
    for copy in loads:
        copy.start()
    stores = []

    def store(source, target, first=0, count=None):
        span = pl.ds(first, source.shape[0] - first if count is None else count)
        copy = pltpu.make_async_copy(source.at[span], target.at[span], store_sem.at[len(stores)])
        copy.start()
        stores.append(copy)

    def split(turned, name, pack, at):
        first = OWN.index(name) * half_rows
        split_rows(place_ref, turned, pack, own.at[pl.ds(first, half_rows)], at, UNITS)
        store(own, own_hbm, first, half_rows)

    places = later_rows(width, wide) | rest_rows(width)

    kept, starts, _, _, center, shifted, _, sigma = series_statistics(lengths_ref, series_ref, flags_ref, patch_len)
    scaled = (shifted / sigma * kept).astype(jnp.bfloat16)
    flag_values = flags_ref[...].astype(jnp.float32).astype(jnp.bfloat16)
    spread_out = belongs(rows, count, patches, jnp.bfloat16)
    inside = own_patch(rows, points, patches, patch_len)
    lane = iota((points, 2 * patch_len), 1)
    point = remainder(iota((points, 2 * patch_len), 0), patch_len)
    fold_left = (lane == point).astype(jnp.bfloat16)
    fold_right = (lane == point + patch_len).astype(jnp.bfloat16)
    left = jnp.where(inside, dot_plain(spread_out, scaled), 0.0).astype(jnp.bfloat16)
    right = jnp.where(inside, dot_plain(spread_out, flag_values), 0.0).astype(jnp.bfloat16)
    tokens = (dot_plain(left, fold_left) + dot_plain(right, fold_right)).astype(jnp.bfloat16)
    tokens_out[...] = tokens
    spread_exact = belongs(rows, count, patches, jnp.float32)
    sigma_rows = dot_exact(spread_exact, jnp.broadcast_to(sigma, (count, wide)))
    center_rows = dot_exact(spread_exact, jnp.broadcast_to(center, (count, wide)))
    starts_rows = dot_exact(spread_exact, jnp.broadcast_to(starts.astype(jnp.float32), (count, wide)))
    patch_row = remainder(iota((rows, wide), 0), patches).astype(jnp.float32)
    valid = (patch_row >= starts_rows - 0.5).astype(jnp.float32)
    block = allowed_ref.shape[1]
    key_at = remainder(iota((rows, block), 0), block)
    query_at = iota((rows, block), 1)
    key_pos, query_pos = remainder(key_at, patches), remainder(query_at, patches)
    allowed_ref[...] = (
        (quotient(key_at, patches) == quotient(query_at, patches))
        & (key_pos <= query_pos)
        & ((key_pos.astype(jnp.float32) >= starts_rows[:, :1] - 0.5) | (key_pos == query_pos))
    ).astype(jnp.float32)

    loads[0].wait()
    hidden_pre = dot_plain(tokens, lift_ref[...])
    hidden_act = (hidden_pre * logistic(hidden_pre)).astype(jnp.bfloat16)
    flip_ref[...] = hidden_act.T
    split(flip_ref, "hidden", rest, places["hidden"])
    store(rest, rest_hbm, places["hidden"], half_rows)
    loads[1].wait()
    loads[2].wait()
    embedded = dot_plain(hidden_act, mix_ref[...]) + dot_plain(tokens, skip_ref[...])
    embedded_ref[...] = embedded
    store(embedded_ref, embedded_hbm)
    scale_one = lax.rsqrt(jnp.mean(embedded * embedded, axis=1, keepdims=True) + epsilon)
    normed_one = (embedded * scale_one * gain_first_ref[...][None, :]).astype(jnp.bfloat16)
    for at in range(3):
        loads[3 + at].wait()
        tile = rows
        for part in range(width // tile):
            result = dot_plain(normed_one, joint_ref[at, :, part * tile : (part + 1) * tile])
            joint_turned[at * width + part * tile : at * width + (part + 1) * tile, :] = result.T
    flip_ref[...] = normed_one.T
    split(flip_ref, "normed_one", rest, places["normed_one"])
    store(rest, rest_hbm, places["normed_one"], half_rows)

    scale = head_dim ** (-0.5)
    cosine, sine = cosine_ref[...], sine_ref[...]

    def one_head(head, _):
        begin = pl.multiple_of(head * head_dim, 16)
        query = joint_turned[pl.ds(begin, head_dim), :]
        key = joint_turned[pl.ds(width + begin, head_dim), :]
        value = joint_turned[pl.ds(2 * width + begin, head_dim), :].astype(jnp.bfloat16)
        query = (query * cosine + turn_half(query) * sine).astype(jnp.bfloat16)
        key = (key * cosine + turn_half(key) * sine).astype(jnp.bfloat16)
        turned_ref[pl.ds(begin, head_dim), :] = query
        turned_ref[pl.ds(width + begin, head_dim), :] = key
        turned_ref[pl.ds(2 * width + begin, head_dim), :] = value
        mixed, sums = [], []
        for at in range(rows // block):
            span = slice(at * block, (at + 1) * block)
            scores = dot_over(key[:, span], query[:, span], 0, 0) * scale
            scores = jnp.where(allowed_ref[span, :] > 0.5, scores, masked_value)
            top = jnp.max(scores, axis=0, keepdims=True)
            raised = jnp.exp(scores - top)
            total = jnp.sum(raised, axis=0, keepdims=True)
            sums.append(top + jnp.log(total))
            probs = (raised / total).astype(jnp.bfloat16)
            mixed.append(dot_plain(value[:, span], probs))
        logsum_out[pl.ds(head, 1), :] = jnp.concatenate(sums, axis=1)
        mixed_turned[pl.ds(begin, head_dim), :] = jnp.concatenate(mixed, axis=1).astype(jnp.bfloat16)
        return 0

    lax.fori_loop(0, heads, one_head, 0, unroll=2)
    store(turned_ref, turned_hbm)
    split(mixed_turned, "mixed", rest, places["mixed"])
    store(rest, rest_hbm, places["mixed"], half_rows)
    mixed = mixed_turned[...].T
    loads[6].wait()
    resid_one = embedded_ref[...] + dot_plain(mixed, merge_ref[...])
    resid_ref[...] = resid_one
    scale_two = lax.rsqrt(jnp.mean(resid_one * resid_one, axis=1, keepdims=True) + epsilon)
    normed_two = (resid_one * scale_two * gain_second_ref[...][None, :]).astype(jnp.bfloat16)
    flip_ref[...] = normed_two.T
    split(flip_ref, "normed_two", later, places["normed_two"])
    store(later, later_hbm, places["normed_two"], half_rows)

    outer = cotangent_ref[...] * valid
    head_back = (outer * sigma_rows).astype(jnp.bfloat16)
    loads[7].wait()
    resid_back = dot_over(head_back, head_ref[...], 1, 1)
    back_ref[...] = resid_back
    branch_back = resid_back.astype(jnp.bfloat16)
    flip_ref[...] = branch_back.T
    split(flip_ref, "branch", soon, 0)

    loads[9].wait()
    upper_pre = dot_plain(normed_two, grow_ref[...])
    upper_ref[...] = upper_pre
    active = (upper_pre * logistic(upper_pre)).astype(jnp.bfloat16)
    put_tiles(soon, half_rows, active)
    store(soon, soon_hbm)
    loads[8].wait()
    upper_pre = upper_ref[...]
    gate = logistic(upper_pre)
    slope = gate * (1.0 + upper_pre * (1.0 - gate))
    upper_back = (dot_over(branch_back, shrink_ref[...], 1, 1) * slope).astype(jnp.bfloat16)
    put_tiles(later, places["upper"], upper_back)
    store(later, later_hbm, places["upper"], width)
    resid_low = (resid_ref[...] + dot_plain(active, shrink_ref[...])).astype(jnp.bfloat16)
    flip_ref[...] = resid_low.T
    split(flip_ref, "resid", later, places["resid"])
    store(later, later_hbm, places["resid"], half_rows)
    later[places["head"] : places["head"] + wide, :] = head_back.astype(jnp.float32).T
    store(later, later_hbm, places["head"], wide)

    normed_back = dot_over(upper_back, grow_ref[...], 1, 1)
    resid_one = resid_ref[...]
    second_out[...] = jnp.sum(normed_back * resid_one * scale_two, axis=0, keepdims=True)
    through = normed_back * gain_second_ref[...][None, :]
    inner = jnp.mean(through * resid_one, axis=1, keepdims=True)
    middle = back_ref[...] + scale_two * through - resid_one * (scale_two * scale_two * scale_two * inner)
    middle_ref[...] = middle
    store(middle_ref, middle_hbm)
    put_tiles(rest, places["middle"], middle.astype(jnp.bfloat16))
    store(rest, rest_hbm, places["middle"], width)

    head_out = dot_plain(resid_low, head_ref[...])
    predictions_ref[...] = valid * (head_out * sigma_rows + center_rows)
    gather = belongs_back(rows, count, patches, jnp.float32)
    sigma_sum_out[...] = dot_exact(gather, outer * head_out)
    center_sum_out[...] = dot_exact(gather, outer)
    for copy in stores:
        copy.wait()


def front(place, lengths, series, flags, cotangent, tables, weights, heads):
    lift, mix, skip, gain_first, joint, merge, gain_second, grow, shrink, head = weights
    rows, horizon = cotangent.shape
    width = mix.shape[0]
    half = width // 2
    count = series.shape[0]
    f32, bf16 = jnp.float32, jnp.bfloat16
    vmem = pl.BlockSpec(memory_space=pltpu.VMEM)
    smem = pl.BlockSpec(memory_space=pltpu.SMEM)
    hbm = pl.BlockSpec(memory_space=pl.ANY)
    shape = jax.ShapeDtypeStruct
    packs = [
        (len(OWN) * half, rows),
        (half + width, rows),
        (later_rows(width, horizon)["end"], rows),
        (rest_rows(width)["end"], rows),
    ]
    outs = [
        TOKEN,
        shape((rows, horizon), f32),
        shape((rows, lift.shape[0]), bf16),
        shape((heads, rows), f32),
        shape((count, horizon), f32),
        shape((count, horizon), f32),
        shape((1, width), f32),
        shape((rows, width), f32),
        shape((rows, width), f32),
        shape((3 * width, rows), bf16),
    ] + [shape(pack, f32) for pack in packs]
    scratch = [
        pltpu.VMEM(lift.shape, bf16),
        pltpu.VMEM(mix.shape, bf16),
        pltpu.VMEM(skip.shape, bf16),
        pltpu.VMEM((3, width, width), bf16),
        pltpu.VMEM(merge.shape, bf16),
        pltpu.VMEM(grow.shape, bf16),
        pltpu.VMEM(shrink.shape, bf16),
        pltpu.VMEM(head.shape, bf16),
        pltpu.VMEM((rows, width), f32),
        pltpu.VMEM((rows, width), f32),
        pltpu.VMEM((3 * width, rows), f32),
        pltpu.VMEM((3 * width, rows), bf16),
        pltpu.VMEM((width, rows), bf16),
        pltpu.VMEM((rows, BLOCK), f32),
        pltpu.VMEM((rows, width), f32),
        pltpu.VMEM((rows, width), f32),
        pltpu.VMEM((rows, width), f32),
        pltpu.VMEM((width, rows), bf16),
    ] + [pltpu.VMEM(pack, f32) for pack in packs]
    scratch += [pltpu.SemaphoreType.DMA((10,)), pltpu.SemaphoreType.DMA((18,))]
    return pl.pallas_call(
        functools.partial(front_kernel, heads),
        out_shape=outs,
        in_specs=[smem, smem] + [vmem] * 7 + [hbm] * 8,
        out_specs=[vmem] * 7 + [hbm] * 7,
        scratch_shapes=scratch,
        compiler_params=pltpu.CompilerParams(vmem_limit_bytes=62 * 1024 * 1024),
        cost_estimate=COST(22.0),
    )(
        lengths,
        place,
        series,
        flags,
        cotangent,
        gain_first,
        gain_second,
        *tables,
        lift,
        mix,
        skip,
        joint,
        merge,
        grow,
        shrink,
        head,
    )


def back_kernel(
    heads,
    lengths_ref,
    place_ref,
    series_ref,
    flags_ref,
    gain_first_ref,
    cosine_ref,
    sine_ref,
    tokens_ref,
    logsum_ref,
    sigma_sum_ref,
    center_sum_ref,
    second_ref,
    middle_ref,
    turned_ref,
    embedded_hbm,
    lift_hbm,
    mix_hbm,
    skip_hbm,
    joint_hbm,
    merge_hbm,
    token_in,
    token_ref,
    series_grad_ref,
    joint_hbm_out,
    last_hbm,
    own_hbm,
    lift_ref,
    mix_ref,
    skip_ref,
    joint_ref,
    merge_ref,
    embedded_ref,
    mixed_turned,
    joint_turned,
    first_ref,
    allowed_ref,
    flip_ref,
    joint_pack,
    last,
    own,
    load_sem,
    store_sem,
):
    rows, width = embedded_ref.shape
    count, points = series_ref.shape
    patches = rows // count
    patch_len = points // patches
    head_dim = width // heads
    half_rows = width // 2
    del token_in
    token_ref[...] = jnp.zeros_like(token_ref)
    loads = [
        pltpu.make_async_copy(source, target, load_sem.at[at])
        for at, (source, target) in enumerate(
            (
                (merge_hbm, merge_ref),
                (joint_hbm, joint_ref),
                (embedded_hbm, embedded_ref),
                (mix_hbm, mix_ref),
                (lift_hbm, lift_ref),
                (skip_hbm, skip_ref),
            )
        )
    ]
    for copy in loads:
        copy.start()
    stores = []

    def store(source, target, first=0, count=None):
        span = pl.ds(first, source.shape[0] - first if count is None else count)
        copy = pltpu.make_async_copy(source.at[span], target.at[span], store_sem.at[len(stores)])
        copy.start()
        stores.append(copy)

    places = last_rows(width, patch_len, rows)

    kept, starts, hot_kept, kept_count, center, shifted, spread, sigma = series_statistics(
        lengths_ref, series_ref, flags_ref, patch_len
    )
    block = allowed_ref.shape[1]
    spread_exact = belongs(rows, count, patches, jnp.float32)
    starts_rows = dot_exact(spread_exact, jnp.broadcast_to(starts.astype(jnp.float32), (count, block)))
    key_at = remainder(iota((rows, block), 0), block)
    query_at = iota((rows, block), 1)
    key_pos, query_pos = remainder(key_at, patches), remainder(query_at, patches)
    allowed_ref[...] = (
        (quotient(key_at, patches) == quotient(query_at, patches))
        & (key_pos <= query_pos)
        & ((key_pos.astype(jnp.float32) >= starts_rows - 0.5) | (key_pos == query_pos))
    ).astype(jnp.float32)
    scale = head_dim ** (-0.5)
    cosine, sine = cosine_ref[...], sine_ref[...]
    loads[0].wait()
    mixed_turned[...] = dot_over(merge_ref[...], middle_ref[...].astype(jnp.bfloat16), 1, 1).astype(jnp.bfloat16)

    def unrotate(gradient):
        return gradient * cosine + turn_half_back(gradient * sine)

    def one_head(head, _):
        begin = pl.multiple_of(head * head_dim, 16)
        query = turned_ref[pl.ds(begin, head_dim), :]
        key = turned_ref[pl.ds(width + begin, head_dim), :]
        value = turned_ref[pl.ds(2 * width + begin, head_dim), :]
        upstream = mixed_turned[pl.ds(begin, head_dim), :]
        logsum = logsum_ref[pl.ds(head, 1), :]
        query_parts, key_parts, value_parts = [], [], []
        for at in range(rows // block):
            span = slice(at * block, (at + 1) * block)
            query_in, key_in, value_in, up = query[:, span], key[:, span], value[:, span], upstream[:, span]
            scores = dot_over(key_in, query_in, 0, 0) * scale
            scores = jnp.where(allowed_ref[span, :] > 0.5, scores, masked_value)
            probs = jnp.exp(scores - logsum[:, span])
            value_parts.append(dot_over(up, probs.astype(jnp.bfloat16), 1, 1))
            probs_back = dot_over(value_in, up, 0, 0)
            inner = jnp.sum(probs * probs_back, axis=0, keepdims=True)
            scores_back = (probs * (probs_back - inner) * scale).astype(jnp.bfloat16)
            query_parts.append(dot_plain(key_in, scores_back))
            key_parts.append(dot_over(query_in, scores_back, 1, 1))
        for at, parts in enumerate((query_parts, key_parts, value_parts)):
            result = jnp.concatenate(parts, axis=1)
            if at < 2:
                result = unrotate(result)
            result = result.astype(jnp.bfloat16)
            joint_turned[pl.ds(at * width + begin, head_dim), :] = result
            joint_pack[pl.ds(at * width + begin, head_dim), :] = result.astype(jnp.float32)
        return 0

    lax.fori_loop(0, heads, one_head, 0, unroll=2)
    store(joint_pack, joint_hbm_out)
    loads[1].wait()
    tile = rows
    for part in range(width // tile):
        span = slice(part * tile, (part + 1) * tile)
        first_ref[:, span] = dot_plain(joint_ref[span, :], joint_turned[...]).T
    loads[2].wait()
    embedded = embedded_ref[...]
    first_back = first_ref[...]
    scale_one = lax.rsqrt(jnp.mean(embedded * embedded, axis=1, keepdims=True) + epsilon)
    first_sum = jnp.sum(first_back * embedded * scale_one, axis=0, keepdims=True)
    through = first_back * gain_first_ref[...][None, :]
    inner = jnp.mean(through * embedded, axis=1, keepdims=True)
    embed_low = (
        middle_ref[...] + scale_one * through - embedded * (scale_one * scale_one * scale_one * inner)
    ).astype(jnp.bfloat16)
    put_tiles(last, places["embed_tiles"], embed_low)
    flip_ref[...] = embed_low.T
    split_rows(place_ref, flip_ref, last, own.at[pl.ds(0, half_rows)], places["embed"], UNITS)
    store(last, last_hbm, places["embed_tiles"], width + half_rows)
    tokens = tokens_ref[...]
    loads[4].wait()
    hidden_pre = dot_plain(tokens, lift_ref[...])
    gate = logistic(hidden_pre)
    slope = gate * (1.0 + hidden_pre * (1.0 - gate))
    loads[3].wait()
    pre_back = (dot_over(embed_low, mix_ref[...], 1, 1) * slope).astype(jnp.bfloat16)
    flip_ref[...] = pre_back.T
    split_rows(place_ref, flip_ref, last, own.at[pl.ds(half_rows, half_rows)], places["pre"], UNITS)
    store(own, own_hbm)
    last[places["tokens"] : places["sums"], :] = tokens.astype(jnp.float32).T
    row = iota((8, width), 0)
    sums = jnp.where(row == 0, second_ref[...], jnp.where(row == 1, first_sum, 0.0))
    for at in range(width // rows):
        first = places["sums"] + 8 * at
        last[first : first + 8, :] = sums[:, at * rows : (at + 1) * rows]
    store(last, last_hbm, places["pre"])

    loads[5].wait()
    token_back = dot_over(pre_back, lift_ref[...], 1, 1) + dot_over(embed_low, skip_ref[...], 1, 1)
    lane = remainder(iota((2 * patch_len, points), 1), patch_len)
    unfold = (lane == iota((2 * patch_len, points), 0)).astype(jnp.float32)
    inside = own_patch(rows, points, patches, patch_len)
    spread_back_rows = jnp.where(inside, dot_exact(token_back, unfold), 0.0)
    scaled_back = dot_exact(belongs_back(rows, count, patches, jnp.float32), spread_back_rows)
    kept_back = scaled_back * kept
    point_back = kept_back / sigma
    sigma_back = jnp.sum(sigma_sum_ref[...], axis=1, keepdims=True)
    center_back = jnp.sum(center_sum_ref[...], axis=1, keepdims=True)
    center_total = center_back - jnp.sum(point_back, axis=1, keepdims=True)
    sigma_total = sigma_back - jnp.sum(kept_back * shifted, axis=1, keepdims=True) / (sigma * sigma)
    spread_grad = jnp.where(spread > 1.0, sigma_total * 0.5 / sigma, 0.0)
    offset_sum = jnp.sum(hot_kept * 2.0 * shifted, axis=1, keepdims=True)
    center_all = center_total - spread_grad * offset_sum / kept_count
    series_grad_ref[...] = point_back + hot_kept * (center_all + 2.0 * shifted * spread_grad) / kept_count
    for copy in stores:
        copy.wait()


def back(token, place, lengths, series, flags, tables, weights, kept_values, heads):
    lift, mix, skip, gain_first, joint, merge = weights
    tokens, logsum, sigma_sum, center_sum, second_sum, embedded, middle, turned = kept_values
    rows, width = embedded.shape
    half = width // 2
    f32, bf16 = jnp.float32, jnp.bfloat16
    vmem = pl.BlockSpec(memory_space=pltpu.VMEM)
    smem = pl.BlockSpec(memory_space=pltpu.SMEM)
    hbm = pl.BlockSpec(memory_space=pl.ANY)
    shape = jax.ShapeDtypeStruct
    packs = [(3 * width, rows), (last_rows(width, lift.shape[0] // 2, rows)["end"], rows), (2 * half, rows)]
    scratch = [
        pltpu.VMEM(lift.shape, bf16),
        pltpu.VMEM(mix.shape, bf16),
        pltpu.VMEM(skip.shape, bf16),
        pltpu.VMEM(joint.shape, bf16),
        pltpu.VMEM(merge.shape, bf16),
        pltpu.VMEM((rows, width), f32),
        pltpu.VMEM((width, rows), bf16),
        pltpu.VMEM((3 * width, rows), bf16),
        pltpu.VMEM((rows, width), f32),
        pltpu.VMEM((rows, BLOCK), f32),
        pltpu.VMEM((width, rows), bf16),
    ] + [pltpu.VMEM(pack, f32) for pack in packs]
    scratch += [pltpu.SemaphoreType.DMA((6,)), pltpu.SemaphoreType.DMA((4,))]
    return pl.pallas_call(
        functools.partial(back_kernel, heads),
        out_shape=[TOKEN, shape(series.shape, f32)] + [shape(pack, f32) for pack in packs],
        in_specs=[smem, smem] + [vmem] * 12 + [hbm] * 7,
        out_specs=[vmem] * 2 + [hbm] * 3,
        scratch_shapes=scratch,
        compiler_params=pltpu.CompilerParams(vmem_limit_bytes=62 * 1024 * 1024),
        cost_estimate=COST(22.0),
    )(
        lengths,
        place,
        series,
        flags,
        gain_first,
        *tables,
        tokens,
        logsum,
        sigma_sum,
        center_sum,
        second_sum,
        middle,
        turned,
        embedded,
        lift,
        mix,
        skip,
        joint,
        merge,
        token,
    )


def gradient_kernel(place_ref, *refs, terms, arrays, unit, axis, columns):
    sources = refs[:arrays]
    token_ref, send_hbm, keep_hbm = refs[arrays + 1 : arrays + 4]
    result_ref, left_raw, left_ref, right_raw, load_sem, store_sem = refs[arrays + 4 :]
    token_ref[...] = jnp.zeros_like(token_ref)
    if axis == "z":
        height, mine = unit // 2, place_ref[3] & 1
        starts = [group * unit + half * height for half in (1 - mine, mine) for group in range(4)]
    else:
        height, mine, core = unit, place_ref[1], place_ref[0]
        stride, across = 1 + core, 2 - core
        starts = [(stride * side + across * other) * unit for side in (1 - mine, mine) for other in (0, 1)]
    total = 4 * unit
    rows = left_raw.shape[2]
    loads = []

    def load(source, first, target):
        copy = pltpu.make_async_copy(sources[source].at[pl.ds(first, target.shape[0])], target, load_sem.at[len(loads)])
        copy.start()
        loads.append(copy)
        return copy

    lefts, rights = [], []
    for at, (own, own_row, other, other_row, near, far, row, kind, width, _) in enumerate(terms):
        if kind != "sum":
            lefts.append((load(own, own_row, left_raw.at[2 * at]), load(other, other_row, left_raw.at[2 * at + 1])))
        else:
            lefts.append(())
        tiles = []
        place = sum(term[8] for term in terms[:at]) * 2
        for tile in range(0, width, rows):
            size = min(rows, width - tile)
            spots = [right_raw.at[pl.ds(place + 2 * tile + side * size, size)] for side in (0, 1)]
            tiles.append((tile, size, spots, [load(side, row + tile, spot) for side, spot in zip((near, far), spots)]))
        rights.append(tiles)
    stores = []

    def store(begin, width):
        for half, target in enumerate((send_hbm, keep_hbm)):
            copy = pltpu.make_async_copy(
                result_ref.at[pl.ds(half * total // 2, total // 2), pl.ds(begin, width)],
                target.at[:, pl.ds(begin, width)],
                store_sem.at[len(stores)],
            )
            copy.start()
            stores.append(copy)

    for at, (_, _, _, _, _, _, _, kind, _, begin) in enumerate(terms):
        for copy in lefts[at]:
            copy.wait()
        if kind == "sum":
            for _, _, _, copies in rights[at]:
                for copy in copies:
                    copy.wait()
            place = sum(term[8] for term in terms[:at]) * 2
            height_in = terms[at][8]
            both = right_raw[place : place + height_in, :] + right_raw[place + height_in : place + 2 * height_in, :]
            lanes = jnp.concatenate([both[part : part + 8, :] for part in range(0, height_in, 8)], axis=1)
            tall = jnp.concatenate([lanes, jnp.zeros((BLOCK - 8, lanes.shape[1]), jnp.float32)], axis=0).T
            unit_rows = tall.reshape(UNITS // 2, 2, unit, BLOCK)
            mine_rows = jnp.where(place_ref[0] == 0, unit_rows[:, 0], unit_rows[:, 1]).reshape(total, BLOCK)
            left_raw[0, :, :BLOCK] = mine_rows
            for slot, first in enumerate(starts):
                result_ref[slot * height : (slot + 1) * height, begin : begin + BLOCK] = left_raw[
                    0, pl.ds(pl.multiple_of(first, 16), height), :BLOCK
                ]
            store(begin, BLOCK)
            continue
        for slot, first in enumerate(starts):
            first = pl.multiple_of(first, 16)
            span = slice(slot * height, (slot + 1) * height)
            for side in (0, 1):
                left_ref[span, side * rows : (side + 1) * rows] = left_raw[2 * at + side, pl.ds(first, height), :].astype(
                    jnp.bfloat16
                )
        left = left_ref[...]
        for tile, size, spots, copies in rights[at]:
            for copy in copies:
                copy.wait()
            near, far = (spot[...].astype(jnp.bfloat16) for spot in spots)
            if kind == "tiles":
                result = dot_plain(left, jnp.concatenate([near, far], axis=0))
            else:
                right = jnp.concatenate([near, far], axis=1)
                if kind != "turned":
                    blank = jnp.zeros_like(right)
                    right = jnp.concatenate((right, blank) if kind == "low" else (blank, right), axis=0)
                result = dot_over(left, right, 1, 1)
            span = slice(begin + tile, begin + tile + result.shape[1])
            if kind == "high":
                result_ref[:, span] += result
            else:
                result_ref[:, span] = result
            if kind != "low":
                store(begin + tile, result.shape[1])
    for copy in stores:
        copy.wait()


def weight_gradient(token, place, axis, arrays, terms, unit, columns):
    rows = arrays[0].shape[1]
    total = 4 * unit
    hbm = pl.BlockSpec(memory_space=pl.ANY)
    vmem = pl.BlockSpec(memory_space=pltpu.VMEM)
    out_type = jax.ShapeDtypeStruct((total // 2, columns), jnp.float32)
    widths = sum(term[8] for term in terms)
    copies = sum(2 + 2 * (-(-term[8] // rows)) for term in terms)
    return pl.pallas_call(
        functools.partial(
            gradient_kernel, terms=terms, arrays=len(arrays), unit=unit, axis=axis, columns=columns
        ),
        in_specs=[pl.BlockSpec(memory_space=pltpu.SMEM)] + [hbm] * (len(arrays) + 1),
        out_specs=[vmem, hbm, hbm],
        scratch_shapes=[
            pltpu.VMEM((total, columns), jnp.float32),
            pltpu.VMEM((2 * len(terms), total, rows), jnp.float32),
            pltpu.VMEM((total, 2 * rows), jnp.bfloat16),
            pltpu.VMEM((2 * widths, rows), jnp.float32),
            pltpu.SemaphoreType.DMA((copies,)),
            pltpu.SemaphoreType.DMA((copies,)),
        ],
        out_shape=[TOKEN, out_type, out_type],
        compiler_params=pltpu.CompilerParams(vmem_limit_bytes=16 * 1024 * 1024),
        cost_estimate=COST(4.0),
    )(place, *arrays, token)


def part_kernel(place_ref, *refs, inputs, parts):
    token_ref, outputs = refs[inputs + 1], refs[inputs + 2 :]
    step = pl.program_id(0)

    @pl.when(jnp.logical_and(step == 0, pl.program_id(1) == 0))
    def _():
        token_ref[...] = jnp.zeros_like(token_ref)

    for at in range(parts):

        @pl.when(step == at)
        def _(at=at):
            total = refs[0][...]
            for ref in refs[1:inputs]:
                total = total + ref[...]
            outputs[at][...] = total


def add_parts(token, place, arrays, parts, which):
    before, _, after, columns = arrays[0].shape
    tiles = 1
    while after % (2 * tiles) == 0 and (after // (2 * tiles)) % 8 == 0 and before * after * columns * 4 // tiles > TILE_BYTES:
        tiles *= 2
    height = after // tiles

    def index_in(step, tile, place_ref):
        mine = place_ref[which] & (parts - 1)
        chosen = mine ^ ((step + 1) & (parts - 1))
        return (0, chosen, tile, 0)

    def index_out(step, tile, place_ref, at):
        return (0, jnp.where(step == at, tile, jnp.where(step < at, 0, tiles - 1)), 0)

    block_in = pl.BlockSpec((before, None, height, columns), index_in)
    blocks_out = [
        pl.BlockSpec((before, height, columns), functools.partial(index_out, at=at)) for at in range(parts)
    ]
    result = jax.ShapeDtypeStruct((before, after, columns), jnp.float32)
    return pl.pallas_call(
        functools.partial(part_kernel, inputs=len(arrays), parts=parts),
        grid_spec=pltpu.PrefetchScalarGridSpec(
            num_scalar_prefetch=1,
            grid=(parts, tiles),
            in_specs=[block_in] * len(arrays) + [pl.BlockSpec(memory_space=pl.ANY)],
            out_specs=[pl.BlockSpec(TOKEN.shape, lambda i, t, s: (0, 0))] + blocks_out,
        ),
        out_shape=[TOKEN] + [result] * parts,
        compiler_params=pltpu.CompilerParams(vmem_limit_bytes=8 * 1024 * 1024),
        cost_estimate=COST(1.5),
    )(place, *arrays, token)


class Layout:
    def __init__(self, mesh_shape):
        self.wide = mesh_shape["wide"]
        self.narrow = mesh_shape["narrow"]
        self.total = self.wide * self.narrow
        self.paired = self.wide == 8 and self.narrow == 4

    def flip(self, bit):
        return [(i, i ^ bit) for i in range(self.total)]

    def middle(self):
        swapped = (0, 2, 1, 3)
        return [(i, (i & ~3) | swapped[i & 3]) for i in range(self.total)]

    def across(self, first):
        return [(i, i ^ (8 if (i & 4 == 0) == first else 16)) for i in range(self.total)]

    def position(self):
        wide = lax.axis_index("wide")
        core, x, y = wide % 2, wide // 2 % 2, wide // 4 % 2
        places = (core, jnp.where(core == 0, x, y), jnp.where(core == 0, y, x), lax.axis_index("narrow"))
        if not self.paired:
            places = tuple(jnp.zeros_like(place) for place in places)
        return jnp.stack(places).astype(jnp.int32)


class Piece:
    def __init__(self, layout, place, order, arrays, terms, unit, columns):
        self.layout, self.place, self.order = layout, place, order
        self.arrays, self.terms, self.unit, self.columns = arrays, terms, unit, columns
        self.plan = []
        for axis in order:
            self.plan += ["half", "middle", "part"] if axis == "z" else [axis]
        self.axes = ["b", "a", "half", "part"]
        self.held = None
        self.result = None

    def move(self, array, step):
        layout = self.layout
        pairs = layout.across(step == "a") if step in ("a", "b") else layout.flip(1)
        return lax.ppermute(array, AXES, pairs)

    def advance(self, token):
        rows = self.unit // 4
        if self.held is None:
            step = self.plan.pop(0)
            token, send, keep = weight_gradient(
                token, self.place, self.order[0], self.arrays, self.terms, self.unit, self.columns
            )
            self.axes.remove({"a": "a", "z": "half"}.get(step, step))
            self.held = [keep, self.move(send, step)]
            return token
        dims = [2] * len(self.axes)
        if not self.plan:
            shaped = [array.reshape(1, 1, rows, self.columns) for array in self.held]
            token, whole = add_parts(token, self.place, shaped, 1, 0)
            self.result = whole.reshape(rows, self.columns)
            return token
        step = self.plan.pop(0)
        if step == "middle":
            size = math.prod(dims) * rows
            shaped = [array.reshape(1, 1, size, self.columns) for array in self.held]
            token, whole = add_parts(token, self.place, shaped, 1, 0)
            self.held = [lax.ppermute(whole, AXES, self.layout.middle())]
        elif step == "Y":
            at = self.axes.index("half")
            before, after = math.prod(dims[:at]), math.prod(dims[at + 2 :]) * rows
            shaped = [array.reshape(1, 1, before * 4 * after, self.columns) for array in self.held]
            token, whole = add_parts(token, self.place, shaped, 1, 0)
            whole = whole.reshape(before, 4, after, self.columns)
            got = lax.all_to_all(whole, "narrow", 1, 1, tiled=True)
            self.axes = [axis for axis in self.axes if axis not in ("half", "part")]
            self.held = [got[:, at] for at in range(4)]
        else:
            at = self.axes.index(step)
            before, after = math.prod(dims[:at]), math.prod(dims[at + 1 :]) * rows
            shaped = [array.reshape(before, 2, after, self.columns) for array in self.held]
            token, send, keep = add_parts(token, self.place, shaped, 2, {"a": 1, "b": 2}.get(step, 3))
            self.held = [keep, self.move(send, step)]
            self.axes.remove(step)
        return token


def whole_rows(own, other):
    unit = own.shape[0] // (UNITS // 2)
    pair = jnp.stack([own.reshape(-1, unit, own.shape[1]), other.reshape(-1, unit, own.shape[1])], axis=1)
    return pair.reshape(2 * own.shape[0], own.shape[1])


def whole_tiles(tiles, rows):
    return jnp.concatenate([tiles[at : at + rows] for at in range(0, tiles.shape[0], rows)], axis=1)


def per_device(
    layout,
    series,
    flags,
    lengths,
    lift_weight,
    mix_weight,
    skip_weight,
    gain_first,
    joint_weight,
    merge_weight,
    gain_second,
    grow_weight,
    shrink_weight,
    head_weight,
    cotangent,
):
    count = series.shape[0]
    patches, horizon = cotangent.shape[1:]
    width = mix_weight.shape[0]
    hidden = shrink_weight.shape[0]
    rows = count * patches
    half = width // 2
    tables = rotary_tables(patches, width // HEADS, count)
    place = layout.position()
    weights = (
        lift_weight,
        mix_weight,
        skip_weight,
        gain_first,
        joint_weight,
        merge_weight,
        gain_second,
        grow_weight,
        shrink_weight,
        head_weight,
    )
    (
        token,
        predictions,
        tokens,
        logsum,
        sigma_sum,
        center_sum,
        second_sum,
        embedded,
        middle,
        turned,
        own,
        soon,
        later,
        rest,
    ) = front(place, lengths, series, flags, cotangent.reshape(rows, horizon), tables, weights, HEADS)
    across = lift_weight.shape[0]
    joint_width = joint_weight.shape[1]

    def run_back(token):
        return back(
            token,
            place,
            lengths,
            series,
            flags,
            tables,
            (lift_weight, mix_weight, skip_weight, gain_first, joint_weight, merge_weight),
            (tokens, logsum, sigma_sum, center_sum, second_sum, embedded, middle, turned),
            HEADS,
        )

    at_own = {name: place * half for place, name in enumerate(OWN)}
    at_later = later_rows(width, horizon)
    at_rest = rest_rows(width)
    at_last = last_rows(width, across // 2, rows)
    if layout.paired:
        swap = lambda array: lax.ppermute(array, AXES, layout.flip(4))
        unit = width // UNITS
        soon_got, later_got, rest_got = swap(soon), swap(later), swap(rest)
        pieces = {}

        def piece(name, arrays, terms, columns):
            pieces[name] = Piece(layout, place, ORDERS[name], arrays, terms, unit, columns)

        piece("A", [own, soon, soon_got], ((0, at_own["branch"], 2, 0, 1, 2, half, "tiles", hidden, 0),), hidden)
        piece(
            "B",
            [own, later, later_got],
            (
                (0, at_own["normed_two"], 2, at_later["normed_two"], 1, 2, at_later["upper"], "tiles", hidden, 0),
                (0, at_own["resid"], 2, at_later["resid"], 1, 2, at_later["head"], "turned", horizon, hidden),
            ),
            hidden + horizon,
        )
        piece(
            "C",
            [own, rest, rest_got],
            ((0, at_own["mixed"], 2, at_rest["mixed"], 1, 2, at_rest["middle"], "tiles", width, 0),),
            width,
        )
        joint_names = [name for name in ORDERS if name.startswith("D")]
        for name in PROGRAM:
            if name == "K":
                token, series_grad, joint, last, last_own = run_back(token)
                joint_got, last_got = swap(joint), swap(last)
                span = joint_width // len(joint_names)
                for at, joint_name in enumerate(joint_names):
                    piece(
                        joint_name,
                        [own, rest_got, joint, joint_got],
                        ((0, at_own["normed_one"], 1, at_rest["normed_one"], 2, 3, at * span, "turned", span, 0),),
                        span,
                    )
                piece(
                    "E",
                    [own, rest_got, last, last_got, last_own],
                    (
                        (0, at_own["hidden"], 1, at_rest["hidden"], 2, 3, at_last["embed_tiles"], "tiles", width, 0),
                        (4, half, 3, at_last["pre"], 2, 3, at_last["tokens"], "low", across, width),
                        (4, 0, 3, at_last["embed"], 2, 3, at_last["tokens"], "high", across, width),
                        (0, 0, 0, 0, 2, 3, at_last["sums"], "sum", 8 * width // rows, width + 2 * across),
                    ),
                    width + 2 * across + BLOCK,
                )
            else:
                token = pieces[name].advance(token)
        shrink_rows, grow_head, merge_grad, mix_small = (pieces[name].result for name in "ABCE")
        grow_grad, head_grad = grow_head[:, :hidden], grow_head[:, hidden:]
        joint_grad = jnp.concatenate([pieces[name].result for name in joint_names], axis=1)
        mix_grad = mix_small[:, :width]
        lift_rows = mix_small[:, width : width + across]
        skip_rows = mix_small[:, width + across : width + 2 * across]
        second_grad = mix_small[:, width + 2 * across]
        first_grad = mix_small[:, width + 2 * across + 1]
    else:
        _, series_grad, joint, last, last_own = run_back(token)
        scatter = lambda left, right: lax.psum_scatter(
            dot_plain(left.astype(jnp.bfloat16), right.astype(jnp.bfloat16)), AXES, scatter_dimension=0, tiled=True
        )
        mine = lambda name: own[at_own[name] : at_own[name] + half]
        theirs = lambda name: (
            later[at_later[name] : at_later[name] + half]
            if name in at_later
            else rest[at_rest[name] : at_rest[name] + half]
        )
        tiles = lambda pack, first: whole_tiles(pack[first : first + width], rows)
        shrink_rows = scatter(whole_rows(mine("branch"), soon[:half]), tiles(soon, half))
        grow_grad = scatter(whole_rows(mine("normed_two"), theirs("normed_two")), tiles(later, at_later["upper"]))
        head_grad = scatter(
            whole_rows(mine("resid"), theirs("resid")), later[at_later["head"] : at_later["head"] + horizon].T
        )
        merge_grad = scatter(whole_rows(mine("mixed"), theirs("mixed")), tiles(rest, at_rest["middle"]))
        joint_grad = scatter(whole_rows(mine("normed_one"), theirs("normed_one")), joint.T)
        mix_grad = scatter(whole_rows(mine("hidden"), theirs("hidden")), tiles(last, at_last["embed_tiles"]))
        lift_rows = scatter(whole_rows(last_own[half:], last[at_last["pre"] : at_last["pre"] + half]), tokens)
        skip_rows = scatter(whole_rows(last_own[:half], last[at_last["embed"] : at_last["embed"] + half]), tokens)
        sums = whole_tiles(last[at_last["sums"] : at_last["end"]].reshape(-1, rows), 8)
        sums = lax.psum_scatter(sums[:2].T, AXES, scatter_dimension=0, tiled=True)
        second_grad, first_grad = sums[:, 0], sums[:, 1]
    return (
        predictions.reshape(count, patches, horizon),
        series_grad,
        lift_rows.T,
        mix_grad,
        skip_rows.T,
        first_grad,
        joint_grad,
        merge_grad,
        second_grad,
        grow_grad,
        shrink_rows.T,
        head_grad,
    )


def solution(mesh):
    both = P(AXES)
    in_specs = (both, both, both) + (P(),) * 10 + (both,)
    out_specs = (
        P(AXES, None, None),
        P(AXES, None),
        P(None, AXES),
        P(AXES, None),
        P(None, AXES),
        P(AXES),
        P(AXES, None),
        P(AXES, None),
        P(AXES),
        P(AXES, None),
        P(None, AXES),
        P(AXES, None),
    )
    return jax.shard_map(
        functools.partial(per_device, Layout(mesh.shape)),
        mesh=mesh,
        in_specs=in_specs,
        out_specs=out_specs,
        check_vma=False,
    )
```

time: 337 us -> 275 us (0.82); the launches traced: 337 us -> 269 us
  waiting for transfers between devices: 167 us -> 65.3 us
  Pallas kernels: 83.6 us -> 120 us
  starting transfers between devices: 55.8 us -> 68.3 us
  other arithmetic: 13.1 us -> 1.45 us
  local copies, waits for them, and re-layouts: 15.8 us -> 11.9 us
    ppermute x30 -> x35, waiting for transfers between devices: 162 us -> 62 us  [the longest x28 61.9 us: move(): return lax.ppermute(array, AXES, pairs)]
    pallas_call x7 -> x43, Pallas kernels: 60.2 us -> 98 us  [the longest x35 38.5 us: add_parts(): pl.pallas_call(functools.partial(part_kernel, inputs=len(arrays), parts=p...]
    ppermute x30 -> x35, starting transfers between devices: 54.1 us -> 66.7 us  [the longest x28 54.6 us: move(): return lax.ppermute(array, AXES, pairs)]
    add x23 -> x0, other arithmetic: 11.3 us -> none  [the longest x6 6.43 us: sum_over_chips(): keep + lax.ppermute(send, AXES, layout.flip({'x': 8, 'y': 16}[first]))]
    unnamed x26 -> x32, local copies, waits for them, and re-layouts: 7.18 us -> 8.52 us
  transfers between devices with their start and end apart: 37 -> 40, of which waited for: 16 -> 16; matrix products, arithmetic and copies ran while one was open for 5% -> 1% of each run, Pallas kernels for 18% -> 36%
where the time goes in v3:
time: 275 us; the launch traced here: 269 us
  Pallas kernels  120 us (44%)
  starting transfers between devices  68.3 us (25%)
  waiting for transfers between devices  65.3 us (24%)
  local copies, waits for them, and re-layouts  11.9 us (4%)
    ppermute x28, waiting for transfers between devices, move(): return lax.ppermute(array, AXES, pairs)  61.9 us
    ppermute x28, starting transfers between devices, move(): return lax.ppermute(array, AXES, pairs)  54.6 us
    pallas_call x35, Pallas kernels, add_parts(): pl.pallas_call(functools.partial(part_kernel, inputs=len(arrays), parts=p...  38.5 us
    pallas_call x7, Pallas kernels, weight_gradient(): pl.pallas_call(functools.partial(gradient_kernel, terms=terms, arrays=len...  37.2 us
    pallas_call x1, Pallas kernels, front(): pl.pallas_call(functools.partial(front_kernel, heads), out_shape=outs, in...  22.5 us
    pallas_call x1, Pallas kernels, back(): pl.pallas_call(functools.partial(back_kernel, heads), out_shape=[TOKEN, s...  22.3 us
    ppermute x7, starting transfers between devices, advance(): self.held = [lax.ppermute(whole, AXES, self.layout.middle())]  12.1 us
    unnamed x32, local copies, waits for them, and re-layouts  8.52 us
  transfers between devices with their start and end apart: 40, of which 16 were waited for; matrix products, arithmetic and copies ran while one was open for 1% of the time, Pallas kernels for 36%

profile of v3, /device:TPU:0, one launch (start us, length us, event | category | flops | bytes accessed | tf_op | source)
XLA Modules:
  0.0 269.1 jit_solution(9785433175583981057)
XLA Ops:
  1.3 22.5 %shard_map.247 = (f32[8,128]{1,0:T(8,128)}, f32[256,128]{1,0:T(8,128)}, bf16[256,64]{1,0:T(8,128)(2,1)}, f32[16,256]{1,0:T(8,128)}, f32[16,128]{1,0:T(8,128)}, /...) custom-call(s32[16]{0:T(128)} %lengths_ref.3, ...), custom_call_target="tpu_custom_call" | custom-call | flops 253000007680 | tf_op jit(solution)/shard_map/pallas_call | solution.py:462
  24.8 3.3 %collective-permute-done.1.refs_2_ = f32[1920,256]{1,0:T(8,128)S(1)} collective-permute-done((f32[1920,256]{1,0:T(8,128)}, f32[1920,256]{1,0:T(8,128)S(1)}, u32[]{:S(2)}, u32[]{:S(2)}) %collective-permute-start.1) | collective-permute-done | bytes 1966112 | tf_op jit(solution)/shard_map/ppermute | solution.py:1082
  28.1 1.5 copy-done.7
  29.7 2.1 copy-done.10
  32.5 4.7 %shard_map.248 = (f32[8,128]{1,0:T(8,128)S(1)}, f32[320,1280]{1,0:T(8,128)}, f32[320,1280]{1,0:T(8,128)S(1)}) custom-call(s32[4]{0:T(128)S(1)} %copy-done, f32[3840,256]{1,0:T(8,128)S(1)} %copy-done.10, f32[1920,256]{1,0:T(8,128)S(1)} %copy-done.7, f32[1920,256]{1,0:T(8,128)S(1)} %collective-permute-done.1.refs_2_, f32[8,128]{1,0:T(8,128)S(1)} %copy-done.15), custom_call_target="tpu_custom_call" | custom-call | flops 46000001024 | tf_op jit(solution)/shard_map/pallas_call | solution.py:843
  37.1 2.9 %collective-permute-start.6 = (f32[320,1280]{1,0:T(8,128)}, f32[320,1280]{1,0:T(8,128)}, u32[]{:S(2)}, u32[]{:S(2)}) collective-permute-start(f32[320,1280]{1,0:T(8,128)} %get-tuple-element.165), channel_id=1, source_target_pairs={{0,8},{1,9},{2,10},{3,11},{4,20},{5,21},{6,22},{7,23},{8,0},{9,1},... | collective-permute-start | bytes 4915208 | tf_op jit(solution)/shard_map/ppermute | solution.py:955
  40.1 6.1 %shard_map.249 = (f32[8,128]{1,0:T(8,128)S(1)}, f32[320,1408]{1,0:T(8,128)}, f32[320,1408]{1,0:T(8,128)S(1)}) custom-call(s32[4]{0:T(128)S(1)} %copy-done, f32[3840,256]{1,0:T(8,128)S(1)} %copy-done.10, f32[2688,256]{1,0:T(8,128)S(1)} %copy-done.5, f32[2688,256]{1,0:T(8,128)S(1)} %collective-permute-done.refs_2_, f32[8,128]{1,0:T(8,128)S(1)} %get-tuple-element.155.refs_3_), custom_call_target="tpu_custom_call" | custom-call | flops 46000001024 | tf_op jit(solution)/shard_map/pallas_call | solution.py:843
  46.8 22.3 %shard_map.250 = (f32[8,128]{1,0:T(8,128)}, f32[16,512]{1,0:T(8,128)}, f32[3840,256]{1,0:T(8,128)}, f32[2664,256]{1,0:T(8,128)}, f32[1280,256]{1,0:T(8,128)}) custom-call(s32[16]{0:T(128)} %lengths_ref.3, s32[4]{0:T(128)} %pad_add_fusion.place_ref, f32[16,512]{1,0:T(8,128)} %series_ref.3, s32[16,512]{1,0:T(8,128)} %flags_ref.3, f32[1280]{0:T(1024)} %gain_first_ref.3, ...), custom_call_target="tpu_custom_call" | custom-call | flops 253000007680 | tf_op jit(solution)/shard_map/pallas_call | solution.py:704
  69.7 1.4 copy-done.9
  71.8 4.6 %shard_map.251 = (f32[8,128]{1,0:T(8,128)S(1)}, f32[2,80,1280]{2,1,0:T(8,128)}, f32[2,80,1280]{2,1,0:T(8,128)S(1)}) custom-call(s32[4]{0:T(128)S(1)} %copy-done.1, f32[2,2,80,1280]{3,2,1,0:T(8,128)S(1)} %bitcast.126, f32[2,2,80,1280]{3,2,1,0:T(8,128)} %bitcast.9.refs_1_, f32[8,128]{1,0:T(8,128)S(1)} %copy-done.13), custom_call_target="tpu_custom_call" | custom-call | flops 17250000896 | tf_op jit(solution)/shard_map/pallas_call | solution.py:901
  76.4 1.6 collective-permute-start.9
  78.0 5.0 %shard_map.252 = (f32[8,128]{1,0:T(8,128)S(1)}, f32[320,1280]{1,0:T(8,128)S(1)}, f32[320,1280]{1,0:T(8,128)S(1)}) custom-call(s32[4]{0:T(128)S(1)} %copy-done.1, f32[3840,256]{1,0:T(8,128)S(1)} %copy-done.11, f32[3200,256]{1,0:T(8,128)S(1)} %copy-done.4, f32[3200,256]{1,0:T(8,128)} %collective-permute-done.2.refs_2_.refs_1_, ...), custom_call_target="tpu_custom_call" | custom-call | flops 46000001024 | tf_op jit(solution)/shard_map/pallas_call | solution.py:843
  83.1 1.5 collective-permute-start.8
  84.6 4.8 %shard_map.253 = (f32[8,128]{1,0:T(8,128)S(1)}, f32[320,1280]{1,0:T(8,128)S(1)}, f32[320,1280]{1,0:T(8,128)S(1)}) custom-call(s32[4]{0:T(128)S(1)} %copy-done.1, f32[3840,256]{1,0:T(8,128)S(1)} %copy-done.11, f32[3200,256]{1,0:T(8,128)} %collective-permute-done.2.refs_2_.refs_1_, f32[3840,256]{1,0:T(8,128)S(1)} %copy-done.2, ...), custom_call_target="tpu_custom_call" | custom-call | flops 46000001024 | tf_op jit(solution)/shard_map/pallas_call | solution.py:843
  89.5 3.5 %shard_map.254 = (f32[8,128]{1,0:T(8,128)S(1)}, f32[2,80,1408]{2,1,0:T(8,128)S(1)}, f32[2,80,1408]{2,1,0:T(8,128)S(1)}) custom-call(s32[4]{0:T(128)S(1)} %copy-done.1, f32[2,2,80,1408]{3,2,1,0:T(8,128)S(1)} %bitcast.121, f32[2,2,80,1408]{3,2,1,0:T(8,128)} %bitcast.7.refs_1_, f32[8,128]{1,0:T(8,128)S(1)} %get-tuple-element.169.refs_2_), custom_call_target="tpu_custom_call" | custom-call | flops 17250000896 | tf_op jit(solution)/shard_map/pallas_call | solution.py:901
  94.0 6.9 %shard_map.255 = (f32[8,128]{1,0:T(8,128)S(1)}, f32[320,1536]{1,0:T(8,128)S(1)}, f32[320,1536]{1,0:T(8,128)S(1)}) custom-call(s32[4]{0:T(128)S(1)} %copy-done.1, f32[3840,256]{1,0:T(8,128)S(1)} %copy-done.11, f32[3200,256]{1,0:T(8,128)} %collective-permute-done.2.refs_2_.refs_1_, f32[2664,256]{1,0:T(8,128)S(1)} %copy-done.6, ...), custom_call_target="tpu_custom_call" | custom-call | flops 46000001024 | tf_op jit(solution)/shard_map/pallas_call | solution.py:843
  100.9 1.8 shard_map.256
  102.7 1.5 collective-permute-done.8
  104.2 1.4 shard_map.257
  106.8 1.6 collective-permute-start.7
  108.4 8.6 %collective-permute-done.13 = f32[2,80,1408]{2,1,0:T(8,128)S(1)} collective-permute-done((f32[2,80,1408]{2,1,0:T(8,128)S(1)}, f32[2,80,1408]{2,1,0:T(8,128)S(1)}, u32[]{:S(2)}, u32[]{:S(2)}) %collective-permute-start.13) | collective-permute-done | bytes 901152 | tf_op jit(solution)/shard_map/ppermute | solution.py:955
  118.4 3.4 %collective-permute-done.12 = f32[320,1280]{1,0:T(8,128)S(1)} collective-permute-done((f32[320,1280]{1,0:T(8,128)S(1)}, f32[320,1280]{1,0:T(8,128)S(1)}, u32[]{:S(2)}, u32[]{:S(2)}) %collective-permute-start.12) | collective-permute-done | bytes 1638432 | tf_op jit(solution)/shard_map/ppermute | solution.py:955
  121.8 0.9 shard_map.259
  123.4 8.2 %collective-permute-start.16 = (f32[2,40,1280]{2,1,0:T(8,128)S(1)}, f32[2,40,1280]{2,1,0:T(8,128)S(1)}, u32[]{:S(2)}, u32[]{:S(2)}) collective-permute-start(f32[2,40,1280]{2,1,0:T(8,128)S(1)} %get-tuple-element.195), channel_id=1, source_target_pairs={{0,1},{1,0},{2,3},{3,2},{4,5},{5,4},{6,7},{7,6},{8,9},{9,8},{10,11... | collective-permute-start | bytes 1228808 | tf_op jit(solution)/shard_map/ppermute | solution.py:955
  131.6 2.9 %collective-permute-done.10 = f32[2,80,1280]{2,1,0:T(8,128)S(1)} collective-permute-done((f32[2,80,1280]{2,1,0:T(8,128)S(1)}, f32[2,80,1280]{2,1,0:T(8,128)S(1)}, u32[]{:S(2)}, u32[]{:S(2)}) %collective-permute-start.10) | collective-permute-done | bytes 819232 | tf_op jit(solution)/shard_map/ppermute | solution.py:955
  134.5 1.6 shard_map.261
  136.1 7.9 %collective-permute-start.15 = (f32[1,160,1280]{2,1,0:T(8,128)}, f32[1,160,1280]{2,1,0:T(8,128)}, u32[]{:S(2)}, u32[]{:S(2)}) collective-permute-start(f32[1,160,1280]{2,1,0:T(8,128)} %get-tuple-element.193), channel_id=1, source_target_pairs={{0,0},{1,2},{2,1},{3,3},{4,4},{5,6},{6,5},{7,7},{8,8},{9,10},{10,9... | collective-permute-start | bytes 2457608 | tf_op jit(solution)/shard_map/ppermute | solution.py:978
  144.0 1.5 collective-permute-start.20
  145.6 1.0 shard_map.262
  147.4 3.6 %collective-permute-start.19 = (f32[2,40,1408]{2,1,0:T(8,128)S(1)}, f32[2,40,1408]{2,1,0:T(8,128)S(1)}, u32[]{:S(2)}, u32[]{:S(2)}) collective-permute-start(f32[2,40,1408]{2,1,0:T(8,128)S(1)} %get-tuple-element.202), channel_id=1, source_target_pairs={{0,1},{1,0},{2,3},{3,2},{4,5},{5,4},{6,7},{7,6},{8,9},{9,8},{10,11... | collective-permute-start | bytes 1351688 | tf_op jit(solution)/shard_map/ppermute | solution.py:955
  150.9 1.5 collective-permute-start.14
  153.7 2.7 collective-permute-done.20
  156.4 1.4 shard_map.265
  158.5 1.6 collective-permute-start.25
  160.1 9.0 %collective-permute-done.18 = f32[1,40,1280]{2,1,0:T(8,128)S(1)} collective-permute-done((f32[1,40,1280]{2,1,0:T(8,128)S(1)}, f32[1,40,1280]{2,1,0:T(8,128)S(1)}, u32[]{:S(2)}, u32[]{:S(2)}) %collective-permute-start.18) | collective-permute-done | bytes 204832 | tf_op jit(solution)/shard_map/ppermute | solution.py:955
  169.1 1.2 shard_map.267
  170.3 4.8 %shard_map.268 = (f32[8,128]{1,0:T(8,128)S(1)}, f32[320,1280]{1,0:T(8,128)S(1)}, f32[320,1280]{1,0:T(8,128)S(1)}) custom-call(s32[4]{0:T(128)S(1)} %copy-done.1, f32[3840,256]{1,0:T(8,128)S(1)} %copy-done.11, f32[3200,256]{1,0:T(8,128)} %collective-permute-done.2.refs_2_.refs_1_, f32[3840,256]{1,0:T(8,128)S(1)} %copy-done.2, ...), custom_call_target="tpu_custom_call" | custom-call | flops 46000001024 | tf_op jit(solution)/shard_map/pallas_call | solution.py:843
  175.2 1.7 shard_map.269
  177.0 1.6 collective-permute-start.22
  180.0 1.5 copy-done.3
  181.5 4.8 %shard_map.272 = (f32[8,128]{1,0:T(8,128)S(1)}, f32[320,1280]{1,0:T(8,128)S(1)}, f32[320,1280]{1,0:T(8,128)S(1)}) custom-call(s32[4]{0:T(128)S(1)} %copy-done.1, f32[3840,256]{1,0:T(8,128)S(1)} %copy-done.11, f32[3200,256]{1,0:T(8,128)} %collective-permute-done.2.refs_2_.refs_1_, f32[3840,256]{1,0:T(8,128)S(1)} %copy-done.3, ...), custom_call_target="tpu_custom_call" | custom-call | flops 46000001024 | tf_op jit(solution)/shard_map/pallas_call | solution.py:843
  186.4 1.6 shard_map.273
  190.6 1.6 collective-permute-start.27
  192.2 5.9 %collective-permute-start.21 = (f32[1,80,1536]{2,1,0:T(8,128)S(1)}, f32[1,80,1536]{2,1,0:T(8,128)S(1)}, u32[]{:S(2)}, u32[]{:S(2)}) collective-permute-start(f32[1,80,1536]{2,1,0:T(8,128)S(1)} %get-tuple-element.212), channel_id=1, source_target_pairs={{0,1},{1,0},{2,3},{3,2},{4,5},{5,4},{6,7},{7,6},{8,9},{9,8},{10,11... | collective-permute-start | bytes 1474568 | tf_op jit(solution)/shard_map/ppermute | solution.py:955
  198.6 1.8 collective-permute-done.22
  200.4 1.4 shard_map.275
  201.8 4.3 %collective-permute-done.21 = f32[1,80,1536]{2,1,0:T(8,128)S(1)} collective-permute-done((f32[1,80,1536]{2,1,0:T(8,128)S(1)}, f32[1,80,1536]{2,1,0:T(8,128)S(1)}, u32[]{:S(2)}, u32[]{:S(2)}) %collective-permute-start.21) | collective-permute-done | bytes 491552 | tf_op jit(solution)/shard_map/ppermute | solution.py:955
  207.4 2.1 collective-permute-start.32
  210.2 1.5 collective-permute-start.33
  211.6 7.6 %collective-permute-done.28 = f32[320,1280]{1,0:T(8,128)S(1)} collective-permute-done((f32[320,1280]{1,0:T(8,128)S(1)}, f32[320,1280]{1,0:T(8,128)S(1)}, u32[]{:S(2)}, u32[]{:S(2)}) %collective-permute-start.28) | collective-permute-done | bytes 1638432 | tf_op jit(solution)/shard_map/ppermute | solution.py:955
  219.2 0.9 shard_map.278
  220.1 1.2 shard_map.279
  222.8 1.5 collective-permute-start.31
  224.3 6.2 %collective-permute-done.33 = f32[2,80,1280]{2,1,0:T(8,128)S(1)} collective-permute-done((f32[2,80,1280]{2,1,0:T(8,128)S(1)}, f32[2,80,1280]{2,1,0:T(8,128)S(1)}, u32[]{:S(2)}, u32[]{:S(2)}) %collective-permute-start.33) | collective-permute-done | bytes 819232 | tf_op jit(solution)/shard_map/ppermute | solution.py:955
  232.5 2.6 collective-permute-done.31
  235.8 1.8 collective-permute-start.35
  240.3 3.6 %collective-permute-done.35 = f32[1,80,1280]{2,1,0:T(8,128)S(1)} collective-permute-done((f32[1,80,1280]{2,1,0:T(8,128)S(1)}, f32[1,80,1280]{2,1,0:T(8,128)S(1)}, u32[]{:S(2)}, u32[]{:S(2)}) %collective-permute-start.35) | collective-permute-done | bytes 409632 | tf_op jit(solution)/shard_map/ppermute | solution.py:955
  245.9 6.2 %collective-permute-start.36 = (f32[2,40,1280]{2,1,0:T(8,128)S(1)}, f32[2,40,1280]{2,1,0:T(8,128)S(1)}, u32[]{:S(2)}, u32[]{:S(2)}) collective-permute-start(f32[2,40,1280]{2,1,0:T(8,128)S(1)} %get-tuple-element.256), channel_id=1, source_target_pairs={{0,1},{1,0},{2,3},{3,2},{4,5},{5,4},{6,7},{7,6},{8,9},{9,8},{10,11... | collective-permute-start | bytes 1228808 | tf_op jit(solution)/shard_map/ppermute | solution.py:955
  252.7 4.8 %collective-permute-start.39 = (f32[1,40,1280]{2,1,0:T(8,128)S(1)}, f32[1,40,1280]{2,1,0:T(8,128)S(1)}, u32[]{:S(2)}, u32[]{:S(2)}) collective-permute-start(f32[1,40,1280]{2,1,0:T(8,128)S(1)} %get-tuple-element.263), channel_id=1, source_target_pairs={{0,1},{1,0},{2,3},{3,2},{4,5},{5,4},{6,7},{7,6},{8,9},{9,8},{10,11... | collective-permute-start | bytes 614408 | tf_op jit(solution)/shard_map/ppermute | solution.py:955
  257.5 2.7 collective-permute-done.36
  260.9 1.5 collective-permute-done.39
  262.9 3.7 %collective-permute-done.38 = f32[1,40,1280]{2,1,0:T(8,128)S(1)} collective-permute-done((f32[1,40,1280]{2,1,0:T(8,128)S(1)}, f32[1,40,1280]{2,1,0:T(8,128)S(1)}, u32[]{:S(2)}, u32[]{:S(2)}) %collective-permute-start.38) | collective-permute-done | bytes 204832 | tf_op jit(solution)/shard_map/ppermute | solution.py:955
  266.7 1.2 shard_map.290
  267.8 0.9 pad_maximum_fusion
  (99 shorter events, 28.5 us)
Async XLA Ops:
  1.3 26.8 %copy-start = (s32[4]{0:T(128)S(1)}, s32[4]{0:T(128)}, u32[]{:S(2)}) copy-start(s32[4]{0:T(128)} %pad_add_fusion.place_ref) | copy-start | bytes 52
  23.8 4.3 %collective-permute-start.1 = (f32[1920,256]{1,0:T(8,128)}, f32[1920,256]{1,0:T(8,128)S(1)}, u32[]{:S(2)}, u32[]{:S(2)}) collective-permute-start(f32[1920,256]{1,0:T(8,128)} %get-tuple-element.153.refs_1_), channel_id=1, source_target_pairs={{0,4},{1,5},{2,6},{3,7},{4,0},{5,1},{6,2},{7,3},{8,12},{9,13},{10,... | collective-permute-start | bytes 5898248 | tf_op jit(solution)/shard_map/ppermute | solution.py:1082
  24.3 15.8 %collective-permute-start = (f32[2688,256]{1,0:T(8,128)}, f32[2688,256]{1,0:T(8,128)S(1)}, u32[]{:S(2)}, u32[]{:S(2)}) collective-permute-start(f32[2688,256]{1,0:T(8,128)} %get-tuple-element.152.refs_1_), channel_id=1, source_target_pairs={{0,4},{1,5},{2,6},{3,7},{4,0},{5,1},{6,2},{7,3},{8,12},{9,13},{10,... | collective-permute-start | bytes 8257544 | tf_op jit(solution)/shard_map/ppermute | solution.py:1082
  24.4 53.6 %collective-permute-start.2 = (f32[3200,256]{1,0:T(8,128)}, f32[3200,256]{1,0:T(8,128)}, u32[]{:S(2)}, u32[]{:S(2)}) collective-permute-start(f32[3200,256]{1,0:T(8,128)} %get-tuple-element.158.refs_1_), channel_id=1, source_target_pairs={{0,4},{1,5},{2,6},{3,7},{4,0},{5,1},{6,2},{7,3},{8,12},{9,13},{10,... | collective-permute-start | bytes 9830408 | tf_op jit(solution)/shard_map/ppermute | solution.py:1082
  28.1 1.5 copy-start.7
  29.7 2.1 copy-start.10
  31.8 0.7 copy-start.15
  32.5 7.6 %copy-start.5 = (f32[2688,256]{1,0:T(8,128)S(1)}, f32[2688,256]{1,0:T(8,128)}, u32[]{:S(2)}) copy-start(f32[2688,256]{1,0:T(8,128)} %get-tuple-element.152.refs_1_) | copy-start | bytes 8257540
  37.1 9.0 %copy-start.8 = (f32[320,1280]{1,0:T(8,128)}, f32[320,1280]{1,0:T(8,128)S(1)}, u32[]{:S(2)}) copy-start(f32[320,1280]{1,0:T(8,128)S(1)} %get-tuple-element.164) | copy-start | bytes 4915204
  37.1 32.5 %collective-permute-start.6 = (f32[320,1280]{1,0:T(8,128)}, f32[320,1280]{1,0:T(8,128)}, u32[]{:S(2)}, u32[]{:S(2)}) collective-permute-start(f32[320,1280]{1,0:T(8,128)} %get-tuple-element.165), channel_id=1, source_target_pairs={{0,8},{1,9},{2,10},{3,11},{4,20},{5,21},{6,22},{7,23},{8,0},{9,1},... | collective-permute-start | bytes 4915208 | tf_op jit(solution)/shard_map/ppermute | solution.py:955
  46.2 0.6 copy-start.14
  46.2 43.3 %collective-permute-start.4 = (f32[320,1408]{1,0:T(8,128)}, f32[320,1408]{1,0:T(8,128)}, u32[]{:S(2)}, u32[]{:S(2)}) collective-permute-start(f32[320,1408]{1,0:T(8,128)} %get-tuple-element.162), channel_id=1, source_target_pairs={{0,8},{1,9},{2,10},{3,11},{4,20},{5,21},{6,22},{7,23},{8,0},{9,1},... | collective-permute-start | bytes 5406728 | tf_op jit(solution)/shard_map/ppermute | solution.py:955
  46.8 22.9 %copy-start.1 = (s32[4]{0:T(128)S(1)}, s32[4]{0:T(128)}, u32[]{:S(2)}) copy-start(s32[4]{0:T(128)} %pad_add_fusion.place_ref) | copy-start | bytes 52
  69.1 24.9 %collective-permute-start.3 = (f32[2664,256]{1,0:T(8,128)}, f32[2664,256]{1,0:T(8,128)S(1)}, u32[]{:S(2)}, u32[]{:S(2)}) collective-permute-start(f32[2664,256]{1,0:T(8,128)} %get-tuple-element.159.refs_2_), channel_id=1, source_target_pairs={{0,4},{1,5},{2,6},{3,7},{4,0},{5,1},{6,2},{7,3},{8,12},{9,13},{10,... | collective-permute-start | bytes 8183816 | tf_op jit(solution)/shard_map/ppermute | solution.py:1082
  69.1 15.5 %collective-permute-start.5 = (f32[3840,256]{1,0:T(8,128)}, f32[3840,256]{1,0:T(8,128)S(1)}, u32[]{:S(2)}, u32[]{:S(2)}) collective-permute-start(f32[3840,256]{1,0:T(8,128)} %get-tuple-element.163.refs_2_), channel_id=1, source_target_pairs={{0,4},{1,5},{2,6},{3,7},{4,0},{5,1},{6,2},{7,3},{8,12},{9,13},{10,... | collective-permute-start | bytes 11796488 | tf_op jit(solution)/shard_map/ppermute | solution.py:1082
  69.6 1.4 copy-start.9
  71.1 0.7 copy-start.13
  71.8 6.2 %copy-start.4 = (f32[3200,256]{1,0:T(8,128)S(1)}, f32[3200,256]{1,0:T(8,128)}, u32[]{:S(2)}) copy-start(f32[3200,256]{1,0:T(8,128)} %get-tuple-element.158.refs_1_) | copy-start | bytes 9830404
  71.8 6.2 %copy-start.11 = (f32[3840,256]{1,0:T(8,128)S(1)}, f32[3840,256]{1,0:T(8,128)}, u32[]{:S(2)}) copy-start(f32[3840,256]{1,0:T(8,128)} %get-tuple-element.151.refs_0_) | copy-start | bytes 11796484
  76.4 24.6 %collective-permute-start.9 = (f32[2,80,1280]{2,1,0:T(8,128)}, f32[2,80,1280]{2,1,0:T(8,128)}, u32[]{:S(2)}, u32[]{:S(2)}) collective-permute-start(f32[2,80,1280]{2,1,0:T(8,128)} %get-tuple-element.176), channel_id=1, source_target_pairs={{0,1},{1,0},{2,3},{3,2},{4,5},{5,4},{6,7},{7,6},{8,9},{9,8},{10,11... | collective-permute-start | bytes 2457608 | tf_op jit(solution)/shard_map/ppermute | solution.py:955
  78.0 6.6 %copy-start.2 = (f32[3840,256]{1,0:T(8,128)S(1)}, f32[3840,256]{1,0:T(8,128)}, u32[]{:S(2)}) copy-start(f32[3840,256]{1,0:T(8,128)} %get-tuple-element.163.refs_2_) | copy-start | bytes 11796484
  83.1 21.2 %collective-permute-start.8 = (f32[320,1280]{1,0:T(8,128)S(1)}, f32[320,1280]{1,0:T(8,128)S(1)}, u32[]{:S(2)}, u32[]{:S(2)}) collective-permute-start(f32[320,1280]{1,0:T(8,128)S(1)} %get-tuple-element.174), channel_id=1, source_target_pairs={{0,8},{1,9},{2,10},{3,11},{4,20},{5,21},{6,22},{7,23},{8,0},{9,1},... | collective-permute-start | bytes 4915208 | tf_op jit(solution)/shard_map/ppermute | solution.py:955
  89.5 4.5 %copy-start.6 = (f32[2664,256]{1,0:T(8,128)S(1)}, f32[2664,256]{1,0:T(8,128)}, u32[]{:S(2)}) copy-start(f32[2664,256]{1,0:T(8,128)} %get-tuple-element.159.refs_2_) | copy-start | bytes 8183812
  89.5 4.5 %copy-start.12 = (f32[1280,256]{1,0:T(8,128)S(1)}, f32[1280,256]{1,0:T(8,128)}, u32[]{:S(2)}) copy-start(f32[1280,256]{1,0:T(8,128)} %get-tuple-element.160.refs_4_) | copy-start | bytes 3932164
  93.0 24.0 %collective-permute-start.13 = (f32[2,80,1408]{2,1,0:T(8,128)S(1)}, f32[2,80,1408]{2,1,0:T(8,128)S(1)}, u32[]{:S(2)}, u32[]{:S(2)}) collective-permute-start(f32[2,80,1408]{2,1,0:T(8,128)S(1)} %get-tuple-element.185), channel_id=1, source_target_pairs={{0,1},{1,0},{2,3},{3,2},{4,5},{5,4},{6,7},{7,6},{8,9},{9,8},{10,11... | collective-permute-start | bytes 2703368 | tf_op jit(solution)/shard_map/ppermute | solution.py:955
  93.5 28.3 %collective-permute-start.12 = (f32[320,1280]{1,0:T(8,128)S(1)}, f32[320,1280]{1,0:T(8,128)S(1)}, u32[]{:S(2)}, u32[]{:S(2)}) collective-permute-start(f32[320,1280]{1,0:T(8,128)S(1)} %get-tuple-element.183), channel_id=1, source_target_pairs={{0,8},{1,9},{2,10},{3,11},{4,20},{5,21},{6,22},{7,23},{8,0},{9,1},... | collective-permute-start | bytes 4915208 | tf_op jit(solution)/shard_map/ppermute | solution.py:955
  105.6 28.9 %collective-permute-start.10 = (f32[2,80,1280]{2,1,0:T(8,128)S(1)}, f32[2,80,1280]{2,1,0:T(8,128)S(1)}, u32[]{:S(2)}, u32[]{:S(2)}) collective-permute-start(f32[2,80,1280]{2,1,0:T(8,128)S(1)} %get-tuple-element.180), channel_id=1, source_target_pairs={{0,1},{1,0},{2,3},{3,2},{4,5},{5,4},{6,7},{7,6},{8,9},{9,8},{10,11... | collective-permute-start | bytes 2457608 | tf_op jit(solution)/shard_map/ppermute | solution.py:955
  106.1 16.5 %collective-permute-start.11 = (f32[1,160,1280]{2,1,0:T(8,128)S(1)}, f32[1,160,1280]{2,1,0:T(8,128)S(1)}, u32[]{:S(2)}, u32[]{:S(2)}) collective-permute-start(f32[1,160,1280]{2,1,0:T(8,128)S(1)} %get-tuple-element.181), channel_id=1, source_target_pairs={{0,0},{1,2},{2,1},{3,3},{4,4},{5,6},{6,5},{7,7},{8,8},{9,10},{10,9... | collective-permute-start | bytes 2457608 | tf_op jit(solution)/shard_map/ppermute | solution.py:978
  106.8 38.7 %collective-permute-start.7 = (f32[320,1536]{1,0:T(8,128)S(1)}, f32[320,1536]{1,0:T(8,128)S(1)}, u32[]{:S(2)}, u32[]{:S(2)}) collective-permute-start(f32[320,1536]{1,0:T(8,128)S(1)} %get-tuple-element.172), channel_id=1, source_target_pairs={{0,8},{1,9},{2,10},{3,11},{4,20},{5,21},{6,22},{7,23},{8,0},{9,1},... | collective-permute-start | bytes 5898248 | tf_op jit(solution)/shard_map/ppermute | solution.py:955
  117.7 28.9 %collective-permute-start.17 = (f32[1,160,1408]{2,1,0:T(8,128)S(1)}, f32[1,160,1408]{2,1,0:T(8,128)S(1)}, u32[]{:S(2)}, u32[]{:S(2)}) collective-permute-start(f32[1,160,1408]{2,1,0:T(8,128)S(1)} %get-tuple-element.196), channel_id=1, source_target_pairs={{0,0},{1,2},{2,1},{3,3},{4,4},{5,6},{6,5},{7,7},{8,8},{9,10},{10,9... | collective-permute-start | bytes 2703368 | tf_op jit(solution)/shard_map/ppermute | solution.py:978
  123.4 29.0 %collective-permute-start.16 = (f32[2,40,1280]{2,1,0:T(8,128)S(1)}, f32[2,40,1280]{2,1,0:T(8,128)S(1)}, u32[]{:S(2)}, u32[]{:S(2)}) collective-permute-start(f32[2,40,1280]{2,1,0:T(8,128)S(1)} %get-tuple-element.195), channel_id=1, source_target_pairs={{0,1},{1,0},{2,3},{3,2},{4,5},{5,4},{6,7},{7,6},{8,9},{9,8},{10,11... | collective-permute-start | bytes 1228808 | tf_op jit(solution)/shard_map/ppermute | solution.py:955
  136.1 39.1 %collective-permute-start.15 = (f32[1,160,1280]{2,1,0:T(8,128)}, f32[1,160,1280]{2,1,0:T(8,128)}, u32[]{:S(2)}, u32[]{:S(2)}) collective-permute-start(f32[1,160,1280]{2,1,0:T(8,128)} %get-tuple-element.193), channel_id=1, source_target_pairs={{0,0},{1,2},{2,1},{3,3},{4,4},{5,6},{6,5},{7,7},{8,8},{9,10},{10,9... | collective-permute-start | bytes 2457608 | tf_op jit(solution)/shard_map/ppermute | solution.py:978
  144.0 12.3 %collective-permute-start.20 = (f32[1,160,1280]{2,1,0:T(8,128)S(1)}, f32[1,160,1280]{2,1,0:T(8,128)S(1)}, u32[]{:S(2)}, u32[]{:S(2)}) collective-permute-start(f32[1,160,1280]{2,1,0:T(8,128)S(1)} %get-tuple-element.204), channel_id=1, source_target_pairs={{0,16},{1,17},{2,18},{3,19},{4,12},{5,13},{6,14},{7,15},{8,24},{9,... | collective-permute-start | bytes 2457608 | tf_op jit(solution)/shard_map/ppermute | solution.py:955
  147.4 10.5 %collective-permute-start.19 = (f32[2,40,1408]{2,1,0:T(8,128)S(1)}, f32[2,40,1408]{2,1,0:T(8,128)S(1)}, u32[]{:S(2)}, u32[]{:S(2)}) collective-permute-start(f32[2,40,1408]{2,1,0:T(8,128)S(1)} %get-tuple-element.202), channel_id=1, source_target_pairs={{0,1},{1,0},{2,3},{3,2},{4,5},{5,4},{6,7},{7,6},{8,9},{9,8},{10,11... | collective-permute-start | bytes 1351688 | tf_op jit(solution)/shard_map/ppermute | solution.py:955
  150.9 27.7 %collective-permute-start.14 = (f32[1,160,1536]{2,1,0:T(8,128)S(1)}, f32[1,160,1536]{2,1,0:T(8,128)S(1)}, u32[]{:S(2)}, u32[]{:S(2)}) collective-permute-start(f32[1,160,1536]{2,1,0:T(8,128)S(1)} %get-tuple-element.192), channel_id=1, source_target_pairs={{0,16},{1,17},{2,18},{3,19},{4,12},{5,13},{6,14},{7,15},{8,24},{9,... | collective-permute-start | bytes 2949128 | tf_op jit(solution)/shard_map/ppermute | solution.py:955
  153.1 16.0 %collective-permute-start.18 = (f32[1,40,1280]{2,1,0:T(8,128)S(1)}, f32[1,40,1280]{2,1,0:T(8,128)S(1)}, u32[]{:S(2)}, u32[]{:S(2)}) collective-permute-start(f32[1,40,1280]{2,1,0:T(8,128)S(1)} %get-tuple-element.200), channel_id=1, source_target_pairs={{0,16},{1,17},{2,18},{3,19},{4,12},{5,13},{6,14},{7,15},{8,24},{9,... | collective-permute-start | bytes 614408 | tf_op jit(solution)/shard_map/ppermute | solution.py:955
  157.8 28.6 %collective-permute-start.24 = (f32[1,80,1280]{2,1,0:T(8,128)}, f32[1,80,1280]{2,1,0:T(8,128)}, u32[]{:S(2)}, u32[]{:S(2)}) collective-permute-start(f32[1,80,1280]{2,1,0:T(8,128)} %get-tuple-element.218), channel_id=1, source_target_pairs={{0,1},{1,0},{2,3},{3,2},{4,5},{5,4},{6,7},{7,6},{8,9},{9,8},{10,11... | collective-permute-start | bytes 1228808 | tf_op jit(solution)/shard_map/ppermute | solution.py:955
  158.5 20.9 %collective-permute-start.25 = (f32[1,40,1408]{2,1,0:T(8,128)S(1)}, f32[1,40,1408]{2,1,0:T(8,128)S(1)}, u32[]{:S(2)}, u32[]{:S(2)}) collective-permute-start(f32[1,40,1408]{2,1,0:T(8,128)S(1)} %get-tuple-element.220), channel_id=1, source_target_pairs={{0,16},{1,17},{2,18},{3,19},{4,12},{5,13},{6,14},{7,15},{8,24},{9,... | collective-permute-start | bytes 675848 | tf_op jit(solution)/shard_map/ppermute | solution.py:955
  176.9 13.0 %collective-permute-start.23 = (f32[2,40,1280]{2,1,0:T(8,128)S(1)}, f32[2,40,1280]{2,1,0:T(8,128)S(1)}, u32[]{:S(2)}, u32[]{:S(2)}) collective-permute-start(f32[2,40,1280]{2,1,0:T(8,128)S(1)} %get-tuple-element.216), channel_id=1, source_target_pairs={{0,1},{1,0},{2,3},{3,2},{4,5},{5,4},{6,7},{7,6},{8,9},{9,8},{10,11... | collective-permute-start | bytes 1228808 | tf_op jit(solution)/shard_map/ppermute | solution.py:955
  177.0 23.4 %collective-permute-start.22 = (f32[320,1280]{1,0:T(8,128)S(1)}, f32[320,1280]{1,0:T(8,128)S(1)}, u32[]{:S(2)}, u32[]{:S(2)}) collective-permute-start(f32[320,1280]{1,0:T(8,128)S(1)} %get-tuple-element.214), channel_id=1, source_target_pairs={{0,8},{1,9},{2,10},{3,11},{4,20},{5,21},{6,22},{7,23},{8,0},{9,1},... | collective-permute-start | bytes 4915208 | tf_op jit(solution)/shard_map/ppermute | solution.py:955
  179.4 2.1 copy-start.3
  189.3 17.5 %collective-permute-start.29 = (f32[1,80,1280]{2,1,0:T(8,128)S(1)}, f32[1,80,1280]{2,1,0:T(8,128)S(1)}, u32[]{:S(2)}, u32[]{:S(2)}) collective-permute-start(f32[1,80,1280]{2,1,0:T(8,128)S(1)} %get-tuple-element.232), channel_id=1, source_target_pairs={{0,0},{1,2},{2,1},{3,3},{4,4},{5,6},{6,5},{7,7},{8,8},{9,10},{10,9... | collective-permute-start | bytes 1228808 | tf_op jit(solution)/shard_map/ppermute | solution.py:978
  190.6 29.5 %collective-permute-start.27 = (f32[1,40,1280]{2,1,0:T(8,128)S(1)}, f32[1,40,1280]{2,1,0:T(8,128)S(1)}, u32[]{:S(2)}, u32[]{:S(2)}) collective-permute-start(f32[1,40,1280]{2,1,0:T(8,128)S(1)} %get-tuple-element.229), channel_id=1, source_target_pairs={{0,16},{1,17},{2,18},{3,19},{4,12},{5,13},{6,14},{7,15},{8,24},{9,... | collective-permute-start | bytes 614408 | tf_op jit(solution)/shard_map/ppermute | solution.py:955
  192.2 13.9 %collective-permute-start.21 = (f32[1,80,1536]{2,1,0:T(8,128)S(1)}, f32[1,80,1536]{2,1,0:T(8,128)S(1)}, u32[]{:S(2)}, u32[]{:S(2)}) collective-permute-start(f32[1,80,1536]{2,1,0:T(8,128)S(1)} %get-tuple-element.212), channel_id=1, source_target_pairs={{0,1},{1,0},{2,3},{3,2},{4,5},{5,4},{6,7},{7,6},{8,9},{9,8},{10,11... | collective-permute-start | bytes 1474568 | tf_op jit(solution)/shard_map/ppermute | solution.py:955
  198.1 21.1 %collective-permute-start.28 = (f32[320,1280]{1,0:T(8,128)S(1)}, f32[320,1280]{1,0:T(8,128)S(1)}, u32[]{:S(2)}, u32[]{:S(2)}) collective-permute-start(f32[320,1280]{1,0:T(8,128)S(1)} %get-tuple-element.231), channel_id=1, source_target_pairs={{0,8},{1,9},{2,10},{3,11},{4,20},{5,21},{6,22},{7,23},{8,0},{9,1},... | collective-permute-start | bytes 4915208 | tf_op jit(solution)/shard_map/ppermute | solution.py:955
  207.4 24.6 %collective-permute-start.32 = (f32[1,40,1280]{2,1,0:T(8,128)S(1)}, f32[1,40,1280]{2,1,0:T(8,128)S(1)}, u32[]{:S(2)}, u32[]{:S(2)}) collective-permute-start(f32[1,40,1280]{2,1,0:T(8,128)S(1)} %get-tuple-element.242), channel_id=1, source_target_pairs={{0,1},{1,0},{2,3},{3,2},{4,5},{5,4},{6,7},{7,6},{8,9},{9,8},{10,11... | collective-permute-start | bytes 614408 | tf_op jit(solution)/shard_map/ppermute | solution.py:955
  209.5 11.9 %collective-permute-start.26 = (f32[1,80,1536]{2,1,0:T(8,128)S(1)}, f32[1,80,1536]{2,1,0:T(8,128)S(1)}, u32[]{:S(2)}, u32[]{:S(2)}) collective-permute-start(f32[1,80,1536]{2,1,0:T(8,128)S(1)} %get-tuple-element.227), channel_id=1, source_target_pairs={{0,0},{1,2},{2,1},{3,3},{4,4},{5,6},{6,5},{7,7},{8,8},{9,10},{10,9... | collective-permute-start | bytes 1474568 | tf_op jit(solution)/shard_map/ppermute | solution.py:978
  210.2 20.4 %collective-permute-start.33 = (f32[2,80,1280]{2,1,0:T(8,128)S(1)}, f32[2,80,1280]{2,1,0:T(8,128)S(1)}, u32[]{:S(2)}, u32[]{:S(2)}) collective-permute-start(f32[2,80,1280]{2,1,0:T(8,128)S(1)} %get-tuple-element.244), channel_id=1, source_target_pairs={{0,1},{1,0},{2,3},{3,2},{4,5},{5,4},{6,7},{7,6},{8,9},{9,8},{10,11... | collective-permute-start | bytes 2457608 | tf_op jit(solution)/shard_map/ppermute | solution.py:955
  222.0 15.6 %collective-permute-start.30 = (f32[1,40,1536]{2,1,0:T(8,128)S(1)}, f32[1,40,1536]{2,1,0:T(8,128)S(1)}, u32[]{:S(2)}, u32[]{:S(2)}) collective-permute-start(f32[1,40,1536]{2,1,0:T(8,128)S(1)} %get-tuple-element.238), channel_id=1, source_target_pairs={{0,1},{1,0},{2,3},{3,2},{4,5},{5,4},{6,7},{7,6},{8,9},{9,8},{10,11... | collective-permute-start | bytes 737288 | tf_op jit(solution)/shard_map/ppermute | solution.py:955
  222.8 12.3 %collective-permute-start.31 = (f32[1,160,1280]{2,1,0:T(8,128)S(1)}, f32[1,160,1280]{2,1,0:T(8,128)S(1)}, u32[]{:S(2)}, u32[]{:S(2)}) collective-permute-start(f32[1,160,1280]{2,1,0:T(8,128)S(1)} %get-tuple-element.240), channel_id=1, source_target_pairs={{0,16},{1,17},{2,18},{3,19},{4,12},{5,13},{6,14},{7,15},{8,24},{9,... | collective-permute-start | bytes 2457608 | tf_op jit(solution)/shard_map/ppermute | solution.py:955
  231.2 13.9 %collective-permute-start.34 = (f32[1,160,1280]{2,1,0:T(8,128)S(1)}, f32[1,160,1280]{2,1,0:T(8,128)S(1)}, u32[]{:S(2)}, u32[]{:S(2)}) collective-permute-start(f32[1,160,1280]{2,1,0:T(8,128)S(1)} %get-tuple-element.250), channel_id=1, source_target_pairs={{0,0},{1,2},{2,1},{3,3},{4,4},{5,6},{6,5},{7,7},{8,8},{9,10},{10,9... | collective-permute-start | bytes 2457608 | tf_op jit(solution)/shard_map/ppermute | solution.py:978
  235.8 8.0 %collective-permute-start.35 = (f32[1,80,1280]{2,1,0:T(8,128)S(1)}, f32[1,80,1280]{2,1,0:T(8,128)S(1)}, u32[]{:S(2)}, u32[]{:S(2)}) collective-permute-start(f32[1,80,1280]{2,1,0:T(8,128)S(1)} %get-tuple-element.252), channel_id=1, source_target_pairs={{0,1},{1,0},{2,3},{3,2},{4,5},{5,4},{6,7},{7,6},{8,9},{9,8},{10,11... | collective-permute-start | bytes 1228808 | tf_op jit(solution)/shard_map/ppermute | solution.py:955
  244.4 7.6 %collective-permute-start.37 = (f32[1,80,1280]{2,1,0:T(8,128)S(1)}, f32[1,80,1280]{2,1,0:T(8,128)S(1)}, u32[]{:S(2)}, u32[]{:S(2)}) collective-permute-start(f32[1,80,1280]{2,1,0:T(8,128)S(1)} %get-tuple-element.257), channel_id=1, source_target_pairs={{0,0},{1,2},{2,1},{3,3},{4,4},{5,6},{6,5},{7,7},{8,8},{9,10},{10,9... | collective-permute-start | bytes 1228808 | tf_op jit(solution)/shard_map/ppermute | solution.py:978
  245.9 14.3 %collective-permute-start.36 = (f32[2,40,1280]{2,1,0:T(8,128)S(1)}, f32[2,40,1280]{2,1,0:T(8,128)S(1)}, u32[]{:S(2)}, u32[]{:S(2)}) collective-permute-start(f32[2,40,1280]{2,1,0:T(8,128)S(1)} %get-tuple-element.256), channel_id=1, source_target_pairs={{0,1},{1,0},{2,3},{3,2},{4,5},{5,4},{6,7},{7,6},{8,9},{9,8},{10,11... | collective-permute-start | bytes 1228808 | tf_op jit(solution)/shard_map/ppermute | solution.py:955
  252.7 9.7 %collective-permute-start.39 = (f32[1,40,1280]{2,1,0:T(8,128)S(1)}, f32[1,40,1280]{2,1,0:T(8,128)S(1)}, u32[]{:S(2)}, u32[]{:S(2)}) collective-permute-start(f32[1,40,1280]{2,1,0:T(8,128)S(1)} %get-tuple-element.263), channel_id=1, source_target_pairs={{0,1},{1,0},{2,3},{3,2},{4,5},{5,4},{6,7},{7,6},{8,9},{9,8},{10,11... | collective-permute-start | bytes 614408 | tf_op jit(solution)/shard_map/ppermute | solution.py:955
  260.8 5.8 %collective-permute-start.38 = (f32[1,40,1280]{2,1,0:T(8,128)S(1)}, f32[1,40,1280]{2,1,0:T(8,128)S(1)}, u32[]{:S(2)}, u32[]{:S(2)}) collective-permute-start(f32[1,40,1280]{2,1,0:T(8,128)S(1)} %get-tuple-element.261), channel_id=1, source_target_pairs={{0,16},{1,17},{2,18},{3,19},{4,12},{5,13},{6,14},{7,15},{8,24},{9,... | collective-permute-start | bytes 614408 | tf_op jit(solution)/shard_map/ppermute | solution.py:955

commit v4 on v3

--- a/solution.py
+++ b/solution.py
@@ -1,5 +1,4 @@
 import functools
-import math
 
 import jax
 import jax.numpy as jnp
@@ -25,10 +24,47 @@
     return jnp.asarray(np.cos(angles)), jnp.asarray(np.sin(angles))
 
 
-TILE_BYTES = 409600
-ORDERS = {"A": "azb", "B": "azb", "C": "azb", "D1": "azb", "D2": "abz", "D3": "abz", "E": "abz"}
+VMEM_GRADIENT = 60
+VMEM_COMBINE = 24
+ORDERS = {"A": "abY", "B": "zab", "C": "azb", "E": "abz", "D1": "abz", "D2": "azb"}
+JOINT_TILES = {"D1": 15, "D2": 15}
 PROGRAM = (
-    "A", "B", "K", "A", "C", "D3", "B", "E", "A", "C", "B", "D3", "A", "C", "E", "B", "A", "D3", "B", "A", "D1", "C", "E", "B", "D2", "D3", "C", "D1", "E", "D3", "D2", "C", "E", "D1", "D3", "D2", "E", "D2", "D1", "D2", "D1", "D2", "D1",
+    ("F", (), 18),
+    ("G", ("A", ), 12),
+    ("G", ("B", ), 25),
+    ("G", ("C", ), 40),
+    ("K", (), 1),
+    ("+", ("A", ), 3),
+    ("+", ("C", ), 40),
+    ("G", ("D2", ), 0),
+    ("+", ("B", ), 8),
+    ("+", ("A", ), 5),
+    ("G", ("D1", ), 3),
+    ("+", ("C", ), 8),
+    ("G", ("E", ), 0),
+    ("+", ("D2", ), 5),
+    ("+", ("B", ), 8),
+    ("+", ("D1", ), 3),
+    ("+", ("A", ), 0),
+    ("+", ("D2", ), 3),
+    ("+", ("E", ), 5),
+    ("+", ("C", ), 3),
+    ("+", ("B", ), 3),
+    ("+", ("D1", ), 0.3),
+    ("+", ("C", ), 1),
+    ("+", ("E", ), 0),
+    ("+", ("B", ), 0.3),
+    ("+", ("C", ), 0),
+    ("+", ("D1", ), 0.3),
+    ("+", ("D2", ), 40),
+    ("+", ("B", ), 0.3),
+    ("+", ("E", ), 2),
+    ("+", ("D1", ), 5),
+    ("+", ("D2", ), 0),
+    ("+", ("E", ), 18),
+    ("+", ("D2", ), 0),
+    ("+", ("D1", ), 18),
+    ("+", ("E", ), 3),
 )
 
 
@@ -128,8 +164,8 @@
 TOKEN = jax.ShapeDtypeStruct((8, 128), jnp.float32)
 
 
-def COST(microseconds):
-    return pl.CostEstimate(flops=int(microseconds * 11500000000.0), bytes_accessed=0, transcendentals=0)
+def expect(microseconds):
+    return pl.CostEstimate(flops=int(microseconds * 1.15e9), bytes_accessed=0, transcendentals=0)
 
 
 OWN = ("branch", "normed_two", "resid", "mixed", "normed_one", "hidden")
@@ -409,7 +445,7 @@
         copy.wait()
 
 
-def front(place, lengths, series, flags, cotangent, tables, weights, heads):
+def front(place, lengths, series, flags, cotangent, tables, weights, heads, cost):
     lift, mix, skip, gain_first, joint, merge, gain_second, grow, shrink, head = weights
     rows, horizon = cotangent.shape
     width = mix.shape[0]
@@ -466,7 +502,7 @@
         out_specs=[vmem] * 7 + [hbm] * 7,
         scratch_shapes=scratch,
         compiler_params=pltpu.CompilerParams(vmem_limit_bytes=62 * 1024 * 1024),
-        cost_estimate=COST(22.0),
+        cost_estimate=expect(cost),
     )(
         lengths,
         place,
@@ -616,7 +652,7 @@
             joint_pack[pl.ds(at * width + begin, head_dim), :] = result.astype(jnp.float32)
         return 0
 
-    lax.fori_loop(0, heads, one_head, 0, unroll=2)
+    lax.fori_loop(0, heads, one_head, 0, unroll=8)
     store(joint_pack, joint_hbm_out)
     loads[1].wait()
     tile = rows
@@ -676,7 +712,7 @@
         copy.wait()
 
 
-def back(token, place, lengths, series, flags, tables, weights, kept_values, heads):
+def back(token, place, lengths, series, flags, tables, weights, kept_values, heads, cost):
     lift, mix, skip, gain_first, joint, merge = weights
     tokens, logsum, sigma_sum, center_sum, second_sum, embedded, middle, turned = kept_values
     rows, width = embedded.shape
@@ -708,7 +744,7 @@
         out_specs=[vmem] * 2 + [hbm] * 3,
         scratch_shapes=scratch,
         compiler_params=pltpu.CompilerParams(vmem_limit_bytes=62 * 1024 * 1024),
-        cost_estimate=COST(22.0),
+        cost_estimate=expect(cost),
     )(
         lengths,
         place,
@@ -733,21 +769,14 @@
     )
 
 
-def gradient_kernel(place_ref, *refs, terms, arrays, unit, axis, columns):
+def gradient_kernel(place_ref, *refs, pieces, arrays, unit):
     sources = refs[:arrays]
-    token_ref, send_hbm, keep_hbm = refs[arrays + 1 : arrays + 4]
-    result_ref, left_raw, left_ref, right_raw, load_sem, store_sem = refs[arrays + 4 :]
+    token_ref, outputs = refs[arrays + 1], refs[arrays + 2 : arrays + 2 + 2 * len(pieces)]
+    result_ref, left_raw, left_ref, right_raw, load_sem, store_sem = refs[arrays + 2 + 2 * len(pieces) :]
     token_ref[...] = jnp.zeros_like(token_ref)
-    if axis == "z":
-        height, mine = unit // 2, place_ref[3] & 1
-        starts = [group * unit + half * height for half in (1 - mine, mine) for group in range(4)]
-    else:
-        height, mine, core = unit, place_ref[1], place_ref[0]
-        stride, across = 1 + core, 2 - core
-        starts = [(stride * side + across * other) * unit for side in (1 - mine, mine) for other in (0, 1)]
     total = 4 * unit
     rows = left_raw.shape[2]
-    loads = []
+    loads, stores, lefts, rights = [], [], {}, []
 
     def load(source, first, target):
         copy = pltpu.make_async_copy(sources[source].at[pl.ds(first, target.shape[0])], target, load_sem.at[len(loads)])
@@ -755,161 +784,232 @@
         loads.append(copy)
         return copy
 
-    lefts, rights = [], []
-    for at, (own, own_row, other, other_row, near, far, row, kind, width, _) in enumerate(terms):
-        if kind != "sum":
-            lefts.append((load(own, own_row, left_raw.at[2 * at]), load(other, other_row, left_raw.at[2 * at + 1])))
+    place = 0
+    for _, terms in pieces:
+        for own, own_row, other, other_row, near, far, row, kind, width in terms:
+            key = (own, own_row, other, other_row)
+            if kind != "sum" and key not in lefts:
+                at = len(lefts)
+                copies = [load(own, own_row, left_raw.at[2 * at]), load(other, other_row, left_raw.at[2 * at + 1])]
+                lefts[key] = (at, copies)
+            tiles = []
+            for tile in range(0, width, rows):
+                size = min(rows, width - tile)
+                spots = [right_raw.at[pl.ds(place + side * size, size)] for side in (0, 1)]
+                place += 2 * size
+                tiles.append((size, spots, [load(side, row + tile, spot) for side, spot in zip((near, far), spots)]))
+            rights.append(tiles)
+    waited = set()
+    number = 0
+    tile_at = 0
+    for order, (axis, terms) in enumerate(pieces):
+        core = place_ref[0]
+        stride, across = 1 + core, 2 - core
+        if axis == "z":
+            height, mine = unit // 2, place_ref[3] & 1
+            groups = [stride * a + across * b for b in (0, 1) for a in (0, 1)]
+            starts = [group * unit + half * height for half in (1 - mine, mine) for group in groups]
         else:
-            lefts.append(())
-        tiles = []
-        place = sum(term[8] for term in terms[:at]) * 2
-        for tile in range(0, width, rows):
-            size = min(rows, width - tile)
-            spots = [right_raw.at[pl.ds(place + 2 * tile + side * size, size)] for side in (0, 1)]
-            tiles.append((tile, size, spots, [load(side, row + tile, spot) for side, spot in zip((near, far), spots)]))
-        rights.append(tiles)
-    stores = []
-
-    def store(begin, width):
-        for half, target in enumerate((send_hbm, keep_hbm)):
-            copy = pltpu.make_async_copy(
-                result_ref.at[pl.ds(half * total // 2, total // 2), pl.ds(begin, width)],
-                target.at[:, pl.ds(begin, width)],
-                store_sem.at[len(stores)],
-            )
-            copy.start()
-            stores.append(copy)
-
-    for at, (_, _, _, _, _, _, _, kind, _, begin) in enumerate(terms):
-        for copy in lefts[at]:
-            copy.wait()
-        if kind == "sum":
-            for _, _, _, copies in rights[at]:
+            height, mine = unit, place_ref[1]
+            starts = [(stride * side + across * other) * unit for side in (1 - mine, mine) for other in (0, 1)]
+        out_tile = 0
+
+        def store(count):
+            for half in (0, 1):
+                copy = pltpu.make_async_copy(
+                    result_ref.at[pl.ds(tile_at, count), pl.ds(half * total // 2, total // 2)],
+                    outputs[2 * order + half].at[pl.ds(out_tile, count)],
+                    store_sem.at[len(stores)],
+                )
+                copy.start()
+                stores.append(copy)
+
+        held = None
+        for own, own_row, other, other_row, _, _, _, kind, width in terms:
+            tiles = rights[number]
+            number += 1
+            if kind == "sum":
+                for _, spots, copies in tiles:
+                    for copy in copies:
+                        copy.wait()
+                both = tiles[0][1][0][...] + tiles[0][1][1][...]
+                lanes = jnp.concatenate([both[part : part + 8, :] for part in range(0, width, 8)], axis=1)
+                tall = jnp.concatenate([lanes, jnp.zeros((BLOCK - 8, lanes.shape[1]), jnp.float32)], axis=0).T
+                unit_rows = tall.reshape(UNITS // 2, 2, unit, BLOCK)
+                spare = left_raw.at[left_raw.shape[0] - 1]
+                spare[:, :BLOCK] = jnp.where(place_ref[0] == 0, unit_rows[:, 0], unit_rows[:, 1]).reshape(total, BLOCK)
+                for slot, first in enumerate(starts):
+                    result_ref[tile_at, slot * height : (slot + 1) * height, :] = spare[
+                        pl.ds(pl.multiple_of(first, 16), height), :BLOCK
+                    ]
+                store(1)
+                tile_at += 1
+                out_tile += 1
+                continue
+            at, copies = lefts[(own, own_row, other, other_row)]
+            if at not in waited:
+                waited.add(at)
                 for copy in copies:
                     copy.wait()
-            place = sum(term[8] for term in terms[:at]) * 2
-            height_in = terms[at][8]
-            both = right_raw[place : place + height_in, :] + right_raw[place + height_in : place + 2 * height_in, :]
-            lanes = jnp.concatenate([both[part : part + 8, :] for part in range(0, height_in, 8)], axis=1)
-            tall = jnp.concatenate([lanes, jnp.zeros((BLOCK - 8, lanes.shape[1]), jnp.float32)], axis=0).T
-            unit_rows = tall.reshape(UNITS // 2, 2, unit, BLOCK)
-            mine_rows = jnp.where(place_ref[0] == 0, unit_rows[:, 0], unit_rows[:, 1]).reshape(total, BLOCK)
-            left_raw[0, :, :BLOCK] = mine_rows
-            for slot, first in enumerate(starts):
-                result_ref[slot * height : (slot + 1) * height, begin : begin + BLOCK] = left_raw[
-                    0, pl.ds(pl.multiple_of(first, 16), height), :BLOCK
-                ]
-            store(begin, BLOCK)
-            continue
-        for slot, first in enumerate(starts):
-            first = pl.multiple_of(first, 16)
-            span = slice(slot * height, (slot + 1) * height)
-            for side in (0, 1):
-                left_ref[span, side * rows : (side + 1) * rows] = left_raw[2 * at + side, pl.ds(first, height), :].astype(
-                    jnp.bfloat16
-                )
-        left = left_ref[...]
-        for tile, size, spots, copies in rights[at]:
-            for copy in copies:
-                copy.wait()
-            near, far = (spot[...].astype(jnp.bfloat16) for spot in spots)
-            if kind == "tiles":
-                result = dot_plain(left, jnp.concatenate([near, far], axis=0))
-            else:
-                right = jnp.concatenate([near, far], axis=1)
-                if kind != "turned":
-                    blank = jnp.zeros_like(right)
-                    right = jnp.concatenate((right, blank) if kind == "low" else (blank, right), axis=0)
-                result = dot_over(left, right, 1, 1)
-            span = slice(begin + tile, begin + tile + result.shape[1])
-            if kind == "high":
-                result_ref[:, span] += result
-            else:
-                result_ref[:, span] = result
-            if kind != "low":
-                store(begin + tile, result.shape[1])
+            if held != at:
+                held = at
+                for slot, first in enumerate(starts):
+                    first = pl.multiple_of(first, 16)
+                    span = slice(slot * height, (slot + 1) * height)
+                    for side in (0, 1):
+                        left_ref[order % 2, span, side * rows : (side + 1) * rows] = left_raw[
+                            2 * at + side, pl.ds(first, height), :
+                        ].astype(jnp.bfloat16)
+            left = left_ref[order % 2]
+            for size, spots, copies in tiles:
+                for copy in copies:
+                    copy.wait()
+                near, far = (spot[...].astype(jnp.bfloat16) for spot in spots)
+                if kind == "tiles":
+                    result = dot_plain(left, jnp.concatenate([near, far], axis=0))
+                else:
+                    right = jnp.concatenate([near, far], axis=1)
+                    if kind != "turned":
+                        blank = jnp.zeros_like(right)
+                        right = jnp.concatenate((right, blank) if kind == "low" else (blank, right), axis=0)
+                    result = dot_over(left, right, 1, 1)
+                count = result.shape[1] // BLOCK
+                for part in range(count):
+                    piece = result[:, part * BLOCK : (part + 1) * BLOCK]
+                    if kind == "high":
+                        result_ref[tile_at + part] += piece
+                    else:
+                        result_ref[tile_at + part] = piece
+                if kind != "low":
+                    store(count)
+                    tile_at += count
+                    out_tile += count
     for copy in stores:
         copy.wait()
 
 
-def weight_gradient(token, place, axis, arrays, terms, unit, columns):
+def tiles_of(terms):
+    widths = {"low": 0, "high": BLOCK, "sum": BLOCK}
+    return sum(widths.get(term[7], term[8]) for term in terms) // BLOCK
+
+
+def weight_gradient(token, place, arrays, pieces, unit, cost):
     rows = arrays[0].shape[1]
     total = 4 * unit
     hbm = pl.BlockSpec(memory_space=pl.ANY)
     vmem = pl.BlockSpec(memory_space=pltpu.VMEM)
-    out_type = jax.ShapeDtypeStruct((total // 2, columns), jnp.float32)
-    widths = sum(term[8] for term in terms)
-    copies = sum(2 + 2 * (-(-term[8] // rows)) for term in terms)
-    return pl.pallas_call(
-        functools.partial(
-            gradient_kernel, terms=terms, arrays=len(arrays), unit=unit, axis=axis, columns=columns
-        ),
+    counts = [tiles_of(terms) for _, terms in pieces]
+    every = [term for _, terms in pieces for term in terms]
+    lefts = len({term[:4] for term in every if term[7] != "sum"})
+    copies = 2 * lefts + sum(2 * (-(-term[8] // rows)) for term in every)
+    shapes = [jax.ShapeDtypeStruct((count, total // 2, BLOCK), jnp.float32) for count in counts for _ in (0, 1)]
+    results = pl.pallas_call(
+        functools.partial(gradient_kernel, pieces=pieces, arrays=len(arrays), unit=unit),
         in_specs=[pl.BlockSpec(memory_space=pltpu.SMEM)] + [hbm] * (len(arrays) + 1),
-        out_specs=[vmem, hbm, hbm],
+        out_specs=[vmem] + [hbm] * len(shapes),
         scratch_shapes=[
-            pltpu.VMEM((total, columns), jnp.float32),
-            pltpu.VMEM((2 * len(terms), total, rows), jnp.float32),
-            pltpu.VMEM((total, 2 * rows), jnp.bfloat16),
-            pltpu.VMEM((2 * widths, rows), jnp.float32),
+            pltpu.VMEM((sum(counts), total, BLOCK), jnp.float32),
+            pltpu.VMEM((2 * lefts + 1, total, rows), jnp.float32),
+            pltpu.VMEM((2, total, 2 * rows), jnp.bfloat16),
+            pltpu.VMEM((2 * sum(term[8] for term in every), rows), jnp.float32),
             pltpu.SemaphoreType.DMA((copies,)),
             pltpu.SemaphoreType.DMA((copies,)),
         ],
-        out_shape=[TOKEN, out_type, out_type],
-        compiler_params=pltpu.CompilerParams(vmem_limit_bytes=16 * 1024 * 1024),
-        cost_estimate=COST(4.0),
+        out_shape=[TOKEN] + shapes,
+        compiler_params=pltpu.CompilerParams(vmem_limit_bytes=VMEM_GRADIENT * 1024 * 1024),
+        cost_estimate=expect(cost),
     )(place, *arrays, token)
-
-
-def part_kernel(place_ref, *refs, inputs, parts):
-    token_ref, outputs = refs[inputs + 1], refs[inputs + 2 :]
-    step = pl.program_id(0)
-
-    @pl.when(jnp.logical_and(step == 0, pl.program_id(1) == 0))
-    def _():
-        token_ref[...] = jnp.zeros_like(token_ref)
-
-    for at in range(parts):
-
-        @pl.when(step == at)
-        def _(at=at):
-            total = refs[0][...]
-            for ref in refs[1:inputs]:
-                total = total + ref[...]
-            outputs[at][...] = total
-
-
-def add_parts(token, place, arrays, parts, which):
-    before, _, after, columns = arrays[0].shape
-    tiles = 1
-    while after % (2 * tiles) == 0 and (after // (2 * tiles)) % 8 == 0 and before * after * columns * 4 // tiles > TILE_BYTES:
-        tiles *= 2
-    height = after // tiles
-
-    def index_in(step, tile, place_ref):
-        mine = place_ref[which] & (parts - 1)
-        chosen = mine ^ ((step + 1) & (parts - 1))
-        return (0, chosen, tile, 0)
-
-    def index_out(step, tile, place_ref, at):
-        return (0, jnp.where(step == at, tile, jnp.where(step < at, 0, tiles - 1)), 0)
-
-    block_in = pl.BlockSpec((before, None, height, columns), index_in)
-    blocks_out = [
-        pl.BlockSpec((before, height, columns), functools.partial(index_out, at=at)) for at in range(parts)
-    ]
-    result = jax.ShapeDtypeStruct((before, after, columns), jnp.float32)
-    return pl.pallas_call(
-        functools.partial(part_kernel, inputs=len(arrays), parts=parts),
-        grid_spec=pltpu.PrefetchScalarGridSpec(
-            num_scalar_prefetch=1,
-            grid=(parts, tiles),
-            in_specs=[block_in] * len(arrays) + [pl.BlockSpec(memory_space=pl.ANY)],
-            out_specs=[pl.BlockSpec(TOKEN.shape, lambda i, t, s: (0, 0))] + blocks_out,
+    return results[0], [results[1 + 2 * at : 3 + 2 * at] for at in range(len(pieces))]
+
+
+def combine_kernel(place_ref, *refs, inputs, parts, which, last, spread, passed):
+    total = sum(inputs)
+    sources = refs[:total]
+    token_ref = refs[total + 1]
+    results = refs[total + 2 : total + 2 + (len(inputs) if last else 1 if spread else parts)]
+    scratch = refs[total + 2 + len(results) :]
+    raws, sums, load_sem, store_sem = scratch[:total], scratch[total], scratch[total + 1], scratch[total + 2]
+    token_ref[...] = jnp.zeros_like(token_ref)
+    mine = place_ref[which] & (parts - 1)
+    chosen = [step if spread else mine ^ ((step + 1) & (parts - 1)) for step in range(parts)]
+    loads, stores = {}, []
+    for step in range(parts):
+        for at in range(total):
+            copy = pltpu.make_async_copy(
+                sources[at].at[:, :, chosen[step]], raws[at].at[step], load_sem.at[step * total + at]
+            )
+            copy.start()
+            loads[step, at] = copy
+    for step in range(parts):
+        first = 0
+        begin = 0
+        for group, count in enumerate(inputs):
+            for at in range(first, first + count):
+                loads[step, at].wait()
+            value = raws[first][step]
+            for at in range(first + 1, first + count):
+                if passed:
+                    outside = jnp.logical_or(place_ref[3] == 0, place_ref[3] == 3)
+                    value = jnp.where(outside, value, raws[at][step])
+                else:
+                    value = value + raws[at][step]
+            tiles = value.shape[0]
+            if last:
+                fold = tiles // (results[group].shape[1] // BLOCK)
+                tiles //= fold
+                for tile in range(tiles):
+                    piece = value[tile, 0]
+                    for part in range(1, fold):
+                        piece = piece + value[part * tiles + tile, 0]
+                    results[group][:, tile * BLOCK : (tile + 1) * BLOCK] = piece
+            else:
+                sums[step, begin : begin + tiles] = value
+                copy = pltpu.make_async_copy(
+                    sums.at[step, pl.ds(begin, tiles)],
+                    results[0].at[step, pl.ds(begin, tiles)] if spread else results[step].at[pl.ds(begin, tiles)],
+                    store_sem.at[len(stores)],
+                )
+                copy.start()
+                stores.append(copy)
+            begin += tiles
+            first += count
+    for copy in stores:
+        copy.wait()
+
+
+def combine(token, place, groups, before, parts, which, cost, last=False, spread=False, fold=1, passed=False):
+    rows = groups[0][0].shape[1]
+    after = rows // (before * parts)
+    flat = [array.reshape(array.shape[0], before, parts, after, BLOCK) for group in groups for array in group]
+    tiles = [group[0].shape[0] for group in groups]
+    hbm = pl.BlockSpec(memory_space=pl.ANY)
+    vmem = pl.BlockSpec(memory_space=pltpu.VMEM)
+    shape = jax.ShapeDtypeStruct
+    if last:
+        shapes = [shape((rows, count // fold * BLOCK), jnp.float32) for count in tiles]
+    elif spread:
+        shapes = [shape((parts, sum(tiles), before, after, BLOCK), jnp.float32)]
+    else:
+        shapes = [shape((sum(tiles), before, after, BLOCK), jnp.float32)] * parts
+    results = pl.pallas_call(
+        functools.partial(
+            combine_kernel, inputs=tuple(len(group) for group in groups), parts=parts, which=which, last=last, spread=spread, passed=passed
         ),
-        out_shape=[TOKEN] + [result] * parts,
-        compiler_params=pltpu.CompilerParams(vmem_limit_bytes=8 * 1024 * 1024),
-        cost_estimate=COST(1.5),
-    )(place, *arrays, token)
+        in_specs=[pl.BlockSpec(memory_space=pltpu.SMEM)] + [hbm] * (len(flat) + 1),
+        out_specs=[vmem] + [vmem if last else hbm] * len(shapes),
+        scratch_shapes=[pltpu.VMEM((parts, array.shape[0], before, after, BLOCK), jnp.float32) for array in flat]
+        + [
+            pltpu.VMEM((1,) * 5 if last else (parts, sum(tiles), before, after, BLOCK), jnp.float32),
+            pltpu.SemaphoreType.DMA((parts * len(flat),)),
+            pltpu.SemaphoreType.DMA((parts * len(groups),)),
+        ],
+        out_shape=[TOKEN] + shapes,
+        compiler_params=pltpu.CompilerParams(vmem_limit_bytes=VMEM_COMBINE * 1024 * 1024),
+        cost_estimate=expect(cost),
+    )(place, *flat, token)
+    if last or spread:
+        return results[0], results[1:]
+    return results[0], [result.reshape(sum(tiles), before * after, BLOCK) for result in results[1:]]
 
 
 class Layout:
@@ -923,8 +1023,8 @@
         return [(i, i ^ bit) for i in range(self.total)]
 
     def middle(self):
-        swapped = (0, 2, 1, 3)
-        return [(i, (i & ~3) | swapped[i & 3]) for i in range(self.total)]
+        swapped = {1: 2, 2: 1}
+        return [(i, (i & ~3) | swapped[i & 3] if i & 3 in swapped else i ^ 4) for i in range(self.total)]
 
     def across(self, first):
         return [(i, i ^ (8 if (i & 4 == 0) == first else 16)) for i in range(self.total)]
@@ -938,61 +1038,62 @@
         return jnp.stack(places).astype(jnp.int32)
 
 
-class Piece:
-    def __init__(self, layout, place, order, arrays, terms, unit, columns):
-        self.layout, self.place, self.order = layout, place, order
-        self.arrays, self.terms, self.unit, self.columns = arrays, terms, unit, columns
-        self.plan = []
-        for axis in order:
-            self.plan += ["half", "middle", "part"] if axis == "z" else [axis]
-        self.axes = ["b", "a", "half", "part"]
-        self.held = None
-        self.result = None
-
-    def move(self, array, step):
-        layout = self.layout
+class Bundle:
+    def __init__(self, names, plan, axes, groups, fold=1, passed=False):
+        self.names, self.plan, self.axes, self.groups = names, plan, axes, groups
+        self.fold, self.passed = fold, passed
+
+
+def steps_of(order):
+    plan = []
+    for axis in order:
+        plan += ["half", "middle", "part"] if axis == "z" else [axis]
+    return plan
+
+
+def move(layout, array, step):
+    if step == "middle":
+        pairs = layout.middle()
+    else:
         pairs = layout.across(step == "a") if step in ("a", "b") else layout.flip(1)
-        return lax.ppermute(array, AXES, pairs)
-
-    def advance(self, token):
-        rows = self.unit // 4
-        if self.held is None:
-            step = self.plan.pop(0)
-            token, send, keep = weight_gradient(
-                token, self.place, self.order[0], self.arrays, self.terms, self.unit, self.columns
-            )
-            self.axes.remove({"a": "a", "z": "half"}.get(step, step))
-            self.held = [keep, self.move(send, step)]
-            return token
-        dims = [2] * len(self.axes)
-        if not self.plan:
-            shaped = [array.reshape(1, 1, rows, self.columns) for array in self.held]
-            token, whole = add_parts(token, self.place, shaped, 1, 0)
-            self.result = whole.reshape(rows, self.columns)
-            return token
-        step = self.plan.pop(0)
-        if step == "middle":
-            size = math.prod(dims) * rows
-            shaped = [array.reshape(1, 1, size, self.columns) for array in self.held]
-            token, whole = add_parts(token, self.place, shaped, 1, 0)
-            self.held = [lax.ppermute(whole, AXES, self.layout.middle())]
-        elif step == "Y":
-            at = self.axes.index("half")
-            before, after = math.prod(dims[:at]), math.prod(dims[at + 2 :]) * rows
-            shaped = [array.reshape(1, 1, before * 4 * after, self.columns) for array in self.held]
-            token, whole = add_parts(token, self.place, shaped, 1, 0)
-            whole = whole.reshape(before, 4, after, self.columns)
-            got = lax.all_to_all(whole, "narrow", 1, 1, tiled=True)
-            self.axes = [axis for axis in self.axes if axis not in ("half", "part")]
-            self.held = [got[:, at] for at in range(4)]
-        else:
-            at = self.axes.index(step)
-            before, after = math.prod(dims[:at]), math.prod(dims[at + 1 :]) * rows
-            shaped = [array.reshape(before, 2, after, self.columns) for array in self.held]
-            token, send, keep = add_parts(token, self.place, shaped, 2, {"a": 1, "b": 2}.get(step, 3))
-            self.held = [keep, self.move(send, step)]
-            self.axes.remove(step)
-        return token
+    return lax.ppermute(array, AXES, pairs)
+
+
+def start_bundles(layout, token, place, arrays, names, terms, unit, cost):
+    plans = [steps_of(ORDERS[name]) for name in names]
+    token, results = weight_gradient(
+        token, place, arrays, tuple((ORDERS[name][0], terms[name]) for name in names), unit, cost
+    )
+    bundles = {}
+    for name, plan, (send, keep) in zip(names, plans, results):
+        step = plan.pop(0)
+        axes = [axis for axis in ("b", "a", "half", "part") if axis != step]
+        bundles[name] = Bundle([name], plan, axes, [[keep, move(layout, send, step)]])
+    return token, bundles
+
+
+def advance(layout, token, place, bundles, rows, cost, finished):
+    plan, axes = bundles[0].plan, bundles[0].axes
+    groups = [group for bundle in bundles for group in bundle.groups]
+    names = [name for bundle in bundles for name in bundle.names]
+    sizes = [group[0].shape[0] for group in groups]
+    if not plan:
+        token, results = combine(token, place, groups, 1, 1, 0, cost, last=True, fold=bundles[0].fold)
+        wide = results[0] if len(results) == 1 else jnp.concatenate(results, axis=1)
+        finished.append((names, wide))
+        return token, None
+    step, plan = plan[0], plan[1:]
+    if step == "middle":
+        token, (whole,) = combine(token, place, groups, 1, 1, 0, cost)
+        return token, Bundle(names, plan, axes, [[whole, move(layout, whole, step)]], passed=True)
+    if step == "Y":
+        token, (whole,) = combine(token, place, groups, 1, 4, 0, cost, spread=True)
+        got = lax.all_to_all(whole, "narrow", 0, 0, tiled=True)
+        return token, Bundle(names, plan, [], [[got.reshape(4 * sum(sizes), rows, BLOCK)]], 4)
+    at = axes.index(step)
+    which = {"a": 1, "b": 2}.get(step, 3)
+    token, (send, keep) = combine(token, place, groups, 2**at, 2, which, cost, passed=bundles[0].passed)
+    return token, Bundle(names, plan, [axis for axis in axes if axis != step], [[keep, move(layout, send, step)]])
 
 
 def whole_rows(own, other):
@@ -1057,11 +1158,11 @@
         soon,
         later,
         rest,
-    ) = front(place, lengths, series, flags, cotangent.reshape(rows, horizon), tables, weights, HEADS)
+    ) = front(place, lengths, series, flags, cotangent.reshape(rows, horizon), tables, weights, HEADS, PROGRAM[0][2])
     across = lift_weight.shape[0]
     joint_width = joint_weight.shape[1]
 
-    def run_back(token):
+    def run_back(token, cost):
         return back(
             token,
             place,
@@ -1072,6 +1173,7 @@
             (lift_weight, mix_weight, skip_weight, gain_first, joint_weight, merge_weight),
             (tokens, logsum, sigma_sum, center_sum, second_sum, embedded, middle, turned),
             HEADS,
+            cost,
         )
 
     at_own = {name: place * half for place, name in enumerate(OWN)}
@@ -1082,63 +1184,68 @@
         swap = lambda array: lax.ppermute(array, AXES, layout.flip(4))
         unit = width // UNITS
         soon_got, later_got, rest_got = swap(soon), swap(later), swap(rest)
-        pieces = {}
-
-        def piece(name, arrays, terms, columns):
-            pieces[name] = Piece(layout, place, ORDERS[name], arrays, terms, unit, columns)
-
-        piece("A", [own, soon, soon_got], ((0, at_own["branch"], 2, 0, 1, 2, half, "tiles", hidden, 0),), hidden)
-        piece(
-            "B",
-            [own, later, later_got],
-            (
-                (0, at_own["normed_two"], 2, at_later["normed_two"], 1, 2, at_later["upper"], "tiles", hidden, 0),
-                (0, at_own["resid"], 2, at_later["resid"], 1, 2, at_later["head"], "turned", horizon, hidden),
+        terms = {
+            "A": ((0, at_own["branch"], 2, 0, 1, 2, half, "tiles", hidden),),
+            "B": (
+                (0, at_own["normed_two"], 4, at_later["normed_two"], 3, 4, at_later["upper"], "tiles", hidden),
+                (0, at_own["resid"], 4, at_later["resid"], 3, 4, at_later["head"], "turned", horizon),
             ),
-            hidden + horizon,
-        )
-        piece(
-            "C",
-            [own, rest, rest_got],
-            ((0, at_own["mixed"], 2, at_rest["mixed"], 1, 2, at_rest["middle"], "tiles", width, 0),),
-            width,
-        )
+            "C": ((0, at_own["mixed"], 6, at_rest["mixed"], 5, 6, at_rest["middle"], "tiles", width),),
+            "E": (
+                (0, at_own["hidden"], 6, at_rest["hidden"], 9, 10, at_last["embed_tiles"], "tiles", width),
+                (11, half, 10, at_last["pre"], 9, 10, at_last["tokens"], "low", across),
+                (11, 0, 10, at_last["embed"], 9, 10, at_last["tokens"], "high", across),
+                (0, 0, 0, 0, 9, 10, at_last["sums"], "sum", 8 * width // rows),
+            ),
+        }
         joint_names = [name for name in ORDERS if name.startswith("D")]
-        for name in PROGRAM:
-            if name == "K":
-                token, series_grad, joint, last, last_own = run_back(token)
-                joint_got, last_got = swap(joint), swap(last)
-                span = joint_width // len(joint_names)
-                for at, joint_name in enumerate(joint_names):
-                    piece(
-                        joint_name,
-                        [own, rest_got, joint, joint_got],
-                        ((0, at_own["normed_one"], 1, at_rest["normed_one"], 2, 3, at * span, "turned", span, 0),),
-                        span,
+        first = 0
+        for name in joint_names:
+            span = JOINT_TILES[name] * BLOCK
+            terms[name] = ((0, at_own["normed_one"], 6, at_rest["normed_one"], 7, 8, first, "turned", span),)
+            first += span
+        arrays = [own, soon, soon_got, later, later_got, rest, rest_got]
+        bundles, finished = {}, []
+        for kind, names, cost in PROGRAM[1:]:
+            if kind == "K":
+                token, series_grad, joint, last, last_own = run_back(token, cost)
+                arrays += [joint, swap(joint), last, swap(last), last_own]
+            elif kind == "G":
+                used = sorted({index for name in names for term in terms[name] for index in (term[0], *term[2:3], *term[4:6])})
+                local = {
+                    name: tuple(
+                        (used.index(t[0]), t[1], used.index(t[2]), t[3], used.index(t[4]), used.index(t[5]), *t[6:])
+                        for t in terms[name]
                     )
-                piece(
-                    "E",
-                    [own, rest_got, last, last_got, last_own],
-                    (
-                        (0, at_own["hidden"], 1, at_rest["hidden"], 2, 3, at_last["embed_tiles"], "tiles", width, 0),
-                        (4, half, 3, at_last["pre"], 2, 3, at_last["tokens"], "low", across, width),
-                        (4, 0, 3, at_last["embed"], 2, 3, at_last["tokens"], "high", across, width),
-                        (0, 0, 0, 0, 2, 3, at_last["sums"], "sum", 8 * width // rows, width + 2 * across),
-                    ),
-                    width + 2 * across + BLOCK,
+                    for name in names
+                }
+                token, fresh = start_bundles(
+                    layout, token, place, [arrays[index] for index in used], names, local, unit, cost
                 )
+                bundles.update(fresh)
             else:
-                token = pieces[name].advance(token)
-        shrink_rows, grow_head, merge_grad, mix_small = (pieces[name].result for name in "ABCE")
-        grow_grad, head_grad = grow_head[:, :hidden], grow_head[:, hidden:]
-        joint_grad = jnp.concatenate([pieces[name].result for name in joint_names], axis=1)
+                token, joined = advance(
+                    layout, token, place, [bundles.pop(name) for name in names], unit // 4, cost, finished
+                )
+                bundles["".join(names)] = joined
+        columns = {}
+        for names, wide in finished:
+            begin = 0
+            for name in names:
+                span = tiles_of(terms[name]) * BLOCK
+                columns[name] = wide[:, begin : begin + span]
+                begin += span
+        shrink_rows, merge_grad = columns["A"], columns["C"]
+        grow_grad, head_grad = columns["B"][:, :hidden], columns["B"][:, hidden:]
+        joint_grad = jnp.concatenate([columns[name] for name in joint_names], axis=1)
+        mix_small = columns["E"]
         mix_grad = mix_small[:, :width]
         lift_rows = mix_small[:, width : width + across]
         skip_rows = mix_small[:, width + across : width + 2 * across]
         second_grad = mix_small[:, width + 2 * across]
         first_grad = mix_small[:, width + 2 * across + 1]
     else:
-        _, series_grad, joint, last, last_own = run_back(token)
+        _, series_grad, joint, last, last_own = run_back(token, 1.0)
         scatter = lambda left, right: lax.psum_scatter(
             dot_plain(left.astype(jnp.bfloat16), right.astype(jnp.bfloat16)), AXES, scatter_dimension=0, tiled=True
         )

time: 275 us -> 262 us (0.953)
  waiting for transfers between devices: 65.3 us -> 38.8 us
  Pallas kernels: 120 us -> 137 us
  starting transfers between devices: 68.3 us -> 59.5 us
  local copies, waits for them, and re-layouts: 11.9 us -> 19.2 us
    ppermute x28 -> x27, waiting for transfers between devices: 61.9 us -> 33.1 us  [move(): return lax.ppermute(array, AXES, pairs)]
    pallas_call x42 -> x34, Pallas kernels: 75.7 us -> 93.2 us  [the longest x28 50.9 us: combine(): pl.pallas_call(functools.partial(combine_kernel, inputs=tuple((len(group)...]
    ppermute x7 -> x0, starting transfers between devices: 12.1 us -> none  [advance(): self.held = [lax.ppermute(whole, AXES, self.layout.middle())]]
    unnamed x32 -> x54, local copies, waits for them, and re-layouts: 8.52 us -> 15.8 us
    all_to_all x0 -> x1, starting transfers between devices: none -> 3.76 us  [advance(): got = lax.all_to_all(whole, 'narrow', 0, 0, tiled=True)]
    ppermute x28 -> x27, starting transfers between devices: 54.6 us -> 54.1 us  [move(): return lax.ppermute(array, AXES, pairs)]
  transfers between devices with their start and end apart: 40 -> 33, of which waited for: 16 -> 11; matrix products, arithmetic and copies ran while one was open for 1% -> 1% of each run, Pallas kernels for 36% -> 44%
where the time goes in v4:
time: 262 us; the launch traced here: 257 us
  Pallas kernels  137 us (52%)
  starting transfers between devices  59.5 us (23%)
  waiting for transfers between devices  38.8 us (15%)
  local copies, waits for them, and re-layouts  19.2 us (7%)
    ppermute x27, starting transfers between devices, move(): return lax.ppermute(array, AXES, pairs)  54.1 us
    pallas_call x28, Pallas kernels, combine(): pl.pallas_call(functools.partial(combine_kernel, inputs=tuple((len(group)...  50.9 us
    pallas_call x6, Pallas kernels, weight_gradient(): pl.pallas_call(functools.partial(gradient_kernel, pieces=pieces, arrays=l...  42.3 us
    ppermute x27, waiting for transfers between devices, move(): return lax.ppermute(array, AXES, pairs)  33.1 us
    pallas_call x1, Pallas kernels, front(): pl.pallas_call(functools.partial(front_kernel, heads), out_shape=outs, in...  22.3 us
    pallas_call x1, Pallas kernels, back(): pl.pallas_call(functools.partial(back_kernel, heads), out_shape=[TOKEN, s...  21.1 us
    unnamed x54, local copies, waits for them, and re-layouts  15.8 us
    ppermute x5, waiting for transfers between devices, per_device(): swap = lambda array: lax.ppermute(array, AXES, layout.flip(4))  5.66 us
  transfers between devices with their start and end apart: 33, of which 11 were waited for; matrix products, arithmetic and copies ran while one was open for 1% of the time, Pallas kernels for 44%

profile of v4, /device:TPU:0, one launch (start us, length us, event | category | flops | bytes accessed | tf_op | source)
XLA Modules:
  0.0 257.2 jit_solution(3934135499950494681)
XLA Ops:
  1.3 22.3 %shard_map.247 = (f32[8,128]{1,0:T(8,128)}, f32[256,128]{1,0:T(8,128)}, bf16[256,64]{1,0:T(8,128)(2,1)}, f32[16,256]{1,0:T(8,128)}, f32[16,128]{1,0:T(8,128)}, /...) custom-call(s32[16]{0:T(128)} %lengths_ref.3, ...), custom_call_target="tpu_custom_call" | custom-call | flops 20700000256 | tf_op jit(solution)/shard_map/pallas_call | solution.py:498
  24.7 5.3 %collective-permute-done.2.refs_2_ = f32[1920,256]{1,0:T(8,128)S(1)} collective-permute-done((f32[1920,256]{1,0:T(8,128)}, f32[1920,256]{1,0:T(8,128)S(1)}, u32[]{:S(2)}, u32[]{:S(2)}) %collective-permute-start.2) | collective-permute-done | bytes 1966112 | tf_op jit(solution)/shard_map/ppermute | solution.py:1184
  30.0 1.3 copy-done.26
  31.3 6.0 %shard_map.248 = (f32[8,128]{1,0:T(8,128)}, f32[10,320,128]{2,1,0:T(8,128)}, f32[10,320,128]{2,1,0:T(8,128)}) custom-call(s32[4]{0:T(128)} %pad_add_fusion.place_ref, f32[3840,256]{1,0:T(8,128)} %get-tuple-element.129.refs_0_, f32[1920,256]{1,0:T(8,128)} %get-tuple-element.132.refs_1_, f32[1920,256]{1,0:T(8,128)} %copy-done.26, ...), custom_call_target="tpu_custom_call" | custom-call | flops 13799999488 | tf_op jit(solution)/shard_map/pallas_call | solution.py:906
  37.3 2.9 %collective-permute-start.5 = (f32[10,320,128]{2,1,0:T(8,128)}, f32[10,320,128]{2,1,0:T(8,128)S(1)}, u32[]{:S(2)}, u32[]{:S(2)}) collective-permute-start(f32[10,320,128]{2,1,0:T(8,128)} %get-tuple-element.143), channel_id=1, source_target_pairs={{0,8},{1,9},{2,10},{3,11},{4,20},{5,21},{6,22},{7,23},{8,0},{9,1},... | collective-permute-start | bytes 4915208 | tf_op jit(solution)/shard_map/ppermute | solution.py:1059
  40.3 6.7 %shard_map.249 = (f32[8,128]{1,0:T(8,128)}, f32[11,320,128]{2,1,0:T(8,128)}, f32[11,320,128]{2,1,0:T(8,128)}) custom-call(s32[4]{0:T(128)} %pad_add_fusion.place_ref, f32[3840,256]{1,0:T(8,128)} %get-tuple-element.129.refs_0_, f32[2688,256]{1,0:T(8,128)} %get-tuple-element.131.refs_1_, f32[2688,256]{1,0:T(8,128)} %collective-permute-done.1.refs_2_, ...), custom_call_target="tpu_custom_call" | custom-call | flops 28750000128 | tf_op jit(solution)/shard_map/pallas_call | solution.py:906
  47.0 6.1 %shard_map.250 = (f32[8,128]{1,0:T(8,128)}, f32[10,320,128]{2,1,0:T(8,128)}, f32[10,320,128]{2,1,0:T(8,128)}) custom-call(s32[4]{0:T(128)} %pad_add_fusion.place_ref, f32[3840,256]{1,0:T(8,128)} %get-tuple-element.129.refs_0_, f32[3200,256]{1,0:T(8,128)} %get-tuple-element.130.refs_1_, f32[3200,256]{1,0:T(8,128)} %collective-permute-done.refs_2_.refs_1_, ...), custom_call_target="tpu_custom_call" | custom-call | flops 46000001024 | tf_op jit(solution)/shard_map/pallas_call | solution.py:906
  53.2 2.1 collective-permute-start.9
  55.3 21.1 %shard_map.251 = (f32[8,128]{1,0:T(8,128)}, f32[16,512]{1,0:T(8,128)}, f32[3840,256]{1,0:T(8,128)}, f32[2664,256]{1,0:T(8,128)}, f32[1280,256]{1,0:T(8,128)}) custom-call(s32[16]{0:T(128)} %lengths_ref.3, s32[4]{0:T(128)} %pad_add_fusion.place_ref, f32[16,512]{1,0:T(8,128)} %series_ref.3, s32[16,512]{1,0:T(8,128)} %flags_ref.3, f32[1280]{0:T(1024)} %gain_first_ref.3, ...), custom_call_target="tpu_custom_call" | custom-call | flops 1150000000 | tf_op jit(solution)/shard_map/pallas_call | solution.py:740
  77.6 1.4 copy-done.15
  79.1 1.3 shard_map.252
  81.2 1.5 collective-permute-start.8
  82.8 2.3 shard_map.253
  87.3 2.0 copy-done.25
  89.3 8.0 %shard_map.254 = (f32[8,128]{1,0:T(8,128)}, f32[15,320,128]{2,1,0:T(8,128)}, f32[15,320,128]{2,1,0:T(8,128)}) custom-call(s32[4]{0:T(128)} %pad_add_fusion.place_ref, f32[3840,256]{1,0:T(8,128)} %get-tuple-element.129.refs_0_, f32[3200,256]{1,0:T(8,128)} %collective-permute-done.refs_2_.refs_1_, f32[3840,256]{1,0:T(8,128)} %get-tuple-element.148.refs_2_, ...), custom_call_target="tpu_custom_call" | custom-call | tf_op jit(solution)/shard_map/pallas_call | solution.py:906
  97.3 1.6 collective-permute-start.11
  99.5 1.5 copy-done.14
  101.0 3.8 %shard_map.255 = (f32[8,128]{1,0:T(8,128)S(1)}, f32[11,1,320,128]{3,2,1,0:T(8,128)}) custom-call(s32[4]{0:T(128)S(1)} %copy-done.1, f32[11,1,1,320,128]{4,3,2,1,0:T(8,128)S(1)} %bitcast.135, f32[11,1,1,320,128]{4,3,2,1,0:T(8,128)} %bitcast.17.refs_1_, f32[8,128]{1,0:T(8,128)S(1)} %copy-done.13), custom_call_target="tpu_custom_call" | custom-call | flops 9200000000 | tf_op jit(solution)/shard_map/pallas_call | solution.py:994
  105.0 2.1 shard_map.256
  107.7 8.0 %shard_map.257 = (f32[8,128]{1,0:T(8,128)}, f32[15,320,128]{2,1,0:T(8,128)}, f32[15,320,128]{2,1,0:T(8,128)}) custom-call(s32[4]{0:T(128)} %pad_add_fusion.place_ref, f32[3840,256]{1,0:T(8,128)} %get-tuple-element.129.refs_0_, f32[3200,256]{1,0:T(8,128)} %collective-permute-done.refs_2_.refs_1_, f32[3840,256]{1,0:T(8,128)} %get-tuple-element.148.refs_2_, ...), custom_call_target="tpu_custom_call" | custom-call | flops 3449999872 | tf_op jit(solution)/shard_map/pallas_call | solution.py:906
  115.7 1.4 collective-permute-start.13
  117.1 3.8 %all-to-all-start = ((f32[4,10,1,40,128]{4,3,2,1,0:T(8,128)}), f32[4,10,1,40,128]{4,3,2,1,0:T(8,128)S(1)}, u32[]{:S(2)}, u32[]{:S(2)}) async-start(f32[4,10,1,40,128]{4,3,2,1,0:T(8,128)} %get-tuple-element.166), calls=%async_computation | async-start | bytes 1638400 | tf_op jit(solution)/shard_map/all_to_all | solution.py:1091
  121.6 1.8 shard_map.258
  124.0 7.5 %shard_map.259 = (f32[8,128]{1,0:T(8,128)}, f32[12,320,128]{2,1,0:T(8,128)}, f32[12,320,128]{2,1,0:T(8,128)}) custom-call(s32[4]{0:T(128)} %pad_add_fusion.place_ref, f32[3840,256]{1,0:T(8,128)} %get-tuple-element.129.refs_0_, f32[3200,256]{1,0:T(8,128)} %collective-permute-done.refs_2_.refs_1_, f32[2664,256]{1,0:T(8,128)} %get-tuple-element.138.refs_2_, ...), custom_call_target="tpu_custom_call" | custom-call | tf_op jit(solution)/shard_map/pallas_call | solution.py:906
  131.5 1.5 collective-permute-start.10
  133.7 3.1 %shard_map.260 = (f32[8,128]{1,0:T(8,128)S(1)}, f32[15,2,80,128]{3,2,1,0:T(8,128)}, f32[15,2,80,128]{3,2,1,0:T(8,128)S(1)}) custom-call(s32[4]{0:T(128)S(1)} %copy-done.3, f32[15,2,2,80,128]{4,3,2,1,0:T(8,128)S(1)} %bitcast.98, f32[15,2,2,80,128]{4,3,2,1,0:T(8,128)} %bitcast.21.refs_1_, f32[8,128]{1,0:T(8,128)S(1)} %copy-done.12), custom_call_target="tpu_custom_call" | custom-call | flops 5750000128 | tf_op jit(solution)/shard_map/pallas_call | solution.py:994
  136.9 1.0 copy-done.17
  137.9 2.1 collective-permute-start.12
  140.0 3.3 %shard_map.261 = (f32[8,128]{1,0:T(8,128)S(1)}, f32[11,4,40,128]{3,2,1,0:T(8,128)}, f32[11,4,40,128]{3,2,1,0:T(8,128)S(1)}) custom-call(s32[4]{0:T(128)S(1)} %copy-done.3, f32[11,4,2,40,128]{4,3,2,1,0:T(8,128)} %bitcast.28.refs_0_, f32[11,4,2,40,128]{4,3,2,1,0:T(8,128)} %bitcast.30.refs_1_, f32[8,128]{1,0:T(8,128)S(1)} %get-tuple-element.170.refs_2_), custom_call_target="tpu_custom_call" | custom-call | flops 9200000000 | tf_op jit(solution)/shard_map/pallas_call | solution.py:994
  144.3 17.5 %collective-permute-start.19 = (f32[11,160,128]{2,1,0:T(8,128)}, f32[11,160,128]{2,1,0:T(8,128)}, u32[]{:S(2)}, u32[]{:S(2)}) collective-permute-start(f32[11,160,128]{2,1,0:T(8,128)} %bitcast.44), channel_id=1, source_target_pairs={{0,1},{1,0},{2,3},{3,2},{4,5},{5,4},{6,7},{7,6},{8,9},{9,8},{10,11... | collective-permute-start | bytes 2703368 | tf_op jit(solution)/shard_map/ppermute | solution.py:1059
  161.8 3.2 %shard_map.262 = (f32[8,128]{1,0:T(8,128)S(1)}, f32[15,1,160,128]{3,2,1,0:T(8,128)}, f32[15,1,160,128]{3,2,1,0:T(8,128)S(1)}) custom-call(s32[4]{0:T(128)S(1)} %copy-done.3, f32[15,1,2,160,128]{4,3,2,1,0:T(8,128)S(1)} %bitcast.99, f32[15,1,2,160,128]{4,3,2,1,0:T(8,128)} %bitcast.27.refs_1_, f32[8,128]{1,0:T(8,128)S(1)} %get-tuple-element.171.refs_2_), custom_call_target="tpu_custom_call" | custom-call | flops 3449999872 | tf_op jit(solution)/shard_map/pallas_call | solution.py:994
  165.0 1.6 collective-permute-start.18
  166.5 1.4 shard_map.263
  167.9 4.7 %collective-permute-done.12 = f32[15,160,128]{2,1,0:T(8,128)} collective-permute-done((f32[15,160,128]{2,1,0:T(8,128)}, f32[15,160,128]{2,1,0:T(8,128)}, u32[]{:S(2)}, u32[]{:S(2)}) %collective-permute-start.12) | collective-permute-done | bytes 1228832 | tf_op jit(solution)/shard_map/ppermute | solution.py:1059
  172.6 1.3 copy-done.18
  173.9 2.6 %shard_map.264 = (f32[8,128]{1,0:T(8,128)S(1)}, f32[15,1,160,128]{3,2,1,0:T(8,128)S(1)}) custom-call(s32[4]{0:T(128)S(1)} %copy-done.3, f32[15,1,1,160,128]{4,3,2,1,0:T(8,128)S(1)} %bitcast.138, f32[15,1,1,160,128]{4,3,2,1,0:T(8,128)} %bitcast.24.refs_1_, f32[8,128]{1,0:T(8,128)S(1)} %get-tuple-element.173.refs_2_), custom_call_target="tpu_custom_call" | custom-call | flops 3449999872 | tf_op jit(solution)/shard_map/pallas_call | solution.py:994
  176.5 6.8 %collective-permute-done.10 = f32[12,320,128]{2,1,0:T(8,128)} collective-permute-done((f32[12,320,128]{2,1,0:T(8,128)}, f32[12,320,128]{2,1,0:T(8,128)}, u32[]{:S(2)}, u32[]{:S(2)}) %collective-permute-start.10) | collective-permute-done | bytes 1966112 | tf_op jit(solution)/shard_map/ppermute | solution.py:1059
  183.3 2.7 %shard_map.265 = (f32[8,128]{1,0:T(8,128)S(1)}, f32[12,1,160,128]{3,2,1,0:T(8,128)S(1)}, f32[12,1,160,128]{3,2,1,0:T(8,128)S(1)}) custom-call(s32[4]{0:T(128)S(1)} %copy-done.3, f32[12,1,2,160,128]{4,3,2,1,0:T(8,128)S(1)} %bitcast.100, f32[12,1,2,160,128]{4,3,2,1,0:T(8,128)} %bitcast.19.refs_1_, f32[8,128]{1,0:T(8,128)S(1)} %get-tuple-element.174.refs_2_), custom_call_target="tpu_custom_call" | custom-call | flops 5750000128 | tf_op jit(solution)/shard_map/pallas_call | solution.py:994
  186.0 3.4 %collective-permute-start.15 = (f32[12,160,128]{2,1,0:T(8,128)S(1)}, f32[12,160,128]{2,1,0:T(8,128)S(1)}, u32[]{:S(2)}, u32[]{:S(2)}) collective-permute-start(f32[12,160,128]{2,1,0:T(8,128)S(1)} %bitcast.105), channel_id=1, source_target_pairs={{0,16},{1,17},{2,18},{3,19},{4,12},{5,13},{6,14},{7,15},{8,24},{9,... | collective-permute-start | bytes 2949128 | tf_op jit(solution)/shard_map/ppermute | solution.py:1059
  189.4 2.2 shard_map.266
  191.7 4.6 %collective-permute-start.17 = (f32[10,80,128]{2,1,0:T(8,128)S(1)}, f32[10,80,128]{2,1,0:T(8,128)S(1)}, u32[]{:S(2)}, u32[]{:S(2)}) collective-permute-start(f32[10,80,128]{2,1,0:T(8,128)S(1)} %bitcast.126), channel_id=1, source_target_pairs={{0,1},{1,0},{2,3},{3,2},{4,5},{5,4},{6,7},{7,6},{8,9},{9,8},{10,11... | collective-permute-start | bytes 1228808 | tf_op jit(solution)/shard_map/ppermute | solution.py:1059
  196.3 2.3 shard_map.267
  198.6 1.3 shard_map.268
  199.9 1.3 collective-permute-start.21
  201.3 5.4 %collective-permute-done.17 = f32[10,80,128]{2,1,0:T(8,128)S(1)} collective-permute-done((f32[10,80,128]{2,1,0:T(8,128)S(1)}, f32[10,80,128]{2,1,0:T(8,128)S(1)}, u32[]{:S(2)}, u32[]{:S(2)}) %collective-permute-start.17) | collective-permute-done | bytes 409632 | tf_op jit(solution)/shard_map/ppermute | solution.py:1059
  206.7 1.3 shard_map.269
  208.1 1.5 shard_map.270
  209.6 1.0 collective-permute-done.21
  210.7 1.3 shard_map.271
  213.0 1.6 collective-permute-start.20
  214.6 1.8 shard_map.272
  216.4 3.4 %collective-permute-done.24 = f32[15,80,128]{2,1,0:T(8,128)S(1)} collective-permute-done((f32[15,80,128]{2,1,0:T(8,128)S(1)}, f32[15,80,128]{2,1,0:T(8,128)S(1)}, u32[]{:S(2)}, u32[]{:S(2)}) %collective-permute-start.24) | collective-permute-done | bytes 614432 | tf_op jit(solution)/shard_map/ppermute | solution.py:1059
  219.9 1.1 shard_map.273
  221.0 1.2 shard_map.274
  222.3 1.2 shard_map.275
  224.8 1.6 collective-permute-start.27
  227.3 1.6 shard_map.276
  229.9 5.4 %collective-permute-start.30 = (f32[15,40,128]{2,1,0:T(8,128)S(1)}, f32[15,40,128]{2,1,0:T(8,128)S(1)}, u32[]{:S(2)}, u32[]{:S(2)}) collective-permute-start(f32[15,40,128]{2,1,0:T(8,128)S(1)} %bitcast.127), channel_id=1, source_target_pairs={{0,1},{1,0},{2,3},{3,2},{4,5},{5,4},{6,7},{7,6},{8,9},{9,8},{10,11... | collective-permute-start | bytes 921608 | tf_op jit(solution)/shard_map/ppermute | solution.py:1059
  235.3 6.1 %collective-permute-done.27 = f32[15,80,128]{2,1,0:T(8,128)S(1)} collective-permute-done((f32[15,80,128]{2,1,0:T(8,128)S(1)}, f32[15,80,128]{2,1,0:T(8,128)S(1)}, u32[]{:S(2)}, u32[]{:S(2)}) %collective-permute-start.27) | collective-permute-done | bytes 614432 | tf_op jit(solution)/shard_map/ppermute | solution.py:1059
  242.5 1.4 shard_map.279
  243.9 1.8 collective-permute-start.29
  245.7 3.6 %collective-permute-done.31 = f32[15,40,128]{2,1,0:T(8,128)S(1)} collective-permute-done((f32[15,40,128]{2,1,0:T(8,128)S(1)}, f32[15,40,128]{2,1,0:T(8,128)S(1)}, u32[]{:S(2)}, u32[]{:S(2)}) %collective-permute-start.31) | collective-permute-done | bytes 307232 | tf_op jit(solution)/shard_map/ppermute | solution.py:1059
  251.7 1.2 collective-permute-done.29
  252.9 1.8 shard_map.282
  (99 shorter events, 20.5 us)
Async XLA Ops:
  23.6 6.3 %collective-permute-start.2 = (f32[1920,256]{1,0:T(8,128)}, f32[1920,256]{1,0:T(8,128)S(1)}, u32[]{:S(2)}, u32[]{:S(2)}) collective-permute-start(f32[1920,256]{1,0:T(8,128)} %get-tuple-element.132.refs_1_), channel_id=1, source_target_pairs={{0,4},{1,5},{2,6},{3,7},{4,0},{5,1},{6,2},{7,3},{8,12},{9,13},{10,... | collective-permute-start | bytes 5898248 | tf_op jit(solution)/shard_map/ppermute | solution.py:1184
  24.2 16.1 %collective-permute-start.1 = (f32[2688,256]{1,0:T(8,128)}, f32[2688,256]{1,0:T(8,128)}, u32[]{:S(2)}, u32[]{:S(2)}) collective-permute-start(f32[2688,256]{1,0:T(8,128)} %get-tuple-element.131.refs_1_), channel_id=1, source_target_pairs={{0,4},{1,5},{2,6},{3,7},{4,0},{5,1},{6,2},{7,3},{8,12},{9,13},{10,... | collective-permute-start | bytes 8257544 | tf_op jit(solution)/shard_map/ppermute | solution.py:1184
  24.2 22.8 %collective-permute-start = (f32[3200,256]{1,0:T(8,128)}, f32[3200,256]{1,0:T(8,128)}, u32[]{:S(2)}, u32[]{:S(2)}) collective-permute-start(f32[3200,256]{1,0:T(8,128)} %get-tuple-element.130.refs_1_), channel_id=1, source_target_pairs={{0,4},{1,5},{2,6},{3,7},{4,0},{5,1},{6,2},{7,3},{8,12},{9,13},{10,... | collective-permute-start | bytes 9830408 | tf_op jit(solution)/shard_map/ppermute | solution.py:1184
  30.0 1.3 copy-start.26
  37.3 39.6 %collective-permute-start.5 = (f32[10,320,128]{2,1,0:T(8,128)}, f32[10,320,128]{2,1,0:T(8,128)S(1)}, u32[]{:S(2)}, u32[]{:S(2)}) collective-permute-start(f32[10,320,128]{2,1,0:T(8,128)} %get-tuple-element.143), channel_id=1, source_target_pairs={{0,8},{1,9},{2,10},{3,11},{4,20},{5,21},{6,22},{7,23},{8,0},{9,1},... | collective-permute-start | bytes 4915208 | tf_op jit(solution)/shard_map/ppermute | solution.py:1059
  53.1 29.7 %collective-permute-start.4 = (f32[10,320,128]{2,1,0:T(8,128)}, f32[10,320,128]{2,1,0:T(8,128)}, u32[]{:S(2)}, u32[]{:S(2)}) collective-permute-start(f32[10,320,128]{2,1,0:T(8,128)} %get-tuple-element.141), channel_id=1, source_target_pairs={{0,8},{1,9},{2,10},{3,11},{4,20},{5,21},{6,22},{7,23},{8,0},{9,1},... | collective-permute-start | bytes 4915208 | tf_op jit(solution)/shard_map/ppermute | solution.py:1059
  53.2 45.7 %collective-permute-start.9 = (f32[11,320,128]{2,1,0:T(8,128)}, f32[11,320,128]{2,1,0:T(8,128)}, u32[]{:S(2)}, u32[]{:S(2)}) collective-permute-start(f32[11,320,128]{2,1,0:T(8,128)} %get-tuple-element.152), channel_id=1, source_target_pairs={{0,1},{1,0},{2,3},{3,2},{4,5},{5,4},{6,7},{7,6},{8,9},{9,8},{10,11... | collective-permute-start | bytes 5406728 | tf_op jit(solution)/shard_map/ppermute | solution.py:1059
  55.3 21.7 %copy-start = (s32[4]{0:T(128)S(1)}, s32[4]{0:T(128)}, u32[]{:S(2)}) copy-start(s32[4]{0:T(128)} %pad_add_fusion.place_ref) | copy-start | bytes 52
  76.4 11.0 %collective-permute-start.7 = (f32[3840,256]{1,0:T(8,128)}, f32[3840,256]{1,0:T(8,128)S(1)}, u32[]{:S(2)}, u32[]{:S(2)}) collective-permute-start(f32[3840,256]{1,0:T(8,128)} %get-tuple-element.148.refs_2_), channel_id=1, source_target_pairs={{0,4},{1,5},{2,6},{3,7},{4,0},{5,1},{6,2},{7,3},{8,12},{9,13},{10,... | collective-permute-start | bytes 11796488 | tf_op jit(solution)/shard_map/ppermute | solution.py:1184
  76.4 47.5 %collective-permute-start.3 = (f32[2664,256]{1,0:T(8,128)}, f32[2664,256]{1,0:T(8,128)}, u32[]{:S(2)}, u32[]{:S(2)}) collective-permute-start(f32[2664,256]{1,0:T(8,128)} %get-tuple-element.138.refs_2_), channel_id=1, source_target_pairs={{0,4},{1,5},{2,6},{3,7},{4,0},{5,1},{6,2},{7,3},{8,12},{9,13},{10,... | collective-permute-start | bytes 8183816 | tf_op jit(solution)/shard_map/ppermute | solution.py:1184
  77.0 0.7 copy-start.10
  77.6 1.4 copy-start.15
  79.1 3.7 %copy-start.16 = (f32[10,320,128]{2,1,0:T(8,128)S(1)}, f32[10,320,128]{2,1,0:T(8,128)}, u32[]{:S(2)}) copy-start(f32[10,320,128]{2,1,0:T(8,128)} %get-tuple-element.140) | copy-start | bytes 4915204
  80.4 0.9 copy-start.23
  81.2 23.7 %collective-permute-start.8 = (f32[10,160,128]{2,1,0:T(8,128)S(1)}, f32[10,160,128]{2,1,0:T(8,128)S(1)}, u32[]{:S(2)}, u32[]{:S(2)}) collective-permute-start(f32[10,160,128]{2,1,0:T(8,128)S(1)} %bitcast.109), channel_id=1, source_target_pairs={{0,16},{1,17},{2,18},{3,19},{4,12},{5,13},{6,14},{7,15},{8,24},{9,... | collective-permute-start | bytes 2457608 | tf_op jit(solution)/shard_map/ppermute | solution.py:1059
  85.0 0.6 copy-start.5
  85.6 0.9 copy-start.21
  86.6 34.3 %collective-permute-start.6 = (f32[10,160,128]{2,1,0:T(8,128)S(1)}, f32[10,160,128]{2,1,0:T(8,128)S(1)}, u32[]{:S(2)}, u32[]{:S(2)}) collective-permute-start(f32[10,160,128]{2,1,0:T(8,128)S(1)} %bitcast.106), channel_id=1, source_target_pairs={{0,1},{1,0},{2,3},{3,2},{4,5},{5,4},{6,7},{7,6},{8,9},{9,8},{10,11... | collective-permute-start | bytes 2457608 | tf_op jit(solution)/shard_map/ppermute | solution.py:1059
  87.3 2.0 copy-start.25
  89.3 9.6 %copy-start.1 = (s32[4]{0:T(128)S(1)}, s32[4]{0:T(128)}, u32[]{:S(2)}) copy-start(s32[4]{0:T(128)} %pad_add_fusion.place_ref) | copy-start | bytes 52
  97.3 35.7 %collective-permute-start.11 = (f32[15,320,128]{2,1,0:T(8,128)}, f32[15,320,128]{2,1,0:T(8,128)}, u32[]{:S(2)}, u32[]{:S(2)}) collective-permute-start(f32[15,320,128]{2,1,0:T(8,128)} %get-tuple-element.162), channel_id=1, source_target_pairs={{0,8},{1,9},{2,10},{3,11},{4,20},{5,21},{6,22},{7,23},{8,0},{9,1},... | collective-permute-start | bytes 7372808 | tf_op jit(solution)/shard_map/ppermute | solution.py:1059
  98.9 0.7 copy-start.13
  99.5 1.5 copy-start.14
  101.0 3.9 %copy-start.24 = (f32[10,1,160,128]{3,2,1,0:T(8,128)S(1)}, f32[10,1,160,128]{3,2,1,0:T(8,128)}, u32[]{:S(2)}) copy-start(f32[10,1,160,128]{3,2,1,0:T(8,128)} %copy-done.23) | copy-start | bytes 2457604
  104.9 35.1 %collective-permute-start.14 = (f32[11,320,128]{2,1,0:T(8,128)}, f32[11,320,128]{2,1,0:T(8,128)}, u32[]{:S(2)}, u32[]{:S(2)}) collective-permute-start(f32[11,320,128]{2,1,0:T(8,128)} %bitcast.29), channel_id=1, source_target_pairs={{0,4},{1,2},{2,1},{3,7},{4,0},{5,6},{6,5},{7,3},{8,12},{9,10},{10,... | collective-permute-start | bytes 5406728 | tf_op jit(solution)/shard_map/ppermute | solution.py:1059
  107.1 0.6 copy-start.6
  107.7 13.2 %copy-start.2 = (s32[4]{0:T(128)S(1)}, s32[4]{0:T(128)}, u32[]{:S(2)}) copy-start(s32[4]{0:T(128)} %pad_add_fusion.place_ref) | copy-start | bytes 52
  107.7 13.2 %copy-start.22 = (f32[10,2,80,128]{3,2,1,0:T(8,128)S(1)}, f32[10,2,80,128]{3,2,1,0:T(8,128)}, u32[]{:S(2)}) copy-start(f32[10,2,80,128]{3,2,1,0:T(8,128)} %copy-done.21) | copy-start | bytes 2457604
  115.7 46.1 %collective-permute-start.13 = (f32[15,320,128]{2,1,0:T(8,128)}, f32[15,320,128]{2,1,0:T(8,128)}, u32[]{:S(2)}, u32[]{:S(2)}) collective-permute-start(f32[15,320,128]{2,1,0:T(8,128)} %get-tuple-element.168), channel_id=1, source_target_pairs={{0,8},{1,9},{2,10},{3,11},{4,20},{5,21},{6,22},{7,23},{8,0},{9,1},... | collective-permute-start | bytes 7372808 | tf_op jit(solution)/shard_map/ppermute | solution.py:1059
  117.1 49.4 %all-to-all-start = ((f32[4,10,1,40,128]{4,3,2,1,0:T(8,128)}), f32[4,10,1,40,128]{4,3,2,1,0:T(8,128)S(1)}, u32[]{:S(2)}, u32[]{:S(2)}) async-start(f32[4,10,1,40,128]{4,3,2,1,0:T(8,128)} %get-tuple-element.166), calls=%async_computation | async-start | bytes 1638400 | tf_op jit(solution)/shard_map/all_to_all | solution.py:1091
  120.9 0.7 copy-start.11
  123.4 0.6 copy-start.4
  124.0 9.1 %copy-start.3 = (s32[4]{0:T(128)S(1)}, s32[4]{0:T(128)}, u32[]{:S(2)}) copy-start(s32[4]{0:T(128)} %pad_add_fusion.place_ref) | copy-start | bytes 52
  124.0 9.1 %copy-start.7 = (f32[15,320,128]{2,1,0:T(8,128)S(1)}, f32[15,320,128]{2,1,0:T(8,128)}, u32[]{:S(2)}) copy-start(f32[15,320,128]{2,1,0:T(8,128)} %get-tuple-element.161) | copy-start | bytes 7372804
  131.5 51.8 %collective-permute-start.10 = (f32[12,320,128]{2,1,0:T(8,128)}, f32[12,320,128]{2,1,0:T(8,128)}, u32[]{:S(2)}, u32[]{:S(2)}) collective-permute-start(f32[12,320,128]{2,1,0:T(8,128)} %get-tuple-element.160), channel_id=1, source_target_pairs={{0,8},{1,9},{2,10},{3,11},{4,20},{5,21},{6,22},{7,23},{8,0},{9,1},... | collective-permute-start | bytes 5898248 | tf_op jit(solution)/shard_map/ppermute | solution.py:1059
  133.0 0.7 copy-start.12
  136.8 1.0 copy-start.17
  137.9 34.7 %collective-permute-start.12 = (f32[15,160,128]{2,1,0:T(8,128)}, f32[15,160,128]{2,1,0:T(8,128)}, u32[]{:S(2)}, u32[]{:S(2)}) collective-permute-start(f32[15,160,128]{2,1,0:T(8,128)} %bitcast.23), channel_id=1, source_target_pairs={{0,1},{1,0},{2,3},{3,2},{4,5},{5,4},{6,7},{7,6},{8,9},{9,8},{10,11... | collective-permute-start | bytes 3686408 | tf_op jit(solution)/shard_map/ppermute | solution.py:1059
  140.0 49.5 %collective-permute-start.16 = (f32[10,160,128]{2,1,0:T(8,128)}, f32[10,160,128]{2,1,0:T(8,128)}, u32[]{:S(2)}, u32[]{:S(2)}) collective-permute-start(f32[10,160,128]{2,1,0:T(8,128)} %bitcast.35), channel_id=1, source_target_pairs={{0,4},{1,2},{2,1},{3,7},{4,0},{5,6},{6,5},{7,3},{8,12},{9,10},{10,... | collective-permute-start | bytes 2457608 | tf_op jit(solution)/shard_map/ppermute | solution.py:1059
  140.0 21.8 %copy-start.8 = (f32[15,320,128]{2,1,0:T(8,128)S(1)}, f32[15,320,128]{2,1,0:T(8,128)}, u32[]{:S(2)}) copy-start(f32[15,320,128]{2,1,0:T(8,128)} %get-tuple-element.167) | copy-start | bytes 7372804
  143.3 1.0 copy-start.19
  144.3 52.0 %collective-permute-start.19 = (f32[11,160,128]{2,1,0:T(8,128)}, f32[11,160,128]{2,1,0:T(8,128)}, u32[]{:S(2)}, u32[]{:S(2)}) collective-permute-start(f32[11,160,128]{2,1,0:T(8,128)} %bitcast.44), channel_id=1, source_target_pairs={{0,1},{1,0},{2,3},{3,2},{4,5},{5,4},{6,7},{7,6},{8,9},{9,8},{10,11... | collective-permute-start | bytes 2703368 | tf_op jit(solution)/shard_map/ppermute | solution.py:1059
  165.0 33.6 %collective-permute-start.18 = (f32[15,160,128]{2,1,0:T(8,128)}, f32[15,160,128]{2,1,0:T(8,128)S(1)}, u32[]{:S(2)}, u32[]{:S(2)}) collective-permute-start(f32[15,160,128]{2,1,0:T(8,128)} %bitcast.41), channel_id=1, source_target_pairs={{0,16},{1,17},{2,18},{3,19},{4,12},{5,13},{6,14},{7,15},{8,24},{9,... | collective-permute-start | bytes 3686408 | tf_op jit(solution)/shard_map/ppermute | solution.py:1059
  172.6 1.3 copy-start.18
  173.9 9.4 %copy-start.9 = (f32[12,320,128]{2,1,0:T(8,128)S(1)}, f32[12,320,128]{2,1,0:T(8,128)}, u32[]{:S(2)}) copy-start(f32[12,320,128]{2,1,0:T(8,128)} %get-tuple-element.159) | copy-start | bytes 5898244
  186.0 22.1 %collective-permute-start.15 = (f32[12,160,128]{2,1,0:T(8,128)S(1)}, f32[12,160,128]{2,1,0:T(8,128)S(1)}, u32[]{:S(2)}, u32[]{:S(2)}) collective-permute-start(f32[12,160,128]{2,1,0:T(8,128)S(1)} %bitcast.105), channel_id=1, source_target_pairs={{0,16},{1,17},{2,18},{3,19},{4,12},{5,13},{6,14},{7,15},{8,24},{9,... | collective-permute-start | bytes 2949128 | tf_op jit(solution)/shard_map/ppermute | solution.py:1059
  189.4 31.6 %collective-permute-start.23 = (f32[15,160,128]{2,1,0:T(8,128)S(1)}, f32[15,160,128]{2,1,0:T(8,128)S(1)}, u32[]{:S(2)}, u32[]{:S(2)}) collective-permute-start(f32[15,160,128]{2,1,0:T(8,128)S(1)} %bitcast.102), channel_id=1, source_target_pairs={{0,4},{1,2},{2,1},{3,7},{4,0},{5,6},{6,5},{7,3},{8,12},{9,10},{10,... | collective-permute-start | bytes 3686408 | tf_op jit(solution)/shard_map/ppermute | solution.py:1059
  189.4 6.9 %copy-start.20 = (f32[11,4,40,128]{3,2,1,0:T(8,128)S(1)}, f32[11,4,40,128]{3,2,1,0:T(8,128)}, u32[]{:S(2)}) copy-start(f32[11,4,40,128]{3,2,1,0:T(8,128)} %copy-done.19) | copy-start | bytes 2703364
  191.7 15.0 %collective-permute-start.17 = (f32[10,80,128]{2,1,0:T(8,128)S(1)}, f32[10,80,128]{2,1,0:T(8,128)S(1)}, u32[]{:S(2)}, u32[]{:S(2)}) collective-permute-start(f32[10,80,128]{2,1,0:T(8,128)S(1)} %bitcast.126), channel_id=1, source_target_pairs={{0,1},{1,0},{2,3},{3,2},{4,5},{5,4},{6,7},{7,6},{8,9},{9,8},{10,11... | collective-permute-start | bytes 1228808 | tf_op jit(solution)/shard_map/ppermute | solution.py:1059
  199.9 20.0 %collective-permute-start.24 = (f32[15,80,128]{2,1,0:T(8,128)S(1)}, f32[15,80,128]{2,1,0:T(8,128)S(1)}, u32[]{:S(2)}, u32[]{:S(2)}) collective-permute-start(f32[15,80,128]{2,1,0:T(8,128)S(1)} %bitcast.111), channel_id=1, source_target_pairs={{0,1},{1,0},{2,3},{3,2},{4,5},{5,4},{6,7},{7,6},{8,9},{9,8},{10,11... | collective-permute-start | bytes 1843208 | tf_op jit(solution)/shard_map/ppermute | solution.py:1059
  199.9 10.7 %collective-permute-start.21 = (f32[11,80,128]{2,1,0:T(8,128)S(1)}, f32[11,80,128]{2,1,0:T(8,128)S(1)}, u32[]{:S(2)}, u32[]{:S(2)}) collective-permute-start(f32[11,80,128]{2,1,0:T(8,128)S(1)} %bitcast.123), channel_id=1, source_target_pairs={{0,8},{1,9},{2,10},{3,11},{4,20},{5,21},{6,22},{7,23},{8,0},{9,1},... | collective-permute-start | bytes 1351688 | tf_op jit(solution)/shard_map/ppermute | solution.py:1059
  208.0 6.7 %collective-permute-start.25 = (f32[10,40,128]{2,1,0:T(8,128)S(1)}, f32[10,40,128]{2,1,0:T(8,128)S(1)}, u32[]{:S(2)}, u32[]{:S(2)}) collective-permute-start(f32[10,40,128]{2,1,0:T(8,128)S(1)} %bitcast.134), channel_id=1, source_target_pairs={{0,16},{1,17},{2,18},{3,19},{4,12},{5,13},{6,14},{7,15},{8,24},{9,... | collective-permute-start | bytes 614408 | tf_op jit(solution)/shard_map/ppermute | solution.py:1059
  212.0 10.3 %collective-permute-start.22 = (f32[11,40,128]{2,1,0:T(8,128)S(1)}, f32[11,40,128]{2,1,0:T(8,128)S(1)}, u32[]{:S(2)}, u32[]{:S(2)}) collective-permute-start(f32[11,40,128]{2,1,0:T(8,128)S(1)} %bitcast.132), channel_id=1, source_target_pairs={{0,16},{1,17},{2,18},{3,19},{4,12},{5,13},{6,14},{7,15},{8,24},{9,... | collective-permute-start | bytes 675848 | tf_op jit(solution)/shard_map/ppermute | solution.py:1059
  213.0 14.3 %collective-permute-start.20 = (f32[12,80,128]{2,1,0:T(8,128)S(1)}, f32[12,80,128]{2,1,0:T(8,128)S(1)}, u32[]{:S(2)}, u32[]{:S(2)}) collective-permute-start(f32[12,80,128]{2,1,0:T(8,128)S(1)} %bitcast.118), channel_id=1, source_target_pairs={{0,1},{1,0},{2,3},{3,2},{4,5},{5,4},{6,7},{7,6},{8,9},{9,8},{10,11... | collective-permute-start | bytes 1474568 | tf_op jit(solution)/shard_map/ppermute | solution.py:1059
  221.0 8.0 %collective-permute-start.28 = (f32[15,80,128]{2,1,0:T(8,128)S(1)}, f32[15,80,128]{2,1,0:T(8,128)S(1)}, u32[]{:S(2)}, u32[]{:S(2)}) collective-permute-start(f32[15,80,128]{2,1,0:T(8,128)S(1)} %bitcast.113), channel_id=1, source_target_pairs={{0,4},{1,2},{2,1},{3,7},{4,0},{5,6},{6,5},{7,3},{8,12},{9,10},{10,... | collective-permute-start | bytes 1843208 | tf_op jit(solution)/shard_map/ppermute | solution.py:1059
  224.8 16.6 %collective-permute-start.27 = (f32[15,80,128]{2,1,0:T(8,128)S(1)}, f32[15,80,128]{2,1,0:T(8,128)S(1)}, u32[]{:S(2)}, u32[]{:S(2)}) collective-permute-start(f32[15,80,128]{2,1,0:T(8,128)S(1)} %bitcast.116), channel_id=1, source_target_pairs={{0,1},{1,0},{2,3},{3,2},{4,5},{5,4},{6,7},{7,6},{8,9},{9,8},{10,11... | collective-permute-start | bytes 1843208 | tf_op jit(solution)/shard_map/ppermute | solution.py:1059
  228.9 13.6 %collective-permute-start.26 = (f32[12,80,128]{2,1,0:T(8,128)S(1)}, f32[12,80,128]{2,1,0:T(8,128)S(1)}, u32[]{:S(2)}, u32[]{:S(2)}) collective-permute-start(f32[12,80,128]{2,1,0:T(8,128)S(1)} %bitcast.120), channel_id=1, source_target_pairs={{0,4},{1,2},{2,1},{3,7},{4,0},{5,6},{6,5},{7,3},{8,12},{9,10},{10,... | collective-permute-start | bytes 1474568 | tf_op jit(solution)/shard_map/ppermute | solution.py:1059
  229.9 20.1 %collective-permute-start.30 = (f32[15,40,128]{2,1,0:T(8,128)S(1)}, f32[15,40,128]{2,1,0:T(8,128)S(1)}, u32[]{:S(2)}, u32[]{:S(2)}) collective-permute-start(f32[15,40,128]{2,1,0:T(8,128)S(1)} %bitcast.127), channel_id=1, source_target_pairs={{0,1},{1,0},{2,3},{3,2},{4,5},{5,4},{6,7},{7,6},{8,9},{9,8},{10,11... | collective-permute-start | bytes 921608 | tf_op jit(solution)/shard_map/ppermute | solution.py:1059
  242.4 6.9 %collective-permute-start.31 = (f32[15,40,128]{2,1,0:T(8,128)S(1)}, f32[15,40,128]{2,1,0:T(8,128)S(1)}, u32[]{:S(2)}, u32[]{:S(2)}) collective-permute-start(f32[15,40,128]{2,1,0:T(8,128)S(1)} %bitcast.129), channel_id=1, source_target_pairs={{0,16},{1,17},{2,18},{3,19},{4,12},{5,13},{6,14},{7,15},{8,24},{9,... | collective-permute-start | bytes 921608 | tf_op jit(solution)/shard_map/ppermute | solution.py:1059
  243.9 8.9 %collective-permute-start.29 = (f32[12,40,128]{2,1,0:T(8,128)S(1)}, f32[12,40,128]{2,1,0:T(8,128)S(1)}, u32[]{:S(2)}, u32[]{:S(2)}) collective-permute-start(f32[12,40,128]{2,1,0:T(8,128)S(1)} %bitcast.131), channel_id=1, source_target_pairs={{0,1},{1,0},{2,3},{3,2},{4,5},{5,4},{6,7},{7,6},{8,9},{9,8},{10,11... | collective-permute-start | bytes 737288 | tf_op jit(solution)/shard_map/ppermute | solution.py:1059
